TPU v7x, 32 devices: a whole 2x2x4 slice. The times are simulated.
32 devices in a mesh: aperture: 16 (over z, x, core), tile: 2 (over y).
Axes of the slice: x: 2, y: 2, z: 4, core: 2. Of those that a mesh axis runs over, the one named last changes fastest.
Arguments:
- raw_echoes: bfloat16 [2, 2048, 2048], P(None, 'aperture', 'tile'), may hold values from -6 to 6
- chirp_taps: bfloat16 [2, 256], replicated, may hold values from -0.25 to 0.25
- steering: bfloat16 [2, 64, 160], replicated, may hold values from -0.3125 to 0.3125
- offsets: int32 [2, 2, 128], replicated, may hold values from 0 to 56
- band_coef: float32 [2, 2, 128, 8], replicated, may hold values from -2.5 to 2.5
- phase_slope: float32 [2, 2, 128], replicated, may hold values from -40 to 40
- phase_base: float32 [2, 2, 128], replicated, may hold values from -3.140625 to 3.140625
Outputs:
- image: float32 [2, 1024, 2048], P(None, 'aperture', 'tile')
Inputs may be any that keep to these rules, and one draw needn't show every extreme that they name: `offsets`: the first input beam of each 8-tap band, so that the band lies within the 64 input beams.
All inputs are finite; a program needn't handle non-finite values.
Results may differ from a plain program's by a relative error of at most 0.0029.
Values may be sent and summed in bfloat16 or wider, within the bound.
No kernel may reach another device: no remote copies, remote signals or barrier semaphores. Data moves between devices by JAX's collectives and lax.ppermute only.
A program may use at most 64 MiB of HBM per device.

v0:
```python
import jax
import jax.numpy as jnp
from jax import lax
from jax.sharding import PartitionSpec as P


def shifted(value, axis, steps):
    count = lax.axis_size(axis)
    initial, last = (max(0, -steps), min(count, count - steps))
    return lax.ppermute(value, axis, [(source, source + steps) for source in range(initial, last)])


def swapped(array, axis, distance):
    return lax.ppermute(array, axis, [(i, i ^ 1 << distance) for i in range(lax.axis_size(axis))])


def chirp_matrix(chirp_taps):
    tap_count = chirp_taps.shape[1]
    row_idx = jnp.arange(tap_count, dtype=jnp.int32)[:, None]
    col_idx = jnp.arange(tap_count, dtype=jnp.int32)[None, :]
    nought = jnp.zeros((), chirp_taps.dtype)
    near_lag = row_idx - col_idx
    far_lag = row_idx - col_idx + tap_count

    def toeplitz(tap_values):
        near_block = jnp.where(
            near_lag >= 0, jnp.take(tap_values, jnp.clip(near_lag, 0, tap_count - 1)), nought
        )
        far_block = jnp.where(
            far_lag < tap_count, jnp.take(tap_values, jnp.clip(far_lag, 0, tap_count - 1)), nought
        )
        return (near_block, far_block)

    near_re, far_re = toeplitz(chirp_taps[0])
    near_im, far_im = toeplitz(chirp_taps[1])
    return jnp.concatenate(
        [
            jnp.concatenate([near_re, -near_im], 1),
            jnp.concatenate([near_im, near_re], 1),
            jnp.concatenate([far_re, -far_im], 1),
            jnp.concatenate([far_im, far_re], 1),
        ],
        0,
    )


def compress(echoes, rim_part, weight):
    tap_count = rim_part.shape[2]
    pulse_count = echoes.shape[1]
    bin_count = echoes.shape[2]
    blocks = bin_count // tap_count
    extended = jnp.concatenate([echoes, rim_part], 2).reshape(2, pulse_count, blocks + 1, tap_count)
    features = jnp.concatenate(
        [extended[0, :, :blocks], extended[1, :, :blocks], extended[0, :, 1:], extended[1, :, 1:]],
        2,
    )
    result = jnp.dot(
        features.reshape(pulse_count * blocks, 4 * tap_count),
        weight,
        preferred_element_type=jnp.float32,
    )
    result = result.reshape(pulse_count, blocks, 2 * tap_count)
    real_part = result[:, :, :tap_count].reshape(pulse_count, bin_count)
    imag_part = result[:, :, tap_count:].reshape(pulse_count, bin_count)
    return jnp.stack([real_part, imag_part]).astype(jnp.bfloat16)


def beamform(steering, compressed):
    real_part = jnp.dot(steering[0], compressed[0], preferred_element_type=jnp.float32) - jnp.dot(
        steering[1], compressed[1], preferred_element_type=jnp.float32
    )
    imag_part = jnp.dot(steering[0], compressed[1], preferred_element_type=jnp.float32) + jnp.dot(
        steering[1], compressed[0], preferred_element_type=jnp.float32
    )
    return jnp.stack([real_part, imag_part])


def band_matrix(starts, weights, col_count):
    columns = jnp.arange(col_count, dtype=jnp.int32)
    taps_idx = jnp.arange(weights.shape[1], dtype=jnp.int32)
    selected = columns[None, None, :] == (starts[:, None] + taps_idx[None, :])[:, :, None]
    return jnp.sum(jnp.where(selected, weights[:, :, None], jnp.zeros((), weights.dtype)), axis=1)


def steered_term(starts, weights, slopes, phase_bases, source, position):
    matrix = band_matrix(starts, weights, source.shape[1])
    real_in = jnp.dot(
        matrix, source[0], precision=lax.Precision.HIGHEST, preferred_element_type=jnp.float32
    )
    imag_in = jnp.dot(
        matrix, source[1], precision=lax.Precision.HIGHEST, preferred_element_type=jnp.float32
    )
    phase_angle = slopes[:, None] * position[None, :] + phase_bases[:, None]
    cosine = jnp.cos(phase_angle)
    sine_part = jnp.sin(phase_angle)
    return jnp.stack(
        [cosine * real_in - sine_part * imag_in, sine_part * real_in + cosine * imag_in]
    )


def side_rows(param_tables, section_no, side_no, start_row, row_count):
    picked = []
    for param_table in param_tables:
        layer = lax.dynamic_index_in_dim(param_table[section_no], side_no, 0, keepdims=False)
        picked.append(lax.dynamic_slice_in_dim(layer, start_row, row_count, 0))
    return picked


def shards(raw_echoes, chirp_taps, steering, offsets, band_coef, phase_slope, phase_base):
    pulse_count = raw_echoes.shape[1]
    bin_count = raw_echoes.shape[2]
    tap_count = chirp_taps.shape[1]
    beam_count = steering.shape[1]
    guard_count = steering.shape[2] - pulse_count
    weight = chirp_matrix(chirp_taps)
    rim_part = shifted(raw_echoes[:, :, :tap_count], "tile", -1)
    own_rows = compress(raw_echoes, rim_part, weight)
    guard_rows = shifted(own_rows[:, :guard_count], "aperture", -1)
    compressed = jnp.concatenate([own_rows, guard_rows], 1)
    subimage = beamform(steering, compressed)
    position = (lax.axis_index("tile") * bin_count + jnp.arange(bin_count, dtype=jnp.int32)).astype(
        jnp.float32
    ) / float(bin_count * lax.axis_size("tile"))
    tables = (offsets, band_coef, phase_slope, phase_base)
    top_bit = lax.axis_size("aperture").bit_length() - 1
    device = lax.axis_index("aperture")
    for section_no in range(2):
        level_bit = top_bit - 2 + section_no
        upper_half = device >> level_bit & 1
        partner_sub = swapped(subimage, "aperture", level_bit)
        low_sub = jnp.where(upper_half == 0, subimage, partner_sub)
        high_sub = jnp.where(upper_half == 0, partner_sub, subimage)
        start_row = upper_half * beam_count
        low_term = steered_term(
            *side_rows(tables, section_no, 0, start_row, beam_count), low_sub, position
        )
        high_term = steered_term(
            *side_rows(tables, section_no, 1, start_row, beam_count), high_sub, position
        )
        subimage = low_term + high_term
    return subimage


def solution(mesh):
    placed = (P(None, "aperture", "tile"), P(), P(), P(), P(), P(), P())
    return jax.shard_map(
        shards, mesh=mesh, in_specs=placed, out_specs=P(None, "aperture", "tile"), check_vma=False
    )
```

profile of v0, /device:TPU:0, one launch (start us, length us, event | category | flops | bytes accessed | tf_op | source)
XLA Modules:
  0.0 1599.9 jit_solution(3145042501038453031)
XLA Ops:
  0.0 1.3 copy.23
  1.3 0.7 slice.150
  2.0 1.3 collective-permute-start
  3.5 0.1 copy.36
  3.7 0.1 copy.37
  3.9 382.6 %gather_fusion.1 = bf16[65536]{0:T(1024)(128)(2,1)S(1)} fusion(bf16[256]{0:T(256)(128)(2,1)S(1)} %get-tuple-element.6, s32[65536]{0:T(1024)S(1)} %broadcast_clamp_fusion.1), kind=kCustom, calls=%fused_computation.1.clone | custom fusion | bytes 524288 | tf_op jit(solution)/shard_map/jit(_take)/gather | solution.py:27
  386.5 382.6 %gather_fusion.3 = bf16[65536]{0:T(1024)(128)(2,1)S(1)} fusion(bf16[256]{0:T(256)(128)(2,1)S(1)} %get-tuple-element.6, s32[65536]{0:T(1024)S(1)} %broadcast_clamp_fusion), kind=kCustom, calls=%fused_computation.3.clone | custom fusion | bytes 524288 | tf_op jit(solution)/shard_map/jit(_take)/gather | solution.py:30
  769.2 382.6 %gather_fusion = bf16[65536]{0:T(1024)(128)(2,1)S(1)} fusion(bf16[256]{0:T(256)(128)(2,1)S(1)} %get-tuple-element.7, s32[65536]{0:T(1024)S(1)} %broadcast_clamp_fusion.1), kind=kCustom, calls=%fused_computation.clone | custom fusion | bytes 524288 | tf_op jit(solution)/shard_map/jit(_take)/gather | solution.py:27
  1151.8 382.6 %gather_fusion.2 = bf16[65536]{0:T(1024)(128)(2,1)S(1)} fusion(bf16[256]{0:T(256)(128)(2,1)S(1)} %get-tuple-element.7, s32[65536]{0:T(1024)S(1)} %broadcast_clamp_fusion), kind=kCustom, calls=%fused_computation.2.clone | custom fusion | bytes 524288 | tf_op jit(solution)/shard_map/jit(_take)/gather | solution.py:30
  1534.8 0.4 copy-done.3
  1535.5 0.2 fusion.77
  1535.7 0.1 fusion.47
  1536.0 1.0 pad_maximum_fusion.1
  1537.0 0.2 fusion.79
  1537.2 0.1 copy.33
  1537.4 0.1 copy.34
  1537.5 0.1 copy.35
  1537.7 0.1 copy.32
  1537.8 0.7 convolution_convert_fusion
  1538.6 0.2 copy.28
  1538.7 0.2 copy.29
  1539.0 1.5 collective-permute-start.1
  1540.6 2.2 collective-permute-done.1
  1542.8 0.2 pad_maximum_fusion
  1543.0 0.3 fusion.24
  1543.3 0.3 fusion.23
  1543.5 0.3 fusion.1
  1543.8 0.3 fusion
  1544.2 8.7 collective-permute-start.2
  1552.9 0.1 copy.21
  1553.1 0.2 select_reduce_fusion.2
  1553.3 0.2 select_reduce_fusion.1
  1553.6 11.7 collective-permute-done.2
  1565.3 0.1 broadcast_select_fusion
  1565.4 0.4 fusion.31
  1565.8 0.4 fusion.32
  1566.1 0.4 fusion.30
  1566.5 2.2 subtract_bitcast_fusion.2
  1568.7 3.4 collective-permute-start.3
  1572.4 0.2 select_reduce_fusion.3
  1572.7 0.2 select_reduce_fusion
  1572.9 22.7 %collective-permute-done.3 = f32[2,64,1024]{2,1,0:T(8,128)S(1)} collective-permute-done((f32[2,64,1024]{2,1,0:T(8,128)S(1)}, f32[2,64,1024]{2,1,0:T(8,128)S(1)}, u32[]{:S(2)}, u32[]{:S(2)}) %collective-permute-start.3) | collective-permute-done | bytes 524320 | tf_op jit(solution)/shard_map/ppermute | solution.py:14
  1595.6 0.2 broadcast_select_fusion.2
  1595.8 0.4 fusion.27
  1596.1 0.4 fusion.28
  1596.5 0.4 fusion.26
  1596.8 2.2 subtract_bitcast_fusion
  1599.0 0.9 maximum_add_fusion.1
  (49 shorter events, 1.8 us)
Async XLA Ops:
  0.0 3.5 copy-start.4
  1.3 2.1 copy-start
  2.0 1534.0 %collective-permute-start = (bf16[2,128,256]{1,2,0:T(8,128)(2,1)}, bf16[2,128,256]{1,2,0:T(8,128)(2,1)}, u32[]{:S(2)}, u32[]{:S(2)}) collective-permute-start(bf16[2,128,256]{1,2,0:T(8,128)(2,1)} %slice.150), channel_id=1, source_target_pairs={{1,0},{3,2},{5,4},{7,6},{9,8},{11,10},{13,12},{15,14},{17,16},{19,... | collective-permute-start | bytes 393224 | tf_op jit(solution)/shard_map/ppermute | solution.py:10
  1534.5 0.7 copy-start.3
  1534.5 0.7 copy-start.5
  1534.5 0.9 copy-start.6
  1534.5 0.9 copy-start.7
  1534.6 1.4 copy-start.1
  1539.0 3.8 collective-permute-start.1
  1540.6 2.4 copy-start.2
  1544.2 21.1 %collective-permute-start.2 = (f32[2,64,1024]{2,1,0:T(8,128)S(1)}, f32[2,64,1024]{2,1,0:T(8,128)S(1)}, u32[]{:S(2)}, u32[]{:S(2)}) collective-permute-start(f32[2,64,1024]{2,1,0:T(8,128)S(1)} %pad_maximum_fusion.3), channel_id=1, source_target_pairs={{0,8},{2,10},{4,12},{6,14},{8,0},{10,2},{12,4},{14,6},{16,24},{18,... | collective-permute-start | bytes 1572872 | tf_op jit(solution)/shard_map/ppermute | solution.py:14
  1568.7 26.9 %collective-permute-start.3 = (f32[2,64,1024]{2,1,0:T(8,128)S(1)}, f32[2,64,1024]{2,1,0:T(8,128)S(1)}, u32[]{:S(2)}, u32[]{:S(2)}) collective-permute-start(f32[2,64,1024]{2,1,0:T(8,128)S(1)} %maximum_add_fusion), channel_id=1, source_target_pairs={{0,16},{2,18},{4,20},{6,22},{8,24},{10,26},{12,28},{14,30},{16,0},... | collective-permute-start | bytes 1572872 | tf_op jit(solution)/shard_map/ppermute | solution.py:14
where the time goes:
time: 1600 us
  local copies, waits for them, and re-layouts  1540 us (96%)
  waiting for transfers between devices  36.5 us (2%)
    gather x4, local copies, waits for them, and re-layouts, toeplitz(): jnp.take(tap_values, jnp.clip(near_lag, 0, tap_count - 1))  765 us
    gather x4, local copies, waits for them, and re-layouts, toeplitz(): jnp.take(tap_values, jnp.clip(far_lag, 0, tap_count - 1))  765 us
    ppermute x2, waiting for transfers between devices, swapped(): lax.ppermute(array, axis, [(i, i ^ 1 << distance) for i in range(lax.axis...  34.4 us
  transfers between devices with their start and end apart: 4, of which 3 were waited for; matrix products, arithmetic and copies ran while one was open for 96% of the time, Pallas kernels for 0%

commit v1 on v0

v1 whole, which is shorter than its diff:
```python
import functools

import jax
import jax.numpy as jnp
from jax import lax
from jax.experimental import pallas as pl
from jax.experimental.pallas import tpu as pltpu
from jax.sharding import PartitionSpec as P

LANES = 128
VMEM = pltpu.CompilerParams(vmem_limit_bytes=24 * 1024 * 1024)


def call(body, outs, args, scratch=(), flops=0, aliases=None, in_specs=None, out_specs=None):
    whole = pl.BlockSpec(memory_space=pltpu.VMEM)
    many = isinstance(outs, (list, tuple))
    moved = sum(a.size * a.dtype.itemsize for a in list(args) + (list(outs) if many else [outs]))
    return pl.pallas_call(
        body,
        out_shape=outs,
        in_specs=in_specs or [whole] * len(args),
        out_specs=out_specs or ([whole] * len(outs) if many else whole),
        scratch_shapes=list(scratch),
        input_output_aliases=aliases or {},
        compiler_params=VMEM,
        cost_estimate=pl.CostEstimate(flops=flops, bytes_accessed=moved, transcendentals=0),
    )(*args)


def toeplitz_kernel(taps_ref, w_ref):
    count = taps_ref.shape[1]
    halves = []
    for part in range(2):
        row = taps_ref[part : part + 1, :].astype(jnp.float32)
        row = jnp.concatenate([row, jnp.zeros_like(row)], 1)
        rows = jnp.broadcast_to(row, (count, 2 * count))
        rolled = pltpu.roll(rows, 0, 1, stride=1, stride_axis=0)
        halves.append(rolled.T)
    for side in range(2):
        re = halves[0][side * count : (side + 1) * count].astype(jnp.bfloat16)
        im = halves[1][side * count : (side + 1) * count].astype(jnp.bfloat16)
        w_ref[side, :count, :count] = re
        w_ref[side, :count, count:] = -im
        w_ref[side, count:, :count] = im
        w_ref[side, count:, count:] = re


def split(value):
    high = value.astype(jnp.bfloat16)
    low = (value - high.astype(jnp.float32)).astype(jnp.bfloat16)
    return high, low


def table_kernel(level, offsets_ref, coef_ref, slope_ref, base_ref, m_ref, e_ref, turned):
    beams = e_ref.shape[3]
    bins = e_ref.shape[4]
    taps = coef_ref.shape[2]
    device = lax.axis_index("aperture")
    tile = lax.axis_index("tile")
    total = bins * lax.axis_size("tile")
    fine_bin = lax.broadcasted_iota(jnp.int32, (beams, LANES), 1)
    coarse_bin = fine_bin * LANES + tile * bins
    for s in range(2):
        upper = (device >> (level + s)) & 1
        start = pl.multiple_of(upper * beams, beams)
        for q in range(2):
            side = jnp.where(upper == q, 0, 1)
            rows = lax.broadcasted_iota(jnp.int32, (beams, 2 * beams), 0)
            lag = rows - offsets_ref[s, q : q + 1, :]
            matrix = jnp.zeros((beams, 2 * beams), jnp.float32)
            for t in range(taps):
                matrix += jnp.where(lag == t, coef_ref[s, q, t : t + 1, :], 0.0)
            pad = jnp.zeros((beams - 2, 2 * beams), jnp.float32)
            stacked = jnp.concatenate(
                [matrix, slope_ref[s, q : q + 1, :], base_ref[s, q : q + 1, :], pad], 0
            )
            turned[...] = stacked.T
            mine = turned[pl.ds(start, beams), :]
            high, low = split(mine[:, :beams])
            m_ref[s, side, :, :] = jnp.concatenate([high, low, high], 1)
            slope = mine[:, beams : beams + 1]
            base = mine[:, beams + 1 : beams + 2]
            fine = slope * (fine_bin.astype(jnp.float32) / float(total))
            coarse = slope * (coarse_bin.astype(jnp.float32) / float(total)) + base
            fine_cos, fine_sin = jnp.cos(fine), jnp.sin(fine)
            coarse_cos, coarse_sin = jnp.cos(coarse), jnp.sin(coarse)
            for k in range(bins // LANES):
                c, d = coarse_cos[:, k : k + 1], coarse_sin[:, k : k + 1]
                at = slice(k * LANES, (k + 1) * LANES)
                e_ref[s, side, 0, :, at] = c * fine_cos - d * fine_sin
                e_ref[s, side, 1, :, at] = d * fine_cos + c * fine_sin


def focus_kernel(first, has_rim, *refs):
    if has_rim:
        raw, guard, rim, corner, w, steering, high_ref, low_ref, x = refs
    else:
        raw, guard, w, steering, high_ref, low_ref, x = refs
    pulses, guards = raw.shape[1], guard.shape[1]
    width = w.shape[1] // 2
    rows = pulses + guards
    bins = high_ref.shape[2]
    blocks = bins // width
    for b in range(blocks + 1):
        at = first + b * width
        for part in range(2):
            lanes = slice(part * width, (part + 1) * width)
            if at < raw.shape[2]:
                own, other = raw[part, :, at : at + width], guard[part, :, at : at + width]
            else:
                own, other = rim[part], corner[part]
            x[b * rows : b * rows + pulses, lanes] = own
            x[b * rows + pulses : (b + 1) * rows, lanes] = other
    turned = jnp.concatenate([steering[0], steering[1]], 0)
    crossed = jnp.concatenate([-steering[1], steering[0]], 0)
    beams = steering.shape[1]
    out = jnp.dot(x[: blocks * rows], w[0], preferred_element_type=jnp.float32)
    out += jnp.dot(x[rows:], w[1], preferred_element_type=jnp.float32)
    out = out.astype(jnp.bfloat16)
    for b in range(blocks):
        re = out[b * rows : (b + 1) * rows, :width]
        im = out[b * rows : (b + 1) * rows, width:]
        sub = jnp.dot(turned, re, preferred_element_type=jnp.float32)
        sub += jnp.dot(crossed, im, preferred_element_type=jnp.float32)
        high, low = split(sub)
        at = slice(b * width, (b + 1) * width)
        high_ref[0, :, at], high_ref[1, :, at] = high[:beams], high[beams:]
        low_ref[0, :, at], low_ref[1, :, at] = low[:beams], low[beams:]


def merged(s, first, high, low, other, m, e):
    bins = high.shape[2]
    beams = high.shape[1]
    at = slice(first, first + bins)
    own_m = m[s, 0]
    other_m = m[s, 1][:, : 2 * beams]
    own, got = [], []
    for part in range(2):
        x = high[part]
        own.append(
            jnp.dot(own_m, jnp.concatenate([x, x, low[part]], 0), preferred_element_type=jnp.float32)
        )
        y = other[part]
        got.append(
            jnp.dot(other_m, jnp.concatenate([y, y], 0), preferred_element_type=jnp.float32)
        )
    c0, s0 = e[s, 0, 0, :, at], e[s, 0, 1, :, at]
    c1, s1 = e[s, 1, 0, :, at], e[s, 1, 1, :, at]
    re = c0 * own[0] - s0 * own[1] + c1 * got[0] - s1 * got[1]
    im = s0 * own[0] + c0 * own[1] + s1 * got[0] + c1 * got[1]
    return re, im


def first_merge_kernel(first, high, low, other, m, e, high_ref, low_ref):
    for part, value in enumerate(merged(0, first, high, low, other, m, e)):
        top, rest = split(value)
        high_ref[part] = top
        low_ref[part] = rest


def last_merge_kernel(first, high, low, other, m, e, *refs):
    image, held, sem = refs[-3:]
    for part, value in enumerate(merged(1, first, high, low, other, m, e)):
        held[part] = value
    copy = pltpu.make_async_copy(held, image.at[:, :, first : first + held.shape[2]], sem)
    copy.start()
    copy.wait()


def cut_kernel(raw, guard, rim, corner, sem):
    guards, width = corner.shape[1:]
    copies = [
        pltpu.make_async_copy(raw.at[:, :guards, :], guard, sem.at[0]),
        pltpu.make_async_copy(raw.at[:, :, :width], rim, sem.at[1]),
        pltpu.make_async_copy(raw.at[:, :guards, :width], corner, sem.at[2]),
    ]
    for copy in copies:
        copy.start()
    for copy in copies:
        copy.wait()


def shards(raw, taps, steering, offsets, coef, slope, base):
    pulses, bins = raw.shape[1:]
    width = taps.shape[1]
    beams = steering.shape[1]
    guards = steering.shape[2] - pulses
    count, tiles = lax.axis_size("aperture"), lax.axis_size("tile")
    level = count.bit_length() - 3
    bf16, f32 = jnp.bfloat16, jnp.float32
    sds = jax.ShapeDtypeStruct
    anywhere = pl.BlockSpec(memory_space=pl.ANY)
    whole = pl.BlockSpec(memory_space=pltpu.VMEM)

    guard, rim, corner = call(
        cut_kernel,
        [sds((2, guards, bins), bf16), sds((2, pulses, width), bf16), sds((2, guards, width), bf16)],
        [raw],
        scratch=[pltpu.SemaphoreType.DMA((3,))],
        in_specs=[anywhere],
        out_specs=[anywhere] * 3,
    )
    guard = lax.ppermute(guard, "aperture", [(d, d - 1) for d in range(1, count)])
    rim = lax.ppermute(rim, "tile", [(t, t - 1) for t in range(1, tiles)])
    corner = lax.ppermute(
        corner,
        ("aperture", "tile"),
        [
            (d * tiles + t, (d - 1) * tiles + t - 1)
            for d in range(1, count)
            for t in range(1, tiles)
        ],
    )
    w = call(toeplitz_kernel, sds((2, 2 * width, 2 * width), bf16), [taps])
    m, e = call(
        functools.partial(table_kernel, level),
        [sds((2, 2, beams, 3 * beams), bf16), sds((2, 2, 2, beams, bins), f32)],
        [offsets, jnp.swapaxes(coef, 2, 3), slope, base],
        scratch=[pltpu.VMEM((2 * beams, 2 * beams), f32)],
        flops=40_000_000,
    )

    half = bins // width // 2 * width
    chunks = [(0, half), (half, bins - half)] if half else [(0, bins)]

    def partner(value, bit):
        return lax.ppermute(value, "aperture", [(d, d ^ (1 << bit)) for d in range(count)])

    subs = []
    for first, size in chunks:
        has_rim = first + size == bins
        rows = pulses + guards
        args = [raw, guard] + ([rim, corner] if has_rim else []) + [w, steering]
        shape = sds((2, beams, size), bf16)
        subs.append(
            call(
                functools.partial(focus_kernel, first, has_rim),
                [shape, shape],
                args,
                scratch=[pltpu.VMEM(((size // width + 1) * rows, 2 * width), bf16)],
                flops=rows * size * 4 * width * 4,
            )
        )
    others = [partner(high, level) for high, _ in subs]
    seconds = []
    for (first, size), (high, low), other in zip(chunks, subs, others):
        shape = sds((2, beams, size), bf16)
        seconds.append(
            call(
                functools.partial(first_merge_kernel, first),
                [shape, shape],
                [high, low, other, m, e],
                flops=beams * size * beams * 40,
            )
        )
    others = [partner(high, level + 1) for high, _ in seconds]
    image = None
    for (first, size), (high, low), other in zip(chunks, seconds, others):
        args = [high, low, other, m, e] + ([] if image is None else [image])
        image = call(
            functools.partial(last_merge_kernel, first),
            sds((2, beams, bins), f32),
            args,
            scratch=[pltpu.VMEM((2, beams, size), f32), pltpu.SemaphoreType.DMA],
            aliases={} if image is None else {5: 0},
            in_specs=[whole] * 5 + ([] if image is None else [anywhere]),
            out_specs=anywhere,
            flops=beams * size * beams * 40,
        )
    return image


def solution(mesh):
    placed = (P(None, "aperture", "tile"), P(), P(), P(), P(), P(), P())
    return jax.shard_map(
        shards, mesh=mesh, in_specs=placed, out_specs=P(None, "aperture", "tile"), check_vma=False
    )
```

time: 1600 us -> 33.4 us (0.02)
  local copies, waits for them, and re-layouts: 1540 us -> 3.61 us
  waiting for transfers between devices: 36.5 us -> 7.73 us
    gather x8 -> x0, local copies, waits for them, and re-layouts: 1530 us -> none  [the longest x4 765 us: toeplitz(): jnp.take(tap_values, jnp.clip(near_lag, 0, tap_count - 1))]
    ppermute x4 -> x7, waiting for transfers between devices: 36.5 us -> 7.73 us  [the longest x4 7.73 us: partner(): lax.ppermute(value, 'aperture', [(d, d ^ 1 << bit) for d in range(count)])]
  transfers between devices with their start and end apart: 4 -> 7, of which waited for: 3 -> 2; matrix products, arithmetic and copies ran while one was open for 96% -> 0% of each run, Pallas kernels for 0% -> 16%
where the time goes in v1:
time: 33.4 us; the launch traced here: 33 us
  starting transfers between devices  15.2 us (46%)
  waiting for transfers between devices  7.73 us (23%)
  Pallas kernels  6.33 us (19%)
  local copies, waits for them, and re-layouts  3.61 us (11%)
    ppermute x4, starting transfers between devices, partner(): lax.ppermute(value, 'aperture', [(d, d ^ 1 << bit) for d in range(count)])  11.4 us
    ppermute x4, waiting for transfers between devices, partner(): lax.ppermute(value, 'aperture', [(d, d ^ 1 << bit) for d in range(count)])  7.73 us
    pallas_call x9, Pallas kernels, call(): pl.pallas_call(body, out_shape=outs, in_specs=in_specs or [whole] * len(a...  6.33 us
    unnamed x18, local copies, waits for them, and re-layouts  3.61 us
    ppermute x1, starting transfers between devices, shards(): lax.ppermute(guard, 'aperture', [(d, d - 1) for d in range(1, count)])  1.29 us
    ppermute x1, starting transfers between devices, shards(): rim = lax.ppermute(rim, 'tile', [(t, t - 1) for t in range(1, tiles)])  1.29 us
    ppermute x1, starting transfers between devices, shards(): lax.ppermute(corner, ('aperture', 'tile'), [(d * tiles + t, (d - 1) * til...  1.29 us
  transfers between devices with their start and end apart: 7, of which 2 were waited for; matrix products, arithmetic and copies ran while one was open for 0% of the time, Pallas kernels for 16%

profile of v1, /device:TPU:0, one launch (start us, length us, event | category | flops | bytes accessed | tf_op | source)
XLA Modules:
  0.0 33.0 jit_solution(10692598187233093777)
XLA Ops:
  0.0 0.0 copy-start
  0.0 1.0 %copy-done = bf16[2,128,1024]{2,1,0:T(8,128)(2,1)S(1)} copy-done((bf16[2,128,1024]{2,1,0:T(8,128)(2,1)S(1)}, bf16[2,128,1024]{2,1,0:T(8,128)(2,1)}, u32[]{:S(2)}) %copy-start) | copy-done | bytes 524312
  1.0 0.0 copy-start.3
  1.0 0.1 shard_map.73
  1.2 1.3 %collective-permute-start = (bf16[2,32,1024]{2,1,0:T(8,128)(2,1)S(1)}, bf16[2,32,1024]{2,1,0:T(8,128)(2,1)S(1)}, u32[]{:S(2)}, u32[]{:S(2)}) collective-permute-start(bf16[2,32,1024]{2,1,0:T(8,128)(2,1)S(1)} %get-tuple-element.18), channel_id=1, source_target_pairs={{2,0},{4,2},{6,4},{8,6},{10,8},{12,10},{14,12},{16,14},{18,16},{20... | collective-permute-start | bytes 393224 | tf_op jit(solution)/shard_map/ppermute | solution.py:203
  2.5 1.3 %collective-permute-start.1 = (bf16[2,128,256]{2,1,0:T(8,128)(2,1)S(1)}, bf16[2,128,256]{2,1,0:T(8,128)(2,1)S(1)}, u32[]{:S(2)}, u32[]{:S(2)}) collective-permute-start(bf16[2,128,256]{2,1,0:T(8,128)(2,1)S(1)} %get-tuple-element.19), channel_id=1, source_target_pairs={{1,0},{3,2},{5,4},{7,6},{9,8},{11,10},{13,12},{15,14},{17,16},{19,... | collective-permute-start | bytes 393224 | tf_op jit(solution)/shard_map/ppermute | solution.py:204
  3.8 1.3 %collective-permute-start.2 = (bf16[2,32,256]{2,1,0:T(8,128)(2,1)S(1)}, bf16[2,32,256]{2,1,0:T(8,128)(2,1)S(1)}, u32[]{:S(2)}, u32[]{:S(2)}) collective-permute-start(bf16[2,32,256]{2,1,0:T(8,128)(2,1)S(1)} %get-tuple-element.20), channel_id=1, source_target_pairs={{3,0},{5,2},{7,4},{9,6},{11,8},{13,10},{15,12},{17,14},{19,16},{21... | collective-permute-start | bytes 98312 | tf_op jit(solution)/shard_map/ppermute | solution.py:205
  5.1 0.0 copy-start.4
  5.1 0.7 %copy-done.4 = bf16[2,256]{1,0:T(2,128)(2,1)S(1)} copy-done((bf16[2,256]{1,0:T(2,128)(2,1)S(1)}, bf16[2,256]{1,0:T(2,128)(2,1)}, u32[]{:S(2)}) %copy-start.4) | copy-done | bytes 1048
  5.8 0.2 shard_map.74.refs_4_.refs_2_
  6.0 0.0 collective-permute-done.refs_1_
  6.0 0.0 copy-start.1
  6.0 1.0 %copy-done.1 = bf16[2,128,1024]{2,1,0:T(8,128)(2,1)S(1)} copy-done((bf16[2,128,1024]{2,1,0:T(8,128)(2,1)S(1)}, bf16[2,128,1024]{2,1,0:T(8,128)(2,1)}, u32[]{:S(2)}) %copy-start.1) | copy-done | bytes 524312
  7.0 0.0 copy-start.2
  7.0 0.8 %copy-done.2 = bf16[2,64,160]{2,1,0:T(8,128)(2,1)S(1)} copy-done((bf16[2,64,160]{2,1,0:T(8,128)(2,1)S(1)}, bf16[2,64,160]{2,1,0:T(8,128)(2,1)}, u32[]{:S(2)}) %copy-start.2) | copy-done | bytes 40984
  7.9 0.0 copy-start.5
  7.9 0.0 copy-start.6
  7.9 0.0 copy-start.7
  7.9 0.0 copy-start.8
  7.9 0.7 %shard_map.78 = (bf16[2,64,512]{2,1,0:T(8,128)(2,1)S(1)}, bf16[2,64,512]{2,1,0:T(8,128)(2,1)S(1)}) custom-call(bf16[2,128,1024]{2,1,0:T(8,128)(2,1)S(1)} %copy-done.1, bf16[2,32,1024]{2,1,0:T(8,128)(2,1)S(1)} %collective-permute-done.refs_1_, bf16[2,512,512]{2,1,0:T(8,128)(2,1)S(1)} %shard_map.74.refs_4_.refs_2_, bf16[2,64,160]{2,1,0:T(8,128)(2,1)S(1)} %copy-done.2), custom_call_target="tpu_custom_call" | custom-call | flops 335544320 | bytes 2007040 | tf_op jit(solution)/shard_map/pallas_call | solution.py:18
  8.6 4.5 %collective-permute-start.5 = (bf16[2,64,512]{2,1,0:T(8,128)(2,1)S(1)}, bf16[2,64,512]{2,1,0:T(8,128)(2,1)S(1)}, u32[]{:S(2)}, u32[]{:S(2)}) collective-permute-start(bf16[2,64,512]{2,1,0:T(8,128)(2,1)S(1)} %get-tuple-element.27.high), channel_id=1, source_target_pairs={{0,8},{2,10},{4,12},{6,14},{8,0},{10,2},{12,4},{14,6},{16,24},{18,... | collective-permute-start | bytes 393224 | tf_op jit(solution)/shard_map/ppermute | solution.py:227
  13.1 0.0 collective-permute-done.2.refs_3_
  13.1 0.0 collective-permute-done.1.refs_2_
  13.1 0.0 copy-done.3
  13.1 0.7 %shard_map.75 = (bf16[2,64,512]{2,1,0:T(8,128)(2,1)S(1)}, bf16[2,64,512]{2,1,0:T(8,128)(2,1)S(1)}) custom-call(bf16[2,128,1024]{2,1,0:T(8,128)(2,1)S(1)} %copy-done.1, bf16[2,32,1024]{2,1,0:T(8,128)(2,1)S(1)} %collective-permute-done.refs_1_, bf16[2,128,256]{2,1,0:T(8,128)(2,1)S(1)} %collective-permute-done.1.refs_2_, ...), custom_call_target="tpu_custom_call" | custom-call | flops 335544320 | bytes 2170880 | tf_op jit(solution)/shard_map/pallas_call | solution.py:18
  13.8 1.6 %collective-permute-start.3 = (bf16[2,64,512]{2,1,0:T(8,128)(2,1)S(1)}, bf16[2,64,512]{2,1,0:T(8,128)(2,1)S(1)}, u32[]{:S(2)}, u32[]{:S(2)}) collective-permute-start(bf16[2,64,512]{2,1,0:T(8,128)(2,1)S(1)} %get-tuple-element.21.high), channel_id=1, source_target_pairs={{0,8},{2,10},{4,12},{6,14},{8,0},{10,2},{12,4},{14,6},{16,24},{18,... | collective-permute-start | bytes 393224 | tf_op jit(solution)/shard_map/ppermute | solution.py:227
  15.4 0.0 copy-done.5
  15.4 0.0 copy-done.6
  15.4 0.0 copy-done.7
  15.4 0.0 copy-done.8
  15.4 2.0 %shard_map.76 = (bf16[2,2,64,192]{3,2,1,0:T(8,128)(2,1)S(1)}, f32[2,2,2,64,1024]{4,3,2,1,0:T(8,128)S(1)}) custom-call(s32[2,2,128]{2,1,0:T(2,128)S(1)} %copy-done.6, f32[2,2,8,128]{3,2,1,0:T(8,128)S(1)} %bitcast.1, f32[2,2,128]{2,1,0:T(2,128)S(1)} %copy-done.7, f32[2,2,128]{2,1,0:T(2,128)S(1)} %copy-done.8), custom_call_target="tpu_custom_call" | custom-call | flops 40000000 | bytes 2217984 | tf_op jit(solution)/shard_map/pallas_call | solution.py:18
  17.4 0.0 collective-permute-done.5.other
  17.5 0.3 shard_map.79
  17.8 2.8 %collective-permute-start.6 = (bf16[2,64,512]{2,1,0:T(8,128)(2,1)S(1)}, bf16[2,64,512]{2,1,0:T(8,128)(2,1)S(1)}, u32[]{:S(2)}, u32[]{:S(2)}) collective-permute-start(bf16[2,64,512]{2,1,0:T(8,128)(2,1)S(1)} %get-tuple-element.29.high), channel_id=1, source_target_pairs={{0,16},{2,18},{4,20},{6,22},{8,24},{10,26},{12,28},{14,30},{16,0},... | collective-permute-start | bytes 393224 | tf_op jit(solution)/shard_map/ppermute | solution.py:227
  20.5 0.0 collective-permute-done.3.other
  20.5 0.3 shard_map.77
  20.9 2.5 %collective-permute-start.4 = (bf16[2,64,512]{2,1,0:T(8,128)(2,1)S(1)}, bf16[2,64,512]{2,1,0:T(8,128)(2,1)S(1)}, u32[]{:S(2)}, u32[]{:S(2)}) collective-permute-start(bf16[2,64,512]{2,1,0:T(8,128)(2,1)S(1)} %get-tuple-element.25.high), channel_id=1, source_target_pairs={{0,16},{2,18},{4,20},{6,22},{8,24},{10,26},{12,28},{14,30},{16,0},... | collective-permute-start | bytes 393224 | tf_op jit(solution)/shard_map/ppermute | solution.py:227
  23.4 6.8 %collective-permute-done.6.other = bf16[2,64,512]{2,1,0:T(8,128)(2,1)S(1)} collective-permute-done((bf16[2,64,512]{2,1,0:T(8,128)(2,1)S(1)}, bf16[2,64,512]{2,1,0:T(8,128)(2,1)S(1)}, u32[]{:S(2)}, u32[]{:S(2)}) %collective-permute-start.6) | collective-permute-done | bytes 131104 | tf_op jit(solution)/shard_map/ppermute | solution.py:227
  30.1 1.0 %shard_map.80.refs_0_ = f32[2,64,1024]{2,1,0:T(8,128)} custom-call(bf16[2,64,512]{2,1,0:T(8,128)(2,1)S(1)} %get-tuple-element.29.high, bf16[2,64,512]{2,1,0:T(8,128)(2,1)S(1)} %get-tuple-element.30.low, bf16[2,64,512]{2,1,0:T(8,128)(2,1)S(1)} %collective-permute-done.6.other, bf16[2,2,64,192]{3,2,1,0:T(8,128)(2,1)S(1)} %get-tuple-element.23.m, ...), custom_call_target="tpu_custom_call" | custom-call | flops 83886080 | bytes 3112960 | tf_op jit(solution)/shard_map/pallas_call | solution.py:18
  31.1 0.9 %collective-permute-done.4.other = bf16[2,64,512]{2,1,0:T(8,128)(2,1)S(1)} collective-permute-done((bf16[2,64,512]{2,1,0:T(8,128)(2,1)S(1)}, bf16[2,64,512]{2,1,0:T(8,128)(2,1)S(1)}, u32[]{:S(2)}, u32[]{:S(2)}) %collective-permute-start.4) | collective-permute-done | bytes 131104 | tf_op jit(solution)/shard_map/ppermute | solution.py:227
  32.0 1.0 %shard_map.81 = f32[2,64,1024]{2,1,0:T(8,128)} custom-call(bf16[2,64,512]{2,1,0:T(8,128)(2,1)S(1)} %get-tuple-element.25.high, bf16[2,64,512]{2,1,0:T(8,128)(2,1)S(1)} %get-tuple-element.26.low, bf16[2,64,512]{2,1,0:T(8,128)(2,1)S(1)} %collective-permute-done.4.other, ...), custom_call_target="tpu_custom_call", output_to_operand_aliasing={{}: (5, {})} | custom-call | flops 83886080 | bytes 3637248 | tf_op jit(solution)/shard_map/pallas_call | solution.py:18
Async XLA Ops:
  0.0 1.0 %copy-start = (bf16[2,128,1024]{2,1,0:T(8,128)(2,1)S(1)}, bf16[2,128,1024]{2,1,0:T(8,128)(2,1)}, u32[]{:S(2)}) copy-start(bf16[2,128,1024]{2,1,0:T(8,128)(2,1)} %refs_0_.3) | copy-start | bytes 1572868
  1.0 12.1 %copy-start.3 = (bf16[2,64,160]{2,1,0:T(8,128)(2,1)S(1)}, bf16[2,64,160]{2,1,0:T(8,128)(2,1)}, u32[]{:S(2)}) copy-start(bf16[2,64,160]{2,1,0:T(8,128)(2,1)} %refs_3_.1) | copy-start | bytes 122884
  1.2 4.8 %collective-permute-start = (bf16[2,32,1024]{2,1,0:T(8,128)(2,1)S(1)}, bf16[2,32,1024]{2,1,0:T(8,128)(2,1)S(1)}, u32[]{:S(2)}, u32[]{:S(2)}) collective-permute-start(bf16[2,32,1024]{2,1,0:T(8,128)(2,1)S(1)} %get-tuple-element.18), channel_id=1, source_target_pairs={{2,0},{4,2},{6,4},{8,6},{10,8},{12,10},{14,12},{16,14},{18,16},{20... | collective-permute-start | bytes 393224 | tf_op jit(solution)/shard_map/ppermute | solution.py:203
  2.5 10.6 %collective-permute-start.1 = (bf16[2,128,256]{2,1,0:T(8,128)(2,1)S(1)}, bf16[2,128,256]{2,1,0:T(8,128)(2,1)S(1)}, u32[]{:S(2)}, u32[]{:S(2)}) collective-permute-start(bf16[2,128,256]{2,1,0:T(8,128)(2,1)S(1)} %get-tuple-element.19), channel_id=1, source_target_pairs={{1,0},{3,2},{5,4},{7,6},{9,8},{11,10},{13,12},{15,14},{17,16},{19,... | collective-permute-start | bytes 393224 | tf_op jit(solution)/shard_map/ppermute | solution.py:204
  3.8 9.3 %collective-permute-start.2 = (bf16[2,32,256]{2,1,0:T(8,128)(2,1)S(1)}, bf16[2,32,256]{2,1,0:T(8,128)(2,1)S(1)}, u32[]{:S(2)}, u32[]{:S(2)}) collective-permute-start(bf16[2,32,256]{2,1,0:T(8,128)(2,1)S(1)} %get-tuple-element.20), channel_id=1, source_target_pairs={{3,0},{5,2},{7,4},{9,6},{11,8},{13,10},{15,12},{17,14},{19,16},{21... | collective-permute-start | bytes 98312 | tf_op jit(solution)/shard_map/ppermute | solution.py:205
  5.1 0.7 %copy-start.4 = (bf16[2,256]{1,0:T(2,128)(2,1)S(1)}, bf16[2,256]{1,0:T(2,128)(2,1)}, u32[]{:S(2)}) copy-start(bf16[2,256]{1,0:T(2,128)(2,1)} %taps_ref.1) | copy-start | bytes 3076
  6.0 1.0 %copy-start.1 = (bf16[2,128,1024]{2,1,0:T(8,128)(2,1)S(1)}, bf16[2,128,1024]{2,1,0:T(8,128)(2,1)}, u32[]{:S(2)}) copy-start(bf16[2,128,1024]{2,1,0:T(8,128)(2,1)} %refs_0_.3) | copy-start | bytes 1572868
  7.0 0.8 %copy-start.2 = (bf16[2,64,160]{2,1,0:T(8,128)(2,1)S(1)}, bf16[2,64,160]{2,1,0:T(8,128)(2,1)}, u32[]{:S(2)}) copy-start(bf16[2,64,160]{2,1,0:T(8,128)(2,1)} %refs_3_.1) | copy-start | bytes 122884
  7.9 7.5 %copy-start.5 = (f32[2,2,128,8]{2,3,1,0:T(8,128)S(1)}, f32[2,2,128,8]{2,3,1,0:T(8,128)}, u32[]{:S(2)}) copy-start(f32[2,2,128,8]{2,3,1,0:T(8,128)} %param.11) | copy-start | bytes 49156
  7.9 7.5 %copy-start.6 = (s32[2,2,128]{2,1,0:T(2,128)S(1)}, s32[2,2,128]{2,1,0:T(2,128)}, u32[]{:S(2)}) copy-start(s32[2,2,128]{2,1,0:T(2,128)} %offsets_ref.1) | copy-start | bytes 6148
  7.9 7.5 %copy-start.7 = (f32[2,2,128]{2,1,0:T(2,128)S(1)}, f32[2,2,128]{2,1,0:T(2,128)}, u32[]{:S(2)}) copy-start(f32[2,2,128]{2,1,0:T(2,128)} %slope_ref.1) | copy-start | bytes 6148
  7.9 7.5 %copy-start.8 = (f32[2,2,128]{2,1,0:T(2,128)S(1)}, f32[2,2,128]{2,1,0:T(2,128)}, u32[]{:S(2)}) copy-start(f32[2,2,128]{2,1,0:T(2,128)} %base_ref.1) | copy-start | bytes 6148
  8.6 8.9 %collective-permute-start.5 = (bf16[2,64,512]{2,1,0:T(8,128)(2,1)S(1)}, bf16[2,64,512]{2,1,0:T(8,128)(2,1)S(1)}, u32[]{:S(2)}, u32[]{:S(2)}) collective-permute-start(bf16[2,64,512]{2,1,0:T(8,128)(2,1)S(1)} %get-tuple-element.27.high), channel_id=1, source_target_pairs={{0,8},{2,10},{4,12},{6,14},{8,0},{10,2},{12,4},{14,6},{16,24},{18,... | collective-permute-start | bytes 393224 | tf_op jit(solution)/shard_map/ppermute | solution.py:227
  13.8 6.7 %collective-permute-start.3 = (bf16[2,64,512]{2,1,0:T(8,128)(2,1)S(1)}, bf16[2,64,512]{2,1,0:T(8,128)(2,1)S(1)}, u32[]{:S(2)}, u32[]{:S(2)}) collective-permute-start(bf16[2,64,512]{2,1,0:T(8,128)(2,1)S(1)} %get-tuple-element.21.high), channel_id=1, source_target_pairs={{0,8},{2,10},{4,12},{6,14},{8,0},{10,2},{12,4},{14,6},{16,24},{18,... | collective-permute-start | bytes 393224 | tf_op jit(solution)/shard_map/ppermute | solution.py:227
  17.8 12.3 %collective-permute-start.6 = (bf16[2,64,512]{2,1,0:T(8,128)(2,1)S(1)}, bf16[2,64,512]{2,1,0:T(8,128)(2,1)S(1)}, u32[]{:S(2)}, u32[]{:S(2)}) collective-permute-start(bf16[2,64,512]{2,1,0:T(8,128)(2,1)S(1)} %get-tuple-element.29.high), channel_id=1, source_target_pairs={{0,16},{2,18},{4,20},{6,22},{8,24},{10,26},{12,28},{14,30},{16,0},... | collective-permute-start | bytes 393224 | tf_op jit(solution)/shard_map/ppermute | solution.py:227
  20.9 11.2 %collective-permute-start.4 = (bf16[2,64,512]{2,1,0:T(8,128)(2,1)S(1)}, bf16[2,64,512]{2,1,0:T(8,128)(2,1)S(1)}, u32[]{:S(2)}, u32[]{:S(2)}) collective-permute-start(bf16[2,64,512]{2,1,0:T(8,128)(2,1)S(1)} %get-tuple-element.25.high), channel_id=1, source_target_pairs={{0,16},{2,18},{4,20},{6,22},{8,24},{10,26},{12,28},{14,30},{16,0},... | collective-permute-start | bytes 393224 | tf_op jit(solution)/shard_map/ppermute | solution.py:227

commit v2 on v1

v2 whole, which is shorter than its diff:
```python
import functools
import math

import jax
import jax.numpy as jnp
from jax import lax
from jax.experimental import pallas as pl
from jax.experimental.pallas import tpu as pltpu
from jax.sharding import PartitionSpec as P

LANES = 128
VMEM = pltpu.CompilerParams(vmem_limit_bytes=24 * 1024 * 1024)


def call(body, outs, args, scratch=(), flops=0, aliases=None, in_specs=None, out_specs=None, after=()):
    whole = pl.BlockSpec(memory_space=pltpu.VMEM)
    if after:
        inner, given, unused = body, len(args), len(after)
        in_specs = (in_specs or [whole] * given) + [pl.BlockSpec(memory_space=pl.ANY)] * unused
        args = list(args) + list(after)

        def body(*refs):
            inner(*refs[:given], *refs[given + unused :])

    many = isinstance(outs, (list, tuple))
    return pl.pallas_call(
        body,
        out_shape=outs,
        in_specs=in_specs or [whole] * len(args),
        out_specs=out_specs or ([whole] * len(outs) if many else whole),
        scratch_shapes=list(scratch),
        input_output_aliases=aliases or {},
        compiler_params=VMEM,
        cost_estimate=pl.CostEstimate(flops=flops, bytes_accessed=0, transcendentals=0),
    )(*args)


def completed(pairs, count):
    needed = dict(pairs)
    back = {t: s for s, t in needed.items() if t not in needed and s not in needed.values()}
    moves = {**needed, **back}
    sources = [d for d in range(count) if d not in moves]
    targets = [d for d in range(count) if d not in moves.values()]
    for d in [d for d in sources if d in targets]:
        ways = [(abs(s - d) + abs(t - d), s) for s, t in moves.items() if needed.get(s) != t]
        if ways:
            start = min(ways)[1]
            moves[d] = moves[start]
            moves[start] = d
        else:
            moves[d] = d
    moves.update(zip([d for d in sources if d not in moves], [d for d in targets if d not in moves.values()]))
    return sorted(moves.items())


def toeplitz_kernel(taps_ref, w_ref):
    count = taps_ref.shape[1]
    halves = []
    for part in range(2):
        row = taps_ref[part : part + 1, :].astype(jnp.float32)
        row = jnp.concatenate([row, jnp.zeros_like(row)], 1)
        rows = jnp.broadcast_to(row, (count, 2 * count))
        rolled = pltpu.roll(rows, 0, 1, stride=1, stride_axis=0)
        halves.append(rolled.T)
    for side in range(2):
        re = halves[0][side * count : (side + 1) * count].astype(jnp.bfloat16)
        im = halves[1][side * count : (side + 1) * count].astype(jnp.bfloat16)
        w_ref[side, :count, :count] = re
        w_ref[side, :count, count:] = -im
        w_ref[side, count:, :count] = im
        w_ref[side, count:, count:] = re


def split(value):
    high = value.astype(jnp.bfloat16)
    low = (value - high.astype(jnp.float32)).astype(jnp.bfloat16)
    return high, low


def turn(angle):
    quarters = jnp.floor(angle * (2 / math.pi) + 0.5)
    rest = angle - quarters * 1.5703125
    rest = rest - quarters * 4.837512969970703125e-4
    rest = rest - quarters * 7.54978995489188216e-8
    z = rest * rest
    sine = rest + rest * z * (-1.6666654611e-1 + z * (8.3321608736e-3 - z * 1.9515295891e-4))
    cosine = 1 - 0.5 * z + z * z * (
        4.166664568298827e-2 + z * (-1.388731625493765e-3 + z * 2.443315711809948e-5)
    )
    which = quarters.astype(jnp.int32)
    odd = (which & 1) == 1
    c, d = jnp.where(odd, sine, cosine), jnp.where(odd, cosine, sine)
    c = jnp.where(((which + 1) & 2) == 2, -c, c)
    d = jnp.where((which & 2) == 2, -d, d)
    return c, d


def table_kernel(s, level, offsets_ref, coef_ref, slope_ref, base_ref, m_ref, e_ref, turned):
    beams, bins = e_ref.shape[2:]
    taps = coef_ref.shape[2]
    device = lax.axis_index("aperture")
    tile = lax.axis_index("tile")
    total = float(bins * lax.axis_size("tile"))
    fine_bin = lax.broadcasted_iota(jnp.int32, (beams, LANES), 1)
    coarse_bin = fine_bin * LANES + tile * bins
    upper = (device >> (level + s)) & 1
    start = pl.multiple_of(upper * beams, beams)
    for q in range(2):
        side = jnp.where(upper == q, 0, 1)
        rows = lax.broadcasted_iota(jnp.int32, (beams, 2 * beams), 0)
        lag = rows - offsets_ref[s, q : q + 1, :]
        matrix = jnp.zeros((beams, 2 * beams), jnp.float32)
        for t in range(taps):
            matrix += jnp.where(lag == t, coef_ref[s, q, t : t + 1, :], 0.0)
        pad = jnp.zeros((beams - 2, 2 * beams), jnp.float32)
        stacked = jnp.concatenate(
            [matrix, slope_ref[s, q : q + 1, :], base_ref[s, q : q + 1, :], pad], 0
        )
        turned[...] = stacked.T
        mine = turned[pl.ds(start, beams), :]
        high, low = split(mine[:, :beams])
        m_ref[side, :, :] = jnp.concatenate([high, low, high], 1)
        slope = mine[:, beams : beams + 1]
        base = mine[:, beams + 1 : beams + 2]
        fine_cos, fine_sin = turn(slope * (fine_bin.astype(jnp.float32) / total))
        coarse_cos, coarse_sin = turn(slope * (coarse_bin.astype(jnp.float32) / total) + base)
        for k in range(bins // LANES):
            c, d = coarse_cos[:, k : k + 1], coarse_sin[:, k : k + 1]
            at = slice(k * LANES, (k + 1) * LANES)
            e_ref[side, 0, :, at] = c * fine_cos - d * fine_sin
            e_ref[side, 1, :, at] = d * fine_cos + c * fine_sin


def focus_kernel(first, has_rim, sizes, *refs):
    if has_rim:
        raw, near, far, rim, corner, w, steering = refs[:7]
    else:
        raw, near, far, w, steering = refs[:5]
    x = refs[-1]
    outs = refs[-1 - 2 * len(sizes) : -1]
    pulses, guards = raw.shape[1], near.shape[1]
    width = w.shape[1] // 2
    rows = pulses + guards
    blocks = sum(sizes) // width
    device = lax.axis_index("aperture")
    even = device % 2 == 0
    followed = device < lax.axis_size("aperture") - 1
    inner = lax.axis_index("tile") < lax.axis_size("tile") - 1
    nought = jnp.zeros((), jnp.bfloat16)
    for b in range(blocks + 1):
        at = first + b * width
        for part in range(2):
            lanes = slice(part * width, (part + 1) * width)
            if at < raw.shape[2]:
                own = raw[part, :, at : at + width]
                other = jnp.where(even, near[part, :, at : at + width], far[part, :, at : at + width])
                other = jnp.where(followed, other, nought)
            else:
                own = jnp.where(inner, rim[part], nought)
                other = jnp.where(inner & followed, corner[part], nought)
            x[b * rows : b * rows + pulses, lanes] = own
            x[b * rows + pulses : (b + 1) * rows, lanes] = other
    turned = jnp.concatenate([steering[0], steering[1]], 0)
    crossed = jnp.concatenate([-steering[1], steering[0]], 0)
    beams = steering.shape[1]
    out = jnp.dot(x[: blocks * rows], w[0], preferred_element_type=jnp.float32)
    out += jnp.dot(x[rows:], w[1], preferred_element_type=jnp.float32)
    out = out.astype(jnp.bfloat16)
    places = [(n, at) for n, size in enumerate(sizes) for at in range(0, size, LANES)]
    for b in range(blocks):
        re = out[b * rows : (b + 1) * rows, :width]
        im = out[b * rows : (b + 1) * rows, width:]
        sub = jnp.dot(turned, re, preferred_element_type=jnp.float32)
        sub += jnp.dot(crossed, im, preferred_element_type=jnp.float32)
        for k in range(width // LANES):
            n, at = places[b * (width // LANES) + k]
            high, low = split(sub[:, k * LANES : (k + 1) * LANES])
            for ref, value in ((outs[2 * n], high), (outs[2 * n + 1], low)):
                ref[0, :, at : at + LANES] = value[:beams]
                ref[1, :, at : at + LANES] = value[beams:]


def merged(first, local, bins, high, low, other, m, e):
    beams = high.shape[1]
    here = slice(local, local + bins)
    at = slice(first, first + bins)
    own_m = m[0]
    other_m = m[1][:, : 2 * beams]
    own, got = [], []
    for part in range(2):
        x = high[part, :, here]
        x = jnp.concatenate([x, x, low[part, :, here]], 0)
        own.append(jnp.dot(own_m, x, preferred_element_type=jnp.float32))
        y = other[part, :, here]
        y = jnp.concatenate([y, y], 0)
        got.append(jnp.dot(other_m, y, preferred_element_type=jnp.float32))
    c0, s0 = e[0, 0, :, at], e[0, 1, :, at]
    c1, s1 = e[1, 0, :, at], e[1, 1, :, at]
    re = c0 * own[0] - s0 * own[1] + c1 * got[0] - s1 * got[1]
    im = s0 * own[0] + c0 * own[1] + s1 * got[0] + c1 * got[1]
    return re, im


def first_merge_kernel(first, local, high, low, other, m, e, high_ref, low_ref):
    bins = high_ref.shape[2]
    for part, value in enumerate(merged(first, local, bins, high, low, other, m, e)):
        top, rest = split(value)
        high_ref[part] = top
        low_ref[part] = rest


def last_merge_kernel(first, high, low, other, m, e, *refs):
    image, held, sem = refs[-3:]
    copies = []
    for part, value in enumerate(merged(first, 0, held.shape[2], high, low, other, m, e)):
        held[part] = value
        place = image.at[part, :, first : first + held.shape[2]]
        copies.append(pltpu.make_async_copy(held.at[part], place, sem.at[part]))
        copies[-1].start()
    for copy in copies:
        copy.wait()


def cut_kernel(raw, guard, rim, corner, sem):
    guards, width = corner.shape[1:]
    copies = [
        pltpu.make_async_copy(raw.at[:, :guards, :], guard, sem.at[0]),
        pltpu.make_async_copy(raw.at[:, :, :width], rim, sem.at[1]),
        pltpu.make_async_copy(raw.at[:, :guards, :width], corner, sem.at[2]),
    ]
    for copy in copies:
        copy.start()
    for copy in copies:
        copy.wait()


def shards(raw, taps, steering, offsets, coef, slope, base):
    pulses, bins = raw.shape[1:]
    width = taps.shape[1]
    beams = steering.shape[1]
    guards = steering.shape[2] - pulses
    count, tiles = lax.axis_size("aperture"), lax.axis_size("tile")
    level = count.bit_length() - 3
    bf16, f32 = jnp.bfloat16, jnp.float32
    sds = jax.ShapeDtypeStruct
    anywhere = pl.BlockSpec(memory_space=pl.ANY)
    whole = pl.BlockSpec(memory_space=pltpu.VMEM)

    guard, rim, corner = call(
        cut_kernel,
        [sds((2, guards, bins), bf16), sds((2, pulses, width), bf16), sds((2, guards, width), bf16)],
        [raw],
        scratch=[pltpu.SemaphoreType.DMA((3,))],
        in_specs=[pl.BlockSpec(memory_space=pltpu.HBM)],
        out_specs=[anywhere] * 3,
    )
    near = lax.ppermute(guard, "aperture", completed([(d, d - 1) for d in range(1, count, 2)], count))
    far = lax.ppermute(guard, "aperture", completed([(d, d - 1) for d in range(2, count, 2)], count))
    rim = lax.ppermute(rim, "tile", completed([(t, t - 1) for t in range(1, tiles)], tiles))
    steps = [(d * tiles + t, (d - 1) * tiles + t - 1) for d in range(1, count) for t in range(1, tiles)]
    corner = lax.ppermute(corner, ("aperture", "tile"), completed(steps, count * tiles))
    w = call(toeplitz_kernel, sds((2, 2 * width, 2 * width), bf16), [taps])
    tables = [
        call(
            functools.partial(table_kernel, s, level),
            [sds((2, beams, 3 * beams), bf16), sds((2, 2, beams, bins), f32)],
            [offsets, jnp.swapaxes(coef, 2, 3), slope, base],
            scratch=[pltpu.VMEM((2 * beams, 2 * beams), f32)],
            flops=20_000_000,
        )
        for s in range(2)
    ]

    def partner(value, bit):
        return lax.ppermute(value, "aperture", [(d, d ^ (1 << bit)) for d in range(count)])

    half = bins // width // 2 * width
    plan = [[half], [bins - half]] if half else [[bins]]
    subs = []
    first = 0
    for sizes in plan:
        size = sum(sizes)
        has_rim = first + size == bins
        rows = pulses + guards
        args = [raw, near, far] + ([rim, corner] if has_rim else []) + [w, steering]
        subs.append(
            call(
                functools.partial(focus_kernel, first, has_rim, [size]),
                [sds((2, beams, size), bf16)] * 2,
                args,
                scratch=[pltpu.VMEM(((size // width + 1) * rows, 2 * width), bf16)],
                flops=rows * size * 4 * width * 4,
                after=[subs[-1][0]] if subs else [],
            )
        )
        first += size
    others = [partner(high, level) for high, _ in subs]
    chunks, seconds = [], []
    first = 0
    for sizes, (high, low), other in zip(plan, subs, others):
        local = 0
        for size in sizes:
            seconds.append(
                call(
                    functools.partial(first_merge_kernel, first + local, local),
                    [sds((2, beams, size), bf16)] * 2,
                    [high, low, other, *tables[0]],
                    flops=beams * size * beams * 40,
                    after=[seconds[-1][0] if seconds else subs[-1][0]],
                )
            )
            chunks.append((first + local, size))
            local += size
        first += local
    others = [partner(high, level + 1) for high, _ in seconds]
    image = None
    for (first, size), (high, low), other in zip(chunks, seconds, others):
        args = [high, low, other, *tables[1]] + ([] if image is None else [image])
        image = call(
            functools.partial(last_merge_kernel, first),
            sds((2, beams, bins), f32),
            args,
            scratch=[pltpu.VMEM((2, beams, size), f32), pltpu.SemaphoreType.DMA((2,))],
            aliases={} if image is None else {5: 0},
            in_specs=[whole] * 5 + ([] if image is None else [anywhere]),
            out_specs=anywhere,
            flops=beams * size * beams * 40,
        )
    return image


def solution(mesh):
    placed = (P(None, "aperture", "tile"), P(), P(), P(), P(), P(), P())
    return jax.shard_map(
        shards, mesh=mesh, in_specs=placed, out_specs=P(None, "aperture", "tile"), check_vma=False
    )
```

time: 33.4 us -> 31.8 us (0.952)
  waiting for transfers between devices: 7.73 us -> 12 us
  starting transfers between devices: 15.2 us -> 12.5 us
  local copies, waits for them, and re-layouts: 3.61 us -> 1.07 us
  Pallas kernels: 6.33 us -> 5.96 us
    ppermute x4, starting transfers between devices: 11.4 us -> 7.36 us  [partner(): lax.ppermute(value, 'aperture', [(d, d ^ 1 << bit) for d in range(count)])]
    unnamed x18 -> x16, local copies, waits for them, and re-layouts: 3.61 us -> 1.07 us
    ppermute x4, waiting for transfers between devices: 7.73 us -> 10.2 us  [partner(): lax.ppermute(value, 'aperture', [(d, d ^ 1 << bit) for d in range(count)])]
    ppermute x3 -> x4, waiting for transfers between devices: 0.01 us -> 1.87 us  [the longest x1 1.86 us: shards(): lax.ppermute(guard, 'aperture', completed([(d, d - 1) for d in range(2, c...]
    ppermute x3 -> x4, starting transfers between devices: 3.88 us -> 5.1 us  [the longest x1 2.55 us: shards(): lax.ppermute(guard, 'aperture', completed([(d, d - 1) for d in range(2, c...]
    pallas_call x9 -> x10, Pallas kernels: 6.33 us -> 5.96 us  [call(): pl.pallas_call(body, out_shape=outs, in_specs=in_specs or [whole] * len(a...]
  transfers between devices with their start and end apart: 7 -> 8, of which waited for: 2 -> 4; matrix products, arithmetic and copies ran while one was open for 0% -> 0% of each run, Pallas kernels for 16% -> 15%
where the time goes in v2:
time: 31.8 us; the launch traced here: 31.6 us
  starting transfers between devices  12.5 us (39%)
  waiting for transfers between devices  12 us (38%)
  Pallas kernels  5.96 us (19%)
  local copies, waits for them, and re-layouts  1.07 us (3%)
    ppermute x4, waiting for transfers between devices, partner(): lax.ppermute(value, 'aperture', [(d, d ^ 1 << bit) for d in range(count)])  10.2 us
    ppermute x4, starting transfers between devices, partner(): lax.ppermute(value, 'aperture', [(d, d ^ 1 << bit) for d in range(count)])  7.36 us
    pallas_call x10, Pallas kernels, call(): pl.pallas_call(body, out_shape=outs, in_specs=in_specs or [whole] * len(a...  5.96 us
    ppermute x1, starting transfers between devices, shards(): lax.ppermute(guard, 'aperture', completed([(d, d - 1) for d in range(2, c...  2.55 us
    ppermute x1, waiting for transfers between devices, shards(): lax.ppermute(guard, 'aperture', completed([(d, d - 1) for d in range(2, c...  1.86 us
    ppermute x1, starting transfers between devices, shards(): lax.ppermute(rim, 'tile', completed([(t, t - 1) for t in range(1, tiles)]...  1.52 us
    unnamed x16, local copies, waits for them, and re-layouts  1.07 us
  transfers between devices with their start and end apart: 8, of which 4 were waited for; matrix products, arithmetic and copies ran while one was open for 0% of the time, Pallas kernels for 15%

profile of v2, /device:TPU:0, one launch (start us, length us, event | category | flops | bytes accessed | tf_op | source)
XLA Modules:
  0.0 31.6 jit_solution(3292155632034041819)
XLA Ops:
  0.0 0.0 copy-start
  0.0 1.0 %copy-done = bf16[2,128,1024]{2,1,0:T(8,128)(2,1)S(1)} copy-done((bf16[2,128,1024]{2,1,0:T(8,128)(2,1)S(1)}, bf16[2,128,1024]{2,1,0:T(8,128)(2,1)}, u32[]{:S(2)}) %copy-start) | copy-done | bytes 524312
  1.0 0.1 shard_map.73
  1.2 0.5 %collective-permute-start = (bf16[2,32,1024]{2,1,0:T(8,128)(2,1)S(1)}, bf16[2,32,1024]{2,1,0:T(8,128)(2,1)S(1)}, u32[]{:S(2)}, u32[]{:S(2)}) collective-permute-start(bf16[2,32,1024]{2,1,0:T(8,128)(2,1)S(1)} %get-tuple-element.20), channel_id=1, source_target_pairs={{0,2},{2,0},{4,6},{6,4},{8,10},{10,8},{12,14},{14,12},{16,18},{18,... | collective-permute-start | bytes 393224 | tf_op jit(solution)/shard_map/ppermute | solution.py:257
  1.7 2.6 %collective-permute-start.1 = (bf16[2,32,1024]{2,1,0:T(8,128)(2,1)S(1)}, bf16[2,32,1024]{2,1,0:T(8,128)(2,1)S(1)}, u32[]{:S(2)}, u32[]{:S(2)}) collective-permute-start(bf16[2,32,1024]{2,1,0:T(8,128)(2,1)S(1)} %get-tuple-element.20), channel_id=1, source_target_pairs={{0,4},{2,0},{4,2},{6,8},{8,6},{10,12},{12,10},{14,16},{16,14},{18,... | collective-permute-start | bytes 393224 | tf_op jit(solution)/shard_map/ppermute | solution.py:258
  4.2 0.0 copy-start.3
  4.2 1.5 %collective-permute-start.2 = (bf16[2,128,256]{2,1,0:T(8,128)(2,1)S(1)}, bf16[2,128,256]{2,1,0:T(8,128)(2,1)S(1)}, u32[]{:S(2)}, u32[]{:S(2)}) collective-permute-start(bf16[2,128,256]{2,1,0:T(8,128)(2,1)S(1)} %get-tuple-element.21), channel_id=1, source_target_pairs={{0,1},{1,0},{2,3},{3,2},{4,5},{5,4},{6,7},{7,6},{8,9},{9,8},{10,11... | collective-permute-start | bytes 393224 | tf_op jit(solution)/shard_map/ppermute | solution.py:259
  5.8 0.0 copy-start.1
  5.8 0.0 copy-start.2
  5.8 0.5 %collective-permute-start.3 = (bf16[2,32,256]{2,1,0:T(8,128)(2,1)S(1)}, bf16[2,32,256]{2,1,0:T(8,128)(2,1)S(1)}, u32[]{:S(2)}, u32[]{:S(2)}) collective-permute-start(bf16[2,32,256]{2,1,0:T(8,128)(2,1)S(1)} %get-tuple-element.22), channel_id=1, source_target_pairs={{0,1},{1,3},{2,5},{3,0},{4,7},{5,2},{6,9},{7,4},{8,11},{9,6},{10,1... | collective-permute-start | bytes 98312 | tf_op jit(solution)/shard_map/ppermute | solution.py:261
  6.3 0.0 copy-done.3
  6.3 0.2 shard_map.74.refs_3_.refs_5_
  6.5 0.0 collective-permute-done.refs_1_
  6.5 1.9 %collective-permute-done.1.refs_2_ = bf16[2,32,1024]{2,1,0:T(8,128)(2,1)S(1)} collective-permute-done((bf16[2,32,1024]{2,1,0:T(8,128)(2,1)S(1)}, bf16[2,32,1024]{2,1,0:T(8,128)(2,1)S(1)}, u32[]{:S(2)}, u32[]{:S(2)}) %collective-permute-start.1) | collective-permute-done | bytes 131104 | tf_op jit(solution)/shard_map/ppermute | solution.py:258
  8.4 0.0 copy-done.1
  8.4 0.0 copy-done.2
  8.4 0.7 %shard_map.75 = (bf16[2,64,512]{2,1,0:T(8,128)(2,1)S(1)}, bf16[2,64,512]{2,1,0:T(8,128)(2,1)S(1)}) custom-call(bf16[2,128,1024]{2,1,0:T(8,128)(2,1)S(1)} %copy-done.1, bf16[2,32,1024]{2,1,0:T(8,128)(2,1)S(1)} %collective-permute-done.refs_1_, bf16[2,32,1024]{2,1,0:T(8,128)(2,1)S(1)} %collective-permute-done.1.refs_2_, ...), custom_call_target="tpu_custom_call" | custom-call | flops 335544320 | tf_op jit(solution)/shard_map/pallas_call | solution.py:26
  9.1 0.0 copy-start.4
  9.1 1.4 %collective-permute-start.5 = (bf16[2,64,512]{2,1,0:T(8,128)(2,1)S(1)}, bf16[2,64,512]{2,1,0:T(8,128)(2,1)S(1)}, u32[]{:S(2)}, u32[]{:S(2)}) collective-permute-start(bf16[2,64,512]{2,1,0:T(8,128)(2,1)S(1)} %get-tuple-element.23.refs_7_.refs_0_), channel_id=1, source_target_pairs={{0,8},{2,10},{4,12},{6,14},{8,0},{10,2},{12,4},{14,6},{16,24},{18,... | collective-permute-start | bytes 393224 | tf_op jit(solution)/shard_map/ppermute | solution.py:275
  10.5 0.0 collective-permute-done.3.refs_4_
  10.5 0.0 collective-permute-done.2.refs_3_
  10.5 0.0 copy-start.6
  10.5 0.0 copy-start.7
  10.5 0.7 %shard_map.76 = (bf16[2,64,512]{2,1,0:T(8,128)(2,1)S(1)}, bf16[2,64,512]{2,1,0:T(8,128)(2,1)S(1)}) custom-call(bf16[2,128,1024]{2,1,0:T(8,128)(2,1)S(1)} %copy-done.1, bf16[2,32,1024]{2,1,0:T(8,128)(2,1)S(1)} %collective-permute-done.refs_1_, bf16[2,32,1024]{2,1,0:T(8,128)(2,1)S(1)} %collective-permute-done.1.refs_2_, ...), custom_call_target="tpu_custom_call" | custom-call | flops 335544320 | tf_op jit(solution)/shard_map/pallas_call | solution.py:26
  11.2 0.0 copy-start.5
  11.3 1.2 %collective-permute-start.4 = (bf16[2,64,512]{2,1,0:T(8,128)(2,1)S(1)}, bf16[2,64,512]{2,1,0:T(8,128)(2,1)S(1)}, u32[]{:S(2)}, u32[]{:S(2)}) collective-permute-start(bf16[2,64,512]{2,1,0:T(8,128)(2,1)S(1)} %get-tuple-element.24.refs_5_.refs_0_), channel_id=1, source_target_pairs={{0,8},{2,10},{4,12},{6,14},{8,0},{10,2},{12,4},{14,6},{16,24},{18,... | collective-permute-start | bytes 393224 | tf_op jit(solution)/shard_map/ppermute | solution.py:275
  12.5 0.0 copy-done.4
  12.5 0.0 copy-done.6
  12.5 0.0 copy-done.7
  12.5 0.0 copy-done.5
  12.5 0.8 %shard_map.77 = (bf16[2,64,192]{2,1,0:T(8,128)(2,1)S(1)}, f32[2,2,64,1024]{3,2,1,0:T(8,128)S(1)}) custom-call(s32[2,2,128]{2,1,0:T(2,128)S(1)} %copy-done.5, f32[2,2,8,128]{3,2,1,0:T(8,128)S(1)} %bitcast.1, f32[2,2,128]{2,1,0:T(2,128)S(1)} %copy-done.6, f32[2,2,128]{2,1,0:T(2,128)S(1)} %copy-done.7), custom_call_target="tpu_custom_call" | custom-call | flops 20000000 | tf_op jit(solution)/shard_map/pallas_call | solution.py:26
  13.3 2.2 %collective-permute-done.5.refs_2_ = bf16[2,64,512]{2,1,0:T(8,128)(2,1)S(1)} collective-permute-done((bf16[2,64,512]{2,1,0:T(8,128)(2,1)S(1)}, bf16[2,64,512]{2,1,0:T(8,128)(2,1)S(1)}, u32[]{:S(2)}, u32[]{:S(2)}) %collective-permute-start.5) | collective-permute-done | bytes 131104 | tf_op jit(solution)/shard_map/ppermute | solution.py:275
  15.5 0.3 shard_map.78
  15.8 2.3 %collective-permute-start.7 = (bf16[2,64,512]{2,1,0:T(8,128)(2,1)S(1)}, bf16[2,64,512]{2,1,0:T(8,128)(2,1)S(1)}, u32[]{:S(2)}, u32[]{:S(2)}) collective-permute-start(bf16[2,64,512]{2,1,0:T(8,128)(2,1)S(1)} %get-tuple-element.29.refs_5_.high), channel_id=1, source_target_pairs={{0,16},{2,18},{4,20},{6,22},{8,24},{10,26},{12,28},{14,30},{16,0},... | collective-permute-start | bytes 393224 | tf_op jit(solution)/shard_map/ppermute | solution.py:275
  18.1 0.0 collective-permute-done.4.refs_2_
  18.1 0.3 shard_map.79
  18.4 2.5 %collective-permute-start.6 = (bf16[2,64,512]{2,1,0:T(8,128)(2,1)S(1)}, bf16[2,64,512]{2,1,0:T(8,128)(2,1)S(1)}, u32[]{:S(2)}, u32[]{:S(2)}) collective-permute-start(bf16[2,64,512]{2,1,0:T(8,128)(2,1)S(1)} %get-tuple-element.30.high), channel_id=1, source_target_pairs={{0,16},{2,18},{4,20},{6,22},{8,24},{10,26},{12,28},{14,30},{16,0},... | collective-permute-start | bytes 393224 | tf_op jit(solution)/shard_map/ppermute | solution.py:275
  20.9 0.8 %shard_map.80 = (bf16[2,64,192]{2,1,0:T(8,128)(2,1)S(1)}, f32[2,2,64,1024]{3,2,1,0:T(8,128)S(1)}) custom-call(s32[2,2,128]{2,1,0:T(2,128)S(1)} %copy-done.5, f32[2,2,8,128]{3,2,1,0:T(8,128)S(1)} %bitcast.2, f32[2,2,128]{2,1,0:T(2,128)S(1)} %copy-done.6, f32[2,2,128]{2,1,0:T(2,128)S(1)} %copy-done.7), custom_call_target="tpu_custom_call" | custom-call | flops 20000000 | tf_op jit(solution)/shard_map/pallas_call | solution.py:26
  21.7 7.1 %collective-permute-done.7.other = bf16[2,64,512]{2,1,0:T(8,128)(2,1)S(1)} collective-permute-done((bf16[2,64,512]{2,1,0:T(8,128)(2,1)S(1)}, bf16[2,64,512]{2,1,0:T(8,128)(2,1)S(1)}, u32[]{:S(2)}, u32[]{:S(2)}) %collective-permute-start.7) | collective-permute-done | bytes 131104 | tf_op jit(solution)/shard_map/ppermute | solution.py:275
  28.8 1.0 %shard_map.81.refs_0_ = f32[2,64,1024]{2,1,0:T(8,128)} custom-call(bf16[2,64,512]{2,1,0:T(8,128)(2,1)S(1)} %get-tuple-element.29.refs_5_.high, bf16[2,64,512]{2,1,0:T(8,128)(2,1)S(1)} %get-tuple-element.34.low, bf16[2,64,512]{2,1,0:T(8,128)(2,1)S(1)} %collective-permute-done.7.other, bf16[2,64,192]{2,1,0:T(8,128)(2,1)S(1)} %get-tuple-element.32.m, ...), custom_call_target="tpu_custom_call" | custom-call | flops 83886080 | tf_op jit(solution)/shard_map/pallas_call | solution.py:26
  29.8 0.9 %collective-permute-done.6.other = bf16[2,64,512]{2,1,0:T(8,128)(2,1)S(1)} collective-permute-done((bf16[2,64,512]{2,1,0:T(8,128)(2,1)S(1)}, bf16[2,64,512]{2,1,0:T(8,128)(2,1)S(1)}, u32[]{:S(2)}, u32[]{:S(2)}) %collective-permute-start.6) | collective-permute-done | bytes 131104 | tf_op jit(solution)/shard_map/ppermute | solution.py:275
  30.6 1.0 %shard_map.82 = f32[2,64,1024]{2,1,0:T(8,128)} custom-call(bf16[2,64,512]{2,1,0:T(8,128)(2,1)S(1)} %get-tuple-element.30.high, bf16[2,64,512]{2,1,0:T(8,128)(2,1)S(1)} %get-tuple-element.31.low, bf16[2,64,512]{2,1,0:T(8,128)(2,1)S(1)} %collective-permute-done.6.other, bf16[2,64,192]{2,1,0:T(8,128)(2,1)S(1)} %get-tuple-element.32.m, ...), custom_call_target="tpu_custom_call", output_to_operand_aliasing={{}: (5, {})} | custom-call | flops 83886080 | tf_op jit(solution)/shard_map/pallas_call | solution.py:26
Async XLA Ops:
  0.0 1.0 %copy-start = (bf16[2,128,1024]{2,1,0:T(8,128)(2,1)S(1)}, bf16[2,128,1024]{2,1,0:T(8,128)(2,1)}, u32[]{:S(2)}) copy-start(bf16[2,128,1024]{2,1,0:T(8,128)(2,1)} %refs_0_.3) | copy-start | bytes 1572868
  1.2 5.3 %collective-permute-start = (bf16[2,32,1024]{2,1,0:T(8,128)(2,1)S(1)}, bf16[2,32,1024]{2,1,0:T(8,128)(2,1)S(1)}, u32[]{:S(2)}, u32[]{:S(2)}) collective-permute-start(bf16[2,32,1024]{2,1,0:T(8,128)(2,1)S(1)} %get-tuple-element.20), channel_id=1, source_target_pairs={{0,2},{2,0},{4,6},{6,4},{8,10},{10,8},{12,14},{14,12},{16,18},{18,... | collective-permute-start | bytes 393224 | tf_op jit(solution)/shard_map/ppermute | solution.py:257
  1.7 6.7 %collective-permute-start.1 = (bf16[2,32,1024]{2,1,0:T(8,128)(2,1)S(1)}, bf16[2,32,1024]{2,1,0:T(8,128)(2,1)S(1)}, u32[]{:S(2)}, u32[]{:S(2)}) collective-permute-start(bf16[2,32,1024]{2,1,0:T(8,128)(2,1)S(1)} %get-tuple-element.20), channel_id=1, source_target_pairs={{0,4},{2,0},{4,2},{6,8},{8,6},{10,12},{12,10},{14,16},{16,14},{18,... | collective-permute-start | bytes 393224 | tf_op jit(solution)/shard_map/ppermute | solution.py:258
  4.2 2.0 %copy-start.3 = (bf16[2,256]{1,0:T(2,128)(2,1)S(1)}, bf16[2,256]{1,0:T(2,128)(2,1)}, u32[]{:S(2)}) copy-start(bf16[2,256]{1,0:T(2,128)(2,1)} %taps_ref.1) | copy-start | bytes 3076
  4.2 6.3 %collective-permute-start.2 = (bf16[2,128,256]{2,1,0:T(8,128)(2,1)S(1)}, bf16[2,128,256]{2,1,0:T(8,128)(2,1)S(1)}, u32[]{:S(2)}, u32[]{:S(2)}) collective-permute-start(bf16[2,128,256]{2,1,0:T(8,128)(2,1)S(1)} %get-tuple-element.21), channel_id=1, source_target_pairs={{0,1},{1,0},{2,3},{3,2},{4,5},{5,4},{6,7},{7,6},{8,9},{9,8},{10,11... | collective-permute-start | bytes 393224 | tf_op jit(solution)/shard_map/ppermute | solution.py:259
  5.8 2.6 %copy-start.1 = (bf16[2,128,1024]{2,1,0:T(8,128)(2,1)S(1)}, bf16[2,128,1024]{2,1,0:T(8,128)(2,1)}, u32[]{:S(2)}) copy-start(bf16[2,128,1024]{2,1,0:T(8,128)(2,1)} %refs_0_.3) | copy-start | bytes 1572868
  5.8 2.6 %copy-start.2 = (bf16[2,64,160]{2,1,0:T(8,128)(2,1)S(1)}, bf16[2,64,160]{2,1,0:T(8,128)(2,1)}, u32[]{:S(2)}) copy-start(bf16[2,64,160]{2,1,0:T(8,128)(2,1)} %refs_6_.1) | copy-start | bytes 122884
  5.8 4.7 %collective-permute-start.3 = (bf16[2,32,256]{2,1,0:T(8,128)(2,1)S(1)}, bf16[2,32,256]{2,1,0:T(8,128)(2,1)S(1)}, u32[]{:S(2)}, u32[]{:S(2)}) collective-permute-start(bf16[2,32,256]{2,1,0:T(8,128)(2,1)S(1)} %get-tuple-element.22), channel_id=1, source_target_pairs={{0,1},{1,3},{2,5},{3,0},{4,7},{5,2},{6,9},{7,4},{8,11},{9,6},{10,1... | collective-permute-start | bytes 98312 | tf_op jit(solution)/shard_map/ppermute | solution.py:261
  9.1 3.4 %copy-start.4 = (f32[2,2,128,8]{2,3,1,0:T(8,128)S(1)}, f32[2,2,128,8]{2,3,1,0:T(8,128)}, u32[]{:S(2)}) copy-start(f32[2,2,128,8]{2,3,1,0:T(8,128)} %param.11) | copy-start | bytes 49156
  9.1 6.4 %collective-permute-start.5 = (bf16[2,64,512]{2,1,0:T(8,128)(2,1)S(1)}, bf16[2,64,512]{2,1,0:T(8,128)(2,1)S(1)}, u32[]{:S(2)}, u32[]{:S(2)}) collective-permute-start(bf16[2,64,512]{2,1,0:T(8,128)(2,1)S(1)} %get-tuple-element.23.refs_7_.refs_0_), channel_id=1, source_target_pairs={{0,8},{2,10},{4,12},{6,14},{8,0},{10,2},{12,4},{14,6},{16,24},{18,... | collective-permute-start | bytes 393224 | tf_op jit(solution)/shard_map/ppermute | solution.py:275
  10.5 2.0 %copy-start.6 = (f32[2,2,128]{2,1,0:T(2,128)S(1)}, f32[2,2,128]{2,1,0:T(2,128)}, u32[]{:S(2)}) copy-start(f32[2,2,128]{2,1,0:T(2,128)} %slope_ref.3) | copy-start | bytes 6148
  10.5 2.0 %copy-start.7 = (f32[2,2,128]{2,1,0:T(2,128)S(1)}, f32[2,2,128]{2,1,0:T(2,128)}, u32[]{:S(2)}) copy-start(f32[2,2,128]{2,1,0:T(2,128)} %base_ref.3) | copy-start | bytes 6148
  11.2 1.2 %copy-start.5 = (s32[2,2,128]{2,1,0:T(2,128)S(1)}, s32[2,2,128]{2,1,0:T(2,128)}, u32[]{:S(2)}) copy-start(s32[2,2,128]{2,1,0:T(2,128)} %offsets_ref.3) | copy-start | bytes 6148
  11.3 6.9 %collective-permute-start.4 = (bf16[2,64,512]{2,1,0:T(8,128)(2,1)S(1)}, bf16[2,64,512]{2,1,0:T(8,128)(2,1)S(1)}, u32[]{:S(2)}, u32[]{:S(2)}) collective-permute-start(bf16[2,64,512]{2,1,0:T(8,128)(2,1)S(1)} %get-tuple-element.24.refs_5_.refs_0_), channel_id=1, source_target_pairs={{0,8},{2,10},{4,12},{6,14},{8,0},{10,2},{12,4},{14,6},{16,24},{18,... | collective-permute-start | bytes 393224 | tf_op jit(solution)/shard_map/ppermute | solution.py:275
  15.8 12.9 %collective-permute-start.7 = (bf16[2,64,512]{2,1,0:T(8,128)(2,1)S(1)}, bf16[2,64,512]{2,1,0:T(8,128)(2,1)S(1)}, u32[]{:S(2)}, u32[]{:S(2)}) collective-permute-start(bf16[2,64,512]{2,1,0:T(8,128)(2,1)S(1)} %get-tuple-element.29.refs_5_.high), channel_id=1, source_target_pairs={{0,16},{2,18},{4,20},{6,22},{8,24},{10,26},{12,28},{14,30},{16,0},... | collective-permute-start | bytes 393224 | tf_op jit(solution)/shard_map/ppermute | solution.py:275
  18.4 12.2 %collective-permute-start.6 = (bf16[2,64,512]{2,1,0:T(8,128)(2,1)S(1)}, bf16[2,64,512]{2,1,0:T(8,128)(2,1)S(1)}, u32[]{:S(2)}, u32[]{:S(2)}) collective-permute-start(bf16[2,64,512]{2,1,0:T(8,128)(2,1)S(1)} %get-tuple-element.30.high), channel_id=1, source_target_pairs={{0,16},{2,18},{4,20},{6,22},{8,24},{10,26},{12,28},{14,30},{16,0},... | collective-permute-start | bytes 393224 | tf_op jit(solution)/shard_map/ppermute | solution.py:275

commit v3 on v2

--- a/solution.py
+++ b/solution.py
@@ -9,6 +9,8 @@
 from jax.sharding import PartitionSpec as P
 
 LANES = 128
+M0 = 2_000_000_000
+F0 = 2_000_000_000
 VMEM = pltpu.CompilerParams(vmem_limit_bytes=24 * 1024 * 1024)
 
 
@@ -180,18 +182,17 @@
                 ref[1, :, at : at + LANES] = value[beams:]
 
 
-def merged(first, local, bins, high, low, other, m, e):
+def merged(first, bins, high, low, other, m, e):
     beams = high.shape[1]
-    here = slice(local, local + bins)
     at = slice(first, first + bins)
     own_m = m[0]
     other_m = m[1][:, : 2 * beams]
     own, got = [], []
     for part in range(2):
-        x = high[part, :, here]
-        x = jnp.concatenate([x, x, low[part, :, here]], 0)
+        x = high[part]
+        x = jnp.concatenate([x, x, low[part]], 0)
         own.append(jnp.dot(own_m, x, preferred_element_type=jnp.float32))
-        y = other[part, :, here]
+        y = other[part]
         y = jnp.concatenate([y, y], 0)
         got.append(jnp.dot(other_m, y, preferred_element_type=jnp.float32))
     c0, s0 = e[0, 0, :, at], e[0, 1, :, at]
@@ -201,9 +202,13 @@
     return re, im
 
 
-def first_merge_kernel(first, local, high, low, other, m, e, high_ref, low_ref):
+def first_merge_kernel(first, high, low, other, m, e, *refs):
+    if len(refs) == 4:
+        refs[3][...] = refs[0][...]
+        refs = refs[1:3]
+    high_ref, low_ref = refs
     bins = high_ref.shape[2]
-    for part, value in enumerate(merged(first, local, bins, high, low, other, m, e)):
+    for part, value in enumerate(merged(first, bins, high, low, other, m, e)):
         top, rest = split(value)
         high_ref[part] = top
         low_ref[part] = rest
@@ -212,7 +217,7 @@
 def last_merge_kernel(first, high, low, other, m, e, *refs):
     image, held, sem = refs[-3:]
     copies = []
-    for part, value in enumerate(merged(first, 0, held.shape[2], high, low, other, m, e)):
+    for part, value in enumerate(merged(first, held.shape[2], high, low, other, m, e)):
         held[part] = value
         place = image.at[part, :, first : first + held.shape[2]]
         copies.append(pltpu.make_async_copy(held.at[part], place, sem.at[part]))
@@ -260,62 +265,63 @@
     steps = [(d * tiles + t, (d - 1) * tiles + t - 1) for d in range(1, count) for t in range(1, tiles)]
     corner = lax.ppermute(corner, ("aperture", "tile"), completed(steps, count * tiles))
     w = call(toeplitz_kernel, sds((2, 2 * width, 2 * width), bf16), [taps])
-    tables = [
-        call(
+    def tables(s, after=()):
+        return call(
             functools.partial(table_kernel, s, level),
             [sds((2, beams, 3 * beams), bf16), sds((2, 2, beams, bins), f32)],
             [offsets, jnp.swapaxes(coef, 2, 3), slope, base],
             scratch=[pltpu.VMEM((2 * beams, 2 * beams), f32)],
             flops=20_000_000,
-        )
-        for s in range(2)
-    ]
+            after=after,
+        )
+
+    first_tables = tables(0)
 
     def partner(value, bit):
         return lax.ppermute(value, "aperture", [(d, d ^ (1 << bit)) for d in range(count)])
 
-    half = bins // width // 2 * width
-    plan = [[half], [bins - half]] if half else [[bins]]
+    blocks = bins // width
+    plan = [[width], [(bins - width) // 2 // LANES * LANES, bins - width - (bins - width) // 2 // LANES * LANES]] if blocks > 2 else [[bins]]
     subs = []
+    chunks = []
     first = 0
     for sizes in plan:
         size = sum(sizes)
         has_rim = first + size == bins
         rows = pulses + guards
         args = [raw, near, far] + ([rim, corner] if has_rim else []) + [w, steering]
-        subs.append(
-            call(
-                functools.partial(focus_kernel, first, has_rim, [size]),
-                [sds((2, beams, size), bf16)] * 2,
-                args,
-                scratch=[pltpu.VMEM(((size // width + 1) * rows, 2 * width), bf16)],
-                flops=rows * size * 4 * width * 4,
-                after=[subs[-1][0]] if subs else [],
-            )
-        )
-        first += size
-    others = [partner(high, level) for high, _ in subs]
-    chunks, seconds = [], []
-    first = 0
-    for sizes, (high, low), other in zip(plan, subs, others):
-        local = 0
-        for size in sizes:
-            seconds.append(
-                call(
-                    functools.partial(first_merge_kernel, first + local, local),
-                    [sds((2, beams, size), bf16)] * 2,
-                    [high, low, other, *tables[0]],
-                    flops=beams * size * beams * 40,
-                    after=[seconds[-1][0] if seconds else subs[-1][0]],
-                )
-            )
-            chunks.append((first + local, size))
-            local += size
-        first += local
+        found = call(
+            functools.partial(focus_kernel, first, has_rim, sizes),
+            [sds((2, beams, part), bf16) for part in sizes for _ in range(2)],
+            args,
+            scratch=[pltpu.VMEM(((size // width + 1) * rows, 2 * width), bf16)],
+            flops=rows * size * 4 * width * 4,
+            after=[subs[-1][0] if subs else first_tables[0]],
+        )
+        for n, part in enumerate(sizes):
+            subs.append(found[2 * n : 2 * n + 2])
+            chunks.append((first, part))
+            first += part
+    others = [partner(high, level) for high, _ in subs[:2]]
+    seconds = []
+    for n, (first, size) in enumerate(chunks):
+        through = [subs[2][0]] if n == 0 and len(chunks) > 2 else []
+        outs = [sds((2, beams, size), bf16)] * 2 + [sds(x.shape, bf16) for x in through]
+        found = call(
+            functools.partial(first_merge_kernel, first),
+            outs,
+            [*subs[n], others[n], *first_tables, *through],
+            flops=beams * size * beams * 40 if seconds else M0,
+            after=[seconds[-1][0] if seconds else subs[-1][0]],
+        )
+        seconds.append(found[:2])
+        if through:
+            others.append(partner(found[2], level))
     others = [partner(high, level + 1) for high, _ in seconds]
+    last_tables = tables(1, [seconds[min(1, len(seconds) - 1)][0]])
     image = None
     for (first, size), (high, low), other in zip(chunks, seconds, others):
-        args = [high, low, other, *tables[1]] + ([] if image is None else [image])
+        args = [high, low, other, *last_tables] + ([] if image is None else [image])
         image = call(
             functools.partial(last_merge_kernel, first),
             sds((2, beams, bins), f32),
@@ -324,7 +330,7 @@
             aliases={} if image is None else {5: 0},
             in_specs=[whole] * 5 + ([] if image is None else [anywhere]),
             out_specs=anywhere,
-            flops=beams * size * beams * 40,
+            flops=F0,
         )
     return image
 

time: 31.8 us -> 30.3 us (0.953)
  waiting for transfers between devices: 12 us -> 6.41 us
  starting transfers between devices: 12.5 us -> 15.6 us
  Pallas kernels: 5.96 us -> 6.88 us
    ppermute x4 -> x6, waiting for transfers between devices: 10.2 us -> 5.06 us  [partner(): lax.ppermute(value, 'aperture', [(d, d ^ 1 << bit) for d in range(count)])]
    ppermute x4 -> x6, starting transfers between devices: 7.36 us -> 10.5 us  [partner(): lax.ppermute(value, 'aperture', [(d, d ^ 1 << bit) for d in range(count)])]
    ppermute x1, waiting for transfers between devices: 1.86 us -> 0.8 us  [shards(): lax.ppermute(guard, 'aperture', completed([(d, d - 1) for d in range(2, c...]
    pallas_call x10 -> x12, Pallas kernels: 5.96 us -> 6.88 us  [call(): pl.pallas_call(body, out_shape=outs, in_specs=in_specs or [whole] * len(a...]
    ppermute x1, starting transfers between devices: 0.52 us -> 0.01 us  [shards(): lax.ppermute(guard, 'aperture', completed([(d, d - 1) for d in range(1, c...]
    ppermute x1, waiting for transfers between devices: 0.01 us -> 0.51 us  [shards(): lax.ppermute(corner, ('aperture', 'tile'), completed(steps, count * tiles))]
    ppermute x1, starting transfers between devices: 2.55 us -> 2.99 us  [shards(): lax.ppermute(guard, 'aperture', completed([(d, d - 1) for d in range(2, c...]
  transfers between devices with their start and end apart: 8 -> 10, of which waited for: 4 -> 5; matrix products, arithmetic and copies ran while one was open for 0% -> 0% of each run, Pallas kernels for 15% -> 19%
where the time goes in v3:
time: 30.3 us; the launch traced here: 30.1 us
  starting transfers between devices  15.6 us (51%)
  Pallas kernels  6.88 us (23%)
  waiting for transfers between devices  6.41 us (21%)
  local copies, waits for them, and re-layouts  1.07 us (4%)
    ppermute x6, starting transfers between devices, partner(): lax.ppermute(value, 'aperture', [(d, d ^ 1 << bit) for d in range(count)])  10.5 us
    pallas_call x12, Pallas kernels, call(): pl.pallas_call(body, out_shape=outs, in_specs=in_specs or [whole] * len(a...  6.88 us
    ppermute x6, waiting for transfers between devices, partner(): lax.ppermute(value, 'aperture', [(d, d ^ 1 << bit) for d in range(count)])  5.06 us
    ppermute x1, starting transfers between devices, shards(): lax.ppermute(guard, 'aperture', completed([(d, d - 1) for d in range(2, c...  2.99 us
    ppermute x1, starting transfers between devices, shards(): lax.ppermute(rim, 'tile', completed([(t, t - 1) for t in range(1, tiles)]...  1.52 us
    unnamed x16, local copies, waits for them, and re-layouts  1.07 us
    ppermute x1, waiting for transfers between devices, shards(): lax.ppermute(guard, 'aperture', completed([(d, d - 1) for d in range(2, c...  0.8 us
  transfers between devices with their start and end apart: 10, of which 5 were waited for; matrix products, arithmetic and copies ran while one was open for 0% of the time, Pallas kernels for 19%

profile of v3, /device:TPU:0, one launch (start us, length us, event | category | flops | bytes accessed | tf_op | source)
XLA Modules:
  0.0 30.1 jit_solution(14292220939873908724)
XLA Ops:
  0.0 0.0 copy-start
  0.0 1.0 %copy-done = bf16[2,128,1024]{2,1,0:T(8,128)(2,1)S(1)} copy-done((bf16[2,128,1024]{2,1,0:T(8,128)(2,1)S(1)}, bf16[2,128,1024]{2,1,0:T(8,128)(2,1)}, u32[]{:S(2)}) %copy-start) | copy-done | bytes 524312
  1.0 0.1 shard_map.73
  1.2 3.0 %collective-permute-start.1 = (bf16[2,32,1024]{2,1,0:T(8,128)(2,1)S(1)}, bf16[2,32,1024]{2,1,0:T(8,128)(2,1)S(1)}, u32[]{:S(2)}, u32[]{:S(2)}) collective-permute-start(bf16[2,32,1024]{2,1,0:T(8,128)(2,1)S(1)} %get-tuple-element.25), channel_id=1, source_target_pairs={{0,4},{2,0},{4,2},{6,8},{8,6},{10,12},{12,10},{14,16},{16,14},{18,... | collective-permute-start | bytes 393224 | tf_op jit(solution)/shard_map/ppermute | solution.py:263
  4.2 0.0 collective-permute-start
  4.2 0.0 copy-start.7
  4.2 1.5 %collective-permute-start.2 = (bf16[2,128,256]{2,1,0:T(8,128)(2,1)S(1)}, bf16[2,128,256]{2,1,0:T(8,128)(2,1)S(1)}, u32[]{:S(2)}, u32[]{:S(2)}) collective-permute-start(bf16[2,128,256]{2,1,0:T(8,128)(2,1)S(1)} %get-tuple-element.26), channel_id=1, source_target_pairs={{0,1},{1,0},{2,3},{3,2},{4,5},{5,4},{6,7},{7,6},{8,9},{9,8},{10,11... | collective-permute-start | bytes 393224 | tf_op jit(solution)/shard_map/ppermute | solution.py:264
  5.7 0.0 copy-start.3
  5.7 0.0 copy-start.4
  5.7 0.0 copy-start.5
  5.7 0.0 copy-start.6
  5.7 0.0 copy-start.1
  5.7 0.6 %collective-permute-start.3 = (bf16[2,32,256]{2,1,0:T(8,128)(2,1)S(1)}, bf16[2,32,256]{2,1,0:T(8,128)(2,1)S(1)}, u32[]{:S(2)}, u32[]{:S(2)}) collective-permute-start(bf16[2,32,256]{2,1,0:T(8,128)(2,1)S(1)} %get-tuple-element.27), channel_id=1, source_target_pairs={{0,1},{1,3},{2,5},{3,0},{4,7},{5,2},{6,9},{7,4},{8,11},{9,6},{10,1... | collective-permute-start | bytes 98312 | tf_op jit(solution)/shard_map/ppermute | solution.py:266
  6.3 0.0 copy-done.7
  6.3 0.2 shard_map.74.refs_3_.refs_5_
  6.5 0.0 copy-start.2
  6.5 0.0 copy-done.3
  6.5 0.0 copy-done.4
  6.5 0.0 copy-done.5
  6.5 0.0 copy-done.6
  6.5 0.8 %shard_map.75 = (bf16[2,64,192]{2,1,0:T(8,128)(2,1)S(1)}, f32[2,2,64,1024]{3,2,1,0:T(8,128)S(1)}) custom-call(s32[2,2,128]{2,1,0:T(2,128)S(1)} %copy-done.4, f32[2,2,8,128]{3,2,1,0:T(8,128)S(1)} %bitcast.1, f32[2,2,128]{2,1,0:T(2,128)S(1)} %copy-done.5, f32[2,2,128]{2,1,0:T(2,128)S(1)} %copy-done.6), custom_call_target="tpu_custom_call" | custom-call | flops 20000000 | tf_op jit(solution)/shard_map/pallas_call | solution.py:28
  7.4 0.8 %collective-permute-done.1.refs_2_ = bf16[2,32,1024]{2,1,0:T(8,128)(2,1)S(1)} collective-permute-done((bf16[2,32,1024]{2,1,0:T(8,128)(2,1)S(1)}, bf16[2,32,1024]{2,1,0:T(8,128)(2,1)S(1)}, u32[]{:S(2)}, u32[]{:S(2)}) %collective-permute-start.1) | collective-permute-done | bytes 131104 | tf_op jit(solution)/shard_map/ppermute | solution.py:263
  8.2 0.0 collective-permute-done.refs_1_
  8.2 0.0 copy-done.1
  8.2 0.0 copy-done.2
  8.2 0.5 %shard_map.76 = (bf16[2,64,256]{2,1,0:T(8,128)(2,1)S(1)}, bf16[2,64,256]{2,1,0:T(8,128)(2,1)S(1)}) custom-call(bf16[2,128,1024]{2,1,0:T(8,128)(2,1)S(1)} %copy-done.1, bf16[2,32,1024]{2,1,0:T(8,128)(2,1)S(1)} %collective-permute-done.refs_1_, bf16[2,32,1024]{2,1,0:T(8,128)(2,1)S(1)} %collective-permute-done.1.refs_2_, ...), custom_call_target="tpu_custom_call" | custom-call | flops 167772160 | tf_op jit(solution)/shard_map/pallas_call | solution.py:28
  8.7 1.5 %collective-permute-start.4 = (bf16[2,64,256]{2,1,0:T(8,128)(2,1)S(1)}, bf16[2,64,256]{2,1,0:T(8,128)(2,1)S(1)}, u32[]{:S(2)}, u32[]{:S(2)}) collective-permute-start(bf16[2,64,256]{2,1,0:T(8,128)(2,1)S(1)} %get-tuple-element.29.refs_7_.refs_0_), channel_id=1, source_target_pairs={{0,8},{2,10},{4,12},{6,14},{8,0},{10,2},{12,4},{14,6},{16,24},{18,... | collective-permute-start | bytes 196616 | tf_op jit(solution)/shard_map/ppermute | solution.py:281
  10.2 0.5 %collective-permute-done.3.refs_4_ = bf16[2,32,256]{2,1,0:T(8,128)(2,1)S(1)} collective-permute-done((bf16[2,32,256]{2,1,0:T(8,128)(2,1)S(1)}, bf16[2,32,256]{2,1,0:T(8,128)(2,1)S(1)}, u32[]{:S(2)}, u32[]{:S(2)}) %collective-permute-start.3) | collective-permute-done | bytes 32800 | tf_op jit(solution)/shard_map/ppermute | solution.py:266
  10.7 0.0 collective-permute-done.2.refs_3_
  10.8 0.9 %shard_map.77 = (bf16[2,64,384]{2,1,0:T(8,128)(2,1)S(1)}, bf16[2,64,384]{2,1,0:T(8,128)(2,1)S(1)}, bf16[2,64,384]{2,1,0:T(8,128)(2,1)S(1)}, bf16[2,64,384]{2,1,0:T(8,128)(2,1)S(1)}) custom-call(bf16[2,128,1024]{2,1,0:T(8,128)(2,1)S(1)} %copy-done.1, bf16[2,32,1024]{2,1,0:T(8,128)(2,1)S(1)} %collective-permute-done.refs_1_, ...), custom_call_target="tpu_custom_call" | custom-call | flops 503316480 | tf_op jit(solution)/shard_map/pallas_call | solution.py:28
  11.7 1.2 %collective-permute-start.6 = (bf16[2,64,384]{2,1,0:T(8,128)(2,1)S(1)}, bf16[2,64,384]{2,1,0:T(8,128)(2,1)S(1)}, u32[]{:S(2)}, u32[]{:S(2)}) collective-permute-start(bf16[2,64,384]{2,1,0:T(8,128)(2,1)S(1)} %get-tuple-element.35.refs_0_), channel_id=1, source_target_pairs={{0,8},{2,10},{4,12},{6,14},{8,0},{10,2},{12,4},{14,6},{16,24},{18,... | collective-permute-start | bytes 294920 | tf_op jit(solution)/shard_map/ppermute | solution.py:281
  12.9 0.3 collective-permute-done.4.refs_2_
  13.2 0.2 shard_map.78
  13.4 2.7 %collective-permute-start.9 = (bf16[2,64,256]{2,1,0:T(8,128)(2,1)S(1)}, bf16[2,64,256]{2,1,0:T(8,128)(2,1)S(1)}, u32[]{:S(2)}, u32[]{:S(2)}) collective-permute-start(bf16[2,64,256]{2,1,0:T(8,128)(2,1)S(1)} %get-tuple-element.37.refs_5_.high), channel_id=1, source_target_pairs={{0,16},{2,18},{4,20},{6,22},{8,24},{10,26},{12,28},{14,30},{16,0},... | collective-permute-start | bytes 196616 | tf_op jit(solution)/shard_map/ppermute | solution.py:281
  16.1 1.6 %collective-permute-start.5 = (bf16[2,64,384]{2,1,0:T(8,128)(2,1)S(1)}, bf16[2,64,384]{2,1,0:T(8,128)(2,1)S(1)}, u32[]{:S(2)}, u32[]{:S(2)}) collective-permute-start(bf16[2,64,384]{2,1,0:T(8,128)(2,1)S(1)} %get-tuple-element.34), channel_id=1, source_target_pairs={{0,8},{2,10},{4,12},{6,14},{8,0},{10,2},{12,4},{14,6},{16,24},{18,... | collective-permute-start | bytes 294920 | tf_op jit(solution)/shard_map/ppermute | solution.py:281
  17.7 0.0 collective-permute-done.6.refs_2_
  17.7 0.3 shard_map.79
  17.9 1.6 %collective-permute-start.8 = (bf16[2,64,384]{2,1,0:T(8,128)(2,1)S(1)}, bf16[2,64,384]{2,1,0:T(8,128)(2,1)S(1)}, u32[]{:S(2)}, u32[]{:S(2)}) collective-permute-start(bf16[2,64,384]{2,1,0:T(8,128)(2,1)S(1)} %get-tuple-element.38.refs_5_.refs_4_.high), channel_id=1, source_target_pairs={{0,16},{2,18},{4,20},{6,22},{8,24},{10,26},{12,28},{14,30},{16,0},... | collective-permute-start | bytes 294920 | tf_op jit(solution)/shard_map/ppermute | solution.py:281
  19.6 0.8 %shard_map.81 = (bf16[2,64,192]{2,1,0:T(8,128)(2,1)S(1)}, f32[2,2,64,1024]{3,2,1,0:T(8,128)S(1)}) custom-call(s32[2,2,128]{2,1,0:T(2,128)S(1)} %copy-done.4, f32[2,2,8,128]{3,2,1,0:T(8,128)S(1)} %bitcast.2, f32[2,2,128]{2,1,0:T(2,128)S(1)} %copy-done.5, f32[2,2,128]{2,1,0:T(2,128)S(1)} %copy-done.6, ...), custom_call_target="tpu_custom_call" | custom-call | flops 20000000 | tf_op jit(solution)/shard_map/pallas_call | solution.py:28
  20.4 0.0 collective-permute-done.9.other
  20.4 0.9 %shard_map.82.refs_0_ = f32[2,64,1024]{2,1,0:T(8,128)} custom-call(bf16[2,64,256]{2,1,0:T(8,128)(2,1)S(1)} %get-tuple-element.37.refs_5_.high, bf16[2,64,256]{2,1,0:T(8,128)(2,1)S(1)} %get-tuple-element.44.low, bf16[2,64,256]{2,1,0:T(8,128)(2,1)S(1)} %collective-permute-done.9.other, bf16[2,64,192]{2,1,0:T(8,128)(2,1)S(1)} %get-tuple-element.41.m, ...), custom_call_target="tpu_custom_call" | custom-call | flops 2000000000 | tf_op jit(solution)/shard_map/pallas_call | solution.py:28
  21.3 0.0 collective-permute-done.5.refs_2_
  21.3 0.3 shard_map.80
  21.6 1.8 %collective-permute-start.7 = (bf16[2,64,384]{2,1,0:T(8,128)(2,1)S(1)}, bf16[2,64,384]{2,1,0:T(8,128)(2,1)S(1)}, u32[]{:S(2)}, u32[]{:S(2)}) collective-permute-start(bf16[2,64,384]{2,1,0:T(8,128)(2,1)S(1)} %get-tuple-element.39.high), channel_id=1, source_target_pairs={{0,16},{2,18},{4,20},{6,22},{8,24},{10,26},{12,28},{14,30},{16,0},... | collective-permute-start | bytes 294920 | tf_op jit(solution)/shard_map/ppermute | solution.py:281
  23.4 3.6 %collective-permute-done.8.other = bf16[2,64,384]{2,1,0:T(8,128)(2,1)S(1)} collective-permute-done((bf16[2,64,384]{2,1,0:T(8,128)(2,1)S(1)}, bf16[2,64,384]{2,1,0:T(8,128)(2,1)S(1)}, u32[]{:S(2)}, u32[]{:S(2)}) %collective-permute-start.8) | collective-permute-done | bytes 98336 | tf_op jit(solution)/shard_map/ppermute | solution.py:281
  27.0 0.9 %shard_map.83.refs_0_ = f32[2,64,1024]{2,1,0:T(8,128)} custom-call(bf16[2,64,384]{2,1,0:T(8,128)(2,1)S(1)} %get-tuple-element.38.refs_5_.refs_4_.high, bf16[2,64,384]{2,1,0:T(8,128)(2,1)S(1)} %get-tuple-element.43.low, bf16[2,64,384]{2,1,0:T(8,128)(2,1)S(1)} %collective-permute-done.8.other, ...), custom_call_target="tpu_custom_call", output_to_operand_aliasing={{}: (5, {})} | custom-call | flops 2000000000 | tf_op jit(solution)/shard_map/pallas_call | solution.py:28
  27.9 1.2 %collective-permute-done.7.other = bf16[2,64,384]{2,1,0:T(8,128)(2,1)S(1)} collective-permute-done((bf16[2,64,384]{2,1,0:T(8,128)(2,1)S(1)}, bf16[2,64,384]{2,1,0:T(8,128)(2,1)S(1)}, u32[]{:S(2)}, u32[]{:S(2)}) %collective-permute-start.7) | collective-permute-done | bytes 98336 | tf_op jit(solution)/shard_map/ppermute | solution.py:281
  29.2 0.9 %shard_map.84 = f32[2,64,1024]{2,1,0:T(8,128)} custom-call(bf16[2,64,384]{2,1,0:T(8,128)(2,1)S(1)} %get-tuple-element.39.high, bf16[2,64,384]{2,1,0:T(8,128)(2,1)S(1)} %get-tuple-element.40.low, bf16[2,64,384]{2,1,0:T(8,128)(2,1)S(1)} %collective-permute-done.7.other, bf16[2,64,192]{2,1,0:T(8,128)(2,1)S(1)} %get-tuple-element.41.m, ...), custom_call_target="tpu_custom_call", output_to_operand_aliasing={{}: (5, {})} | custom-call | flops 2000000000 | tf_op jit(solution)/shard_map/pallas_call | solution.py:28
Async XLA Ops:
  0.0 1.0 %copy-start = (bf16[2,128,1024]{2,1,0:T(8,128)(2,1)S(1)}, bf16[2,128,1024]{2,1,0:T(8,128)(2,1)}, u32[]{:S(2)}) copy-start(bf16[2,128,1024]{2,1,0:T(8,128)(2,1)} %refs_0_.4) | copy-start | bytes 1572868
  1.2 7.0 %collective-permute-start.1 = (bf16[2,32,1024]{2,1,0:T(8,128)(2,1)S(1)}, bf16[2,32,1024]{2,1,0:T(8,128)(2,1)S(1)}, u32[]{:S(2)}, u32[]{:S(2)}) collective-permute-start(bf16[2,32,1024]{2,1,0:T(8,128)(2,1)S(1)} %get-tuple-element.25), channel_id=1, source_target_pairs={{0,4},{2,0},{4,2},{6,8},{8,6},{10,12},{12,10},{14,16},{16,14},{18,... | collective-permute-start | bytes 393224 | tf_op jit(solution)/shard_map/ppermute | solution.py:263
  4.2 4.0 %collective-permute-start = (bf16[2,32,1024]{2,1,0:T(8,128)(2,1)S(1)}, bf16[2,32,1024]{2,1,0:T(8,128)(2,1)S(1)}, u32[]{:S(2)}, u32[]{:S(2)}) collective-permute-start(bf16[2,32,1024]{2,1,0:T(8,128)(2,1)S(1)} %get-tuple-element.25), channel_id=1, source_target_pairs={{0,2},{2,0},{4,6},{6,4},{8,10},{10,8},{12,14},{14,12},{16,18},{18,... | collective-permute-start | bytes 393224 | tf_op jit(solution)/shard_map/ppermute | solution.py:262
  4.2 2.1 %copy-start.7 = (bf16[2,256]{1,0:T(2,128)(2,1)S(1)}, bf16[2,256]{1,0:T(2,128)(2,1)}, u32[]{:S(2)}) copy-start(bf16[2,256]{1,0:T(2,128)(2,1)} %taps_ref.1) | copy-start | bytes 3076
  4.2 6.6 %collective-permute-start.2 = (bf16[2,128,256]{2,1,0:T(8,128)(2,1)S(1)}, bf16[2,128,256]{2,1,0:T(8,128)(2,1)S(1)}, u32[]{:S(2)}, u32[]{:S(2)}) collective-permute-start(bf16[2,128,256]{2,1,0:T(8,128)(2,1)S(1)} %get-tuple-element.26), channel_id=1, source_target_pairs={{0,1},{1,0},{2,3},{3,2},{4,5},{5,4},{6,7},{7,6},{8,9},{9,8},{10,11... | collective-permute-start | bytes 393224 | tf_op jit(solution)/shard_map/ppermute | solution.py:264
  5.7 0.8 %copy-start.3 = (f32[2,2,128,8]{2,3,1,0:T(8,128)S(1)}, f32[2,2,128,8]{2,3,1,0:T(8,128)}, u32[]{:S(2)}) copy-start(f32[2,2,128,8]{2,3,1,0:T(8,128)} %param.11) | copy-start | bytes 49156
  5.7 0.8 %copy-start.4 = (s32[2,2,128]{2,1,0:T(2,128)S(1)}, s32[2,2,128]{2,1,0:T(2,128)}, u32[]{:S(2)}) copy-start(s32[2,2,128]{2,1,0:T(2,128)} %refs_0_.5) | copy-start | bytes 6148
  5.7 0.8 %copy-start.5 = (f32[2,2,128]{2,1,0:T(2,128)S(1)}, f32[2,2,128]{2,1,0:T(2,128)}, u32[]{:S(2)}) copy-start(f32[2,2,128]{2,1,0:T(2,128)} %refs_2_.1) | copy-start | bytes 6148
  5.7 0.8 %copy-start.6 = (f32[2,2,128]{2,1,0:T(2,128)S(1)}, f32[2,2,128]{2,1,0:T(2,128)}, u32[]{:S(2)}) copy-start(f32[2,2,128]{2,1,0:T(2,128)} %refs_3_.1) | copy-start | bytes 6148
  5.7 2.5 %copy-start.1 = (bf16[2,128,1024]{2,1,0:T(8,128)(2,1)S(1)}, bf16[2,128,1024]{2,1,0:T(8,128)(2,1)}, u32[]{:S(2)}) copy-start(bf16[2,128,1024]{2,1,0:T(8,128)(2,1)} %refs_0_.4) | copy-start | bytes 1572868
  5.7 5.0 %collective-permute-start.3 = (bf16[2,32,256]{2,1,0:T(8,128)(2,1)S(1)}, bf16[2,32,256]{2,1,0:T(8,128)(2,1)S(1)}, u32[]{:S(2)}, u32[]{:S(2)}) collective-permute-start(bf16[2,32,256]{2,1,0:T(8,128)(2,1)S(1)} %get-tuple-element.27), channel_id=1, source_target_pairs={{0,1},{1,3},{2,5},{3,0},{4,7},{5,2},{6,9},{7,4},{8,11},{9,6},{10,1... | collective-permute-start | bytes 98312 | tf_op jit(solution)/shard_map/ppermute | solution.py:266
  6.5 1.7 %copy-start.2 = (bf16[2,64,160]{2,1,0:T(8,128)(2,1)S(1)}, bf16[2,64,160]{2,1,0:T(8,128)(2,1)}, u32[]{:S(2)}) copy-start(bf16[2,64,160]{2,1,0:T(8,128)(2,1)} %refs_6_.1) | copy-start | bytes 122884
  8.7 4.5 %collective-permute-start.4 = (bf16[2,64,256]{2,1,0:T(8,128)(2,1)S(1)}, bf16[2,64,256]{2,1,0:T(8,128)(2,1)S(1)}, u32[]{:S(2)}, u32[]{:S(2)}) collective-permute-start(bf16[2,64,256]{2,1,0:T(8,128)(2,1)S(1)} %get-tuple-element.29.refs_7_.refs_0_), channel_id=1, source_target_pairs={{0,8},{2,10},{4,12},{6,14},{8,0},{10,2},{12,4},{14,6},{16,24},{18,... | collective-permute-start | bytes 196616 | tf_op jit(solution)/shard_map/ppermute | solution.py:281
  11.7 6.0 %collective-permute-start.6 = (bf16[2,64,384]{2,1,0:T(8,128)(2,1)S(1)}, bf16[2,64,384]{2,1,0:T(8,128)(2,1)S(1)}, u32[]{:S(2)}, u32[]{:S(2)}) collective-permute-start(bf16[2,64,384]{2,1,0:T(8,128)(2,1)S(1)} %get-tuple-element.35.refs_0_), channel_id=1, source_target_pairs={{0,8},{2,10},{4,12},{6,14},{8,0},{10,2},{12,4},{14,6},{16,24},{18,... | collective-permute-start | bytes 294920 | tf_op jit(solution)/shard_map/ppermute | solution.py:281
  13.4 7.0 %collective-permute-start.9 = (bf16[2,64,256]{2,1,0:T(8,128)(2,1)S(1)}, bf16[2,64,256]{2,1,0:T(8,128)(2,1)S(1)}, u32[]{:S(2)}, u32[]{:S(2)}) collective-permute-start(bf16[2,64,256]{2,1,0:T(8,128)(2,1)S(1)} %get-tuple-element.37.refs_5_.high), channel_id=1, source_target_pairs={{0,16},{2,18},{4,20},{6,22},{8,24},{10,26},{12,28},{14,30},{16,0},... | collective-permute-start | bytes 196616 | tf_op jit(solution)/shard_map/ppermute | solution.py:281
  16.1 5.2 %collective-permute-start.5 = (bf16[2,64,384]{2,1,0:T(8,128)(2,1)S(1)}, bf16[2,64,384]{2,1,0:T(8,128)(2,1)S(1)}, u32[]{:S(2)}, u32[]{:S(2)}) collective-permute-start(bf16[2,64,384]{2,1,0:T(8,128)(2,1)S(1)} %get-tuple-element.34), channel_id=1, source_target_pairs={{0,8},{2,10},{4,12},{6,14},{8,0},{10,2},{12,4},{14,6},{16,24},{18,... | collective-permute-start | bytes 294920 | tf_op jit(solution)/shard_map/ppermute | solution.py:281
  17.9 9.1 %collective-permute-start.8 = (bf16[2,64,384]{2,1,0:T(8,128)(2,1)S(1)}, bf16[2,64,384]{2,1,0:T(8,128)(2,1)S(1)}, u32[]{:S(2)}, u32[]{:S(2)}) collective-permute-start(bf16[2,64,384]{2,1,0:T(8,128)(2,1)S(1)} %get-tuple-element.38.refs_5_.refs_4_.high), channel_id=1, source_target_pairs={{0,16},{2,18},{4,20},{6,22},{8,24},{10,26},{12,28},{14,30},{16,0},... | collective-permute-start | bytes 294920 | tf_op jit(solution)/shard_map/ppermute | solution.py:281
  21.6 7.6 %collective-permute-start.7 = (bf16[2,64,384]{2,1,0:T(8,128)(2,1)S(1)}, bf16[2,64,384]{2,1,0:T(8,128)(2,1)S(1)}, u32[]{:S(2)}, u32[]{:S(2)}) collective-permute-start(bf16[2,64,384]{2,1,0:T(8,128)(2,1)S(1)} %get-tuple-element.39.high), channel_id=1, source_target_pairs={{0,16},{2,18},{4,20},{6,22},{8,24},{10,26},{12,28},{14,30},{16,0},... | collective-permute-start | bytes 294920 | tf_op jit(solution)/shard_map/ppermute | solution.py:281

commit v4 on v3

--- a/solution.py
+++ b/solution.py
@@ -37,20 +37,19 @@
     )(*args)
 
 
-def completed(pairs, count):
+def completed(pairs, count, spare=None):
     needed = dict(pairs)
-    back = {t: s for s, t in needed.items() if t not in needed and s not in needed.values()}
-    moves = {**needed, **back}
+    if spare is None:
+        spare = {t: s for s, t in needed.items()}
+    taken = set(needed.values())
+    moves = {**needed, **{s: t for s, t in spare.items() if s not in needed and t not in taken}}
     sources = [d for d in range(count) if d not in moves]
     targets = [d for d in range(count) if d not in moves.values()]
     for d in [d for d in sources if d in targets]:
         ways = [(abs(s - d) + abs(t - d), s) for s, t in moves.items() if needed.get(s) != t]
-        if ways:
-            start = min(ways)[1]
-            moves[d] = moves[start]
-            moves[start] = d
-        else:
-            moves[d] = d
+        start = min(ways)[1] if ways else d
+        moves[d] = moves.get(start, d)
+        moves[start] = d
     moves.update(zip([d for d in sources if d not in moves], [d for d in targets if d not in moves.values()]))
     return sorted(moves.items())
 
@@ -260,7 +259,8 @@
         out_specs=[anywhere] * 3,
     )
     near = lax.ppermute(guard, "aperture", completed([(d, d - 1) for d in range(1, count, 2)], count))
-    far = lax.ppermute(guard, "aperture", completed([(d, d - 1) for d in range(2, count, 2)], count))
+    spare = {d: d - 1 if d % 4 == 3 else d + 3 for d in range(1, count, 2) if d % 4 == 3 or d + 3 < count}
+    far = lax.ppermute(guard, "aperture", completed([(d, d - 1) for d in range(2, count, 2)], count, spare))
     rim = lax.ppermute(rim, "tile", completed([(t, t - 1) for t in range(1, tiles)], tiles))
     steps = [(d * tiles + t, (d - 1) * tiles + t - 1) for d in range(1, count) for t in range(1, tiles)]
     corner = lax.ppermute(corner, ("aperture", "tile"), completed(steps, count * tiles))

time: 30.3 us -> 28.8 us (0.950)
  waiting for transfers between devices: 6.41 us -> 5.29 us
  starting transfers between devices: 15.6 us -> 15.2 us
    ppermute x6, waiting for transfers between devices: 5.06 us -> 4.23 us  [partner(): lax.ppermute(value, 'aperture', [(d, d ^ 1 << bit) for d in range(count)])]
    ppermute x1, waiting for transfers between devices: 0.8 us -> 0.01 us  [shards(): lax.ppermute(guard, 'aperture', completed([(d, d - 1) for d in range(2, c...]
    ppermute x1, waiting for transfers between devices: 0.51 us -> 1.02 us  [shards(): lax.ppermute(corner, ('aperture', 'tile'), completed(steps, count * tiles))]
    ppermute x6, starting transfers between devices: 10.5 us -> 10.1 us  [partner(): lax.ppermute(value, 'aperture', [(d, d ^ 1 << bit) for d in range(count)])]
  transfers between devices with their start and end apart: 10 -> 10, of which waited for: 5 -> 4; matrix products, arithmetic and copies ran while one was open for 0% -> 0% of each run, Pallas kernels for 19% -> 20%
where the time goes in v4:
time: 28.8 us; the launch traced here: 28.7 us
  starting transfers between devices  15.2 us (53%)
  Pallas kernels  6.88 us (24%)
  waiting for transfers between devices  5.29 us (18%)
  local copies, waits for them, and re-layouts  1.07 us (4%)
    ppermute x6, starting transfers between devices, partner(): lax.ppermute(value, 'aperture', [(d, d ^ 1 << bit) for d in range(count)])  10.1 us
    pallas_call x12, Pallas kernels, call(): pl.pallas_call(body, out_shape=outs, in_specs=in_specs or [whole] * len(a...  6.88 us
    ppermute x6, waiting for transfers between devices, partner(): lax.ppermute(value, 'aperture', [(d, d ^ 1 << bit) for d in range(count)])  4.23 us
    ppermute x1, starting transfers between devices, shards(): lax.ppermute(guard, 'aperture', completed([(d, d - 1) for d in range(2, c...  3.08 us
    ppermute x1, starting transfers between devices, shards(): lax.ppermute(rim, 'tile', completed([(t, t - 1) for t in range(1, tiles)]...  1.52 us
    unnamed x16, local copies, waits for them, and re-layouts  1.07 us
    ppermute x1, waiting for transfers between devices, shards(): lax.ppermute(corner, ('aperture', 'tile'), completed(steps, count * tiles))  1.02 us
  transfers between devices with their start and end apart: 10, of which 4 were waited for; matrix products, arithmetic and copies ran while one was open for 0% of the time, Pallas kernels for 20%

profile of v4, /device:TPU:0, one launch (start us, length us, event | category | flops | bytes accessed | tf_op | source)
XLA Modules:
  0.0 28.7 jit_solution(6720886374872766434)
XLA Ops:
  0.0 0.0 copy-start
  0.0 1.0 %copy-done = bf16[2,128,1024]{2,1,0:T(8,128)(2,1)S(1)} copy-done((bf16[2,128,1024]{2,1,0:T(8,128)(2,1)S(1)}, bf16[2,128,1024]{2,1,0:T(8,128)(2,1)}, u32[]{:S(2)}) %copy-start) | copy-done | bytes 524312
  1.0 0.1 shard_map.73
  1.2 3.1 %collective-permute-start.1 = (bf16[2,32,1024]{2,1,0:T(8,128)(2,1)S(1)}, bf16[2,32,1024]{2,1,0:T(8,128)(2,1)S(1)}, u32[]{:S(2)}, u32[]{:S(2)}) collective-permute-start(bf16[2,32,1024]{2,1,0:T(8,128)(2,1)S(1)} %get-tuple-element.25), channel_id=1, source_target_pairs={{0,8},{2,0},{4,2},{6,4},{8,6},{10,16},{12,10},{14,12},{16,14},{18,... | collective-permute-start | bytes 393224 | tf_op jit(solution)/shard_map/ppermute | solution.py:263
  4.3 0.0 collective-permute-start
  4.3 0.0 copy-start.7
  4.3 1.5 %collective-permute-start.2 = (bf16[2,128,256]{2,1,0:T(8,128)(2,1)S(1)}, bf16[2,128,256]{2,1,0:T(8,128)(2,1)S(1)}, u32[]{:S(2)}, u32[]{:S(2)}) collective-permute-start(bf16[2,128,256]{2,1,0:T(8,128)(2,1)S(1)} %get-tuple-element.26), channel_id=1, source_target_pairs={{0,1},{1,0},{2,3},{3,2},{4,5},{5,4},{6,7},{7,6},{8,9},{9,8},{10,11... | collective-permute-start | bytes 393224 | tf_op jit(solution)/shard_map/ppermute | solution.py:264
  5.8 0.0 copy-start.3
  5.8 0.0 copy-start.4
  5.8 0.0 copy-start.5
  5.8 0.0 copy-start.6
  5.8 0.0 copy-start.1
  5.8 0.6 %collective-permute-start.3 = (bf16[2,32,256]{2,1,0:T(8,128)(2,1)S(1)}, bf16[2,32,256]{2,1,0:T(8,128)(2,1)S(1)}, u32[]{:S(2)}, u32[]{:S(2)}) collective-permute-start(bf16[2,32,256]{2,1,0:T(8,128)(2,1)S(1)} %get-tuple-element.27), channel_id=1, source_target_pairs={{0,1},{1,3},{2,5},{3,0},{4,7},{5,2},{6,9},{7,4},{8,11},{9,6},{10,1... | collective-permute-start | bytes 98312 | tf_op jit(solution)/shard_map/ppermute | solution.py:266
  6.4 0.0 copy-done.7
  6.4 0.2 shard_map.74.refs_3_.refs_5_
  6.6 0.0 copy-start.2
  6.6 0.0 copy-done.3
  6.6 0.0 copy-done.4
  6.6 0.0 copy-done.5
  6.6 0.0 copy-done.6
  6.6 0.8 %shard_map.75 = (bf16[2,64,192]{2,1,0:T(8,128)(2,1)S(1)}, f32[2,2,64,1024]{3,2,1,0:T(8,128)S(1)}) custom-call(s32[2,2,128]{2,1,0:T(2,128)S(1)} %copy-done.4, f32[2,2,8,128]{3,2,1,0:T(8,128)S(1)} %bitcast.1, f32[2,2,128]{2,1,0:T(2,128)S(1)} %copy-done.5, f32[2,2,128]{2,1,0:T(2,128)S(1)} %copy-done.6), custom_call_target="tpu_custom_call" | custom-call | flops 20000000 | tf_op jit(solution)/shard_map/pallas_call | solution.py:28
  7.5 0.0 collective-permute-done.1.refs_2_
  7.5 0.0 collective-permute-done.refs_1_
  7.5 0.0 copy-done.1
  7.5 0.0 copy-done.2
  7.5 0.5 %shard_map.76 = (bf16[2,64,256]{2,1,0:T(8,128)(2,1)S(1)}, bf16[2,64,256]{2,1,0:T(8,128)(2,1)S(1)}) custom-call(bf16[2,128,1024]{2,1,0:T(8,128)(2,1)S(1)} %copy-done.1, bf16[2,32,1024]{2,1,0:T(8,128)(2,1)S(1)} %collective-permute-done.refs_1_, bf16[2,32,1024]{2,1,0:T(8,128)(2,1)S(1)} %collective-permute-done.1.refs_2_, ...), custom_call_target="tpu_custom_call" | custom-call | flops 167772160 | tf_op jit(solution)/shard_map/pallas_call | solution.py:28
  8.0 1.8 %collective-permute-start.4 = (bf16[2,64,256]{2,1,0:T(8,128)(2,1)S(1)}, bf16[2,64,256]{2,1,0:T(8,128)(2,1)S(1)}, u32[]{:S(2)}, u32[]{:S(2)}) collective-permute-start(bf16[2,64,256]{2,1,0:T(8,128)(2,1)S(1)} %get-tuple-element.29.refs_7_.refs_0_), channel_id=1, source_target_pairs={{0,8},{2,10},{4,12},{6,14},{8,0},{10,2},{12,4},{14,6},{16,24},{18,... | collective-permute-start | bytes 196616 | tf_op jit(solution)/shard_map/ppermute | solution.py:281
  9.8 1.0 %collective-permute-done.3.refs_4_ = bf16[2,32,256]{2,1,0:T(8,128)(2,1)S(1)} collective-permute-done((bf16[2,32,256]{2,1,0:T(8,128)(2,1)S(1)}, bf16[2,32,256]{2,1,0:T(8,128)(2,1)S(1)}, u32[]{:S(2)}, u32[]{:S(2)}) %collective-permute-start.3) | collective-permute-done | bytes 32800 | tf_op jit(solution)/shard_map/ppermute | solution.py:266
  10.8 0.0 collective-permute-done.2.refs_3_
  10.9 0.9 %shard_map.77 = (bf16[2,64,384]{2,1,0:T(8,128)(2,1)S(1)}, bf16[2,64,384]{2,1,0:T(8,128)(2,1)S(1)}, bf16[2,64,384]{2,1,0:T(8,128)(2,1)S(1)}, bf16[2,64,384]{2,1,0:T(8,128)(2,1)S(1)}) custom-call(bf16[2,128,1024]{2,1,0:T(8,128)(2,1)S(1)} %copy-done.1, bf16[2,32,1024]{2,1,0:T(8,128)(2,1)S(1)} %collective-permute-done.refs_1_, ...), custom_call_target="tpu_custom_call" | custom-call | flops 503316480 | tf_op jit(solution)/shard_map/pallas_call | solution.py:28
  11.8 1.2 %collective-permute-start.6 = (bf16[2,64,384]{2,1,0:T(8,128)(2,1)S(1)}, bf16[2,64,384]{2,1,0:T(8,128)(2,1)S(1)}, u32[]{:S(2)}, u32[]{:S(2)}) collective-permute-start(bf16[2,64,384]{2,1,0:T(8,128)(2,1)S(1)} %get-tuple-element.35.refs_0_), channel_id=1, source_target_pairs={{0,8},{2,10},{4,12},{6,14},{8,0},{10,2},{12,4},{14,6},{16,24},{18,... | collective-permute-start | bytes 294920 | tf_op jit(solution)/shard_map/ppermute | solution.py:281
  13.0 0.0 collective-permute-done.4.refs_2_
  13.0 0.2 shard_map.78
  13.3 2.3 %collective-permute-start.9 = (bf16[2,64,256]{2,1,0:T(8,128)(2,1)S(1)}, bf16[2,64,256]{2,1,0:T(8,128)(2,1)S(1)}, u32[]{:S(2)}, u32[]{:S(2)}) collective-permute-start(bf16[2,64,256]{2,1,0:T(8,128)(2,1)S(1)} %get-tuple-element.37.refs_5_.high), channel_id=1, source_target_pairs={{0,16},{2,18},{4,20},{6,22},{8,24},{10,26},{12,28},{14,30},{16,0},... | collective-permute-start | bytes 196616 | tf_op jit(solution)/shard_map/ppermute | solution.py:281
  15.6 0.9 %collective-permute-start.5 = (bf16[2,64,384]{2,1,0:T(8,128)(2,1)S(1)}, bf16[2,64,384]{2,1,0:T(8,128)(2,1)S(1)}, u32[]{:S(2)}, u32[]{:S(2)}) collective-permute-start(bf16[2,64,384]{2,1,0:T(8,128)(2,1)S(1)} %get-tuple-element.34), channel_id=1, source_target_pairs={{0,8},{2,10},{4,12},{6,14},{8,0},{10,2},{12,4},{14,6},{16,24},{18,... | collective-permute-start | bytes 294920 | tf_op jit(solution)/shard_map/ppermute | solution.py:281
  16.5 0.7 %collective-permute-done.6.refs_2_ = bf16[2,64,384]{2,1,0:T(8,128)(2,1)S(1)} collective-permute-done((bf16[2,64,384]{2,1,0:T(8,128)(2,1)S(1)}, bf16[2,64,384]{2,1,0:T(8,128)(2,1)S(1)}, u32[]{:S(2)}, u32[]{:S(2)}) %collective-permute-start.6) | collective-permute-done | bytes 98336 | tf_op jit(solution)/shard_map/ppermute | solution.py:281
  17.2 0.3 shard_map.79
  17.4 2.7 %collective-permute-start.8 = (bf16[2,64,384]{2,1,0:T(8,128)(2,1)S(1)}, bf16[2,64,384]{2,1,0:T(8,128)(2,1)S(1)}, u32[]{:S(2)}, u32[]{:S(2)}) collective-permute-start(bf16[2,64,384]{2,1,0:T(8,128)(2,1)S(1)} %get-tuple-element.38.refs_5_.refs_4_.high), channel_id=1, source_target_pairs={{0,16},{2,18},{4,20},{6,22},{8,24},{10,26},{12,28},{14,30},{16,0},... | collective-permute-start | bytes 294920 | tf_op jit(solution)/shard_map/ppermute | solution.py:281
  20.1 0.8 %shard_map.81 = (bf16[2,64,192]{2,1,0:T(8,128)(2,1)S(1)}, f32[2,2,64,1024]{3,2,1,0:T(8,128)S(1)}) custom-call(s32[2,2,128]{2,1,0:T(2,128)S(1)} %copy-done.4, f32[2,2,8,128]{3,2,1,0:T(8,128)S(1)} %bitcast.2, f32[2,2,128]{2,1,0:T(2,128)S(1)} %copy-done.5, f32[2,2,128]{2,1,0:T(2,128)S(1)} %copy-done.6, ...), custom_call_target="tpu_custom_call" | custom-call | flops 20000000 | tf_op jit(solution)/shard_map/pallas_call | solution.py:28
  21.0 0.0 collective-permute-done.9.other
  21.0 0.9 %shard_map.82.refs_0_ = f32[2,64,1024]{2,1,0:T(8,128)} custom-call(bf16[2,64,256]{2,1,0:T(8,128)(2,1)S(1)} %get-tuple-element.37.refs_5_.high, bf16[2,64,256]{2,1,0:T(8,128)(2,1)S(1)} %get-tuple-element.44.low, bf16[2,64,256]{2,1,0:T(8,128)(2,1)S(1)} %collective-permute-done.9.other, bf16[2,64,192]{2,1,0:T(8,128)(2,1)S(1)} %get-tuple-element.41.m, ...), custom_call_target="tpu_custom_call" | custom-call | flops 2000000000 | tf_op jit(solution)/shard_map/pallas_call | solution.py:28
  21.9 0.0 collective-permute-done.5.refs_2_
  21.9 0.3 shard_map.80
  22.1 1.1 %collective-permute-start.7 = (bf16[2,64,384]{2,1,0:T(8,128)(2,1)S(1)}, bf16[2,64,384]{2,1,0:T(8,128)(2,1)S(1)}, u32[]{:S(2)}, u32[]{:S(2)}) collective-permute-start(bf16[2,64,384]{2,1,0:T(8,128)(2,1)S(1)} %get-tuple-element.39.high), channel_id=1, source_target_pairs={{0,16},{2,18},{4,20},{6,22},{8,24},{10,26},{12,28},{14,30},{16,0},... | collective-permute-start | bytes 294920 | tf_op jit(solution)/shard_map/ppermute | solution.py:281
  23.2 2.5 %collective-permute-done.8.other = bf16[2,64,384]{2,1,0:T(8,128)(2,1)S(1)} collective-permute-done((bf16[2,64,384]{2,1,0:T(8,128)(2,1)S(1)}, bf16[2,64,384]{2,1,0:T(8,128)(2,1)S(1)}, u32[]{:S(2)}, u32[]{:S(2)}) %collective-permute-start.8) | collective-permute-done | bytes 98336 | tf_op jit(solution)/shard_map/ppermute | solution.py:281
  25.7 0.9 %shard_map.83.refs_0_ = f32[2,64,1024]{2,1,0:T(8,128)} custom-call(bf16[2,64,384]{2,1,0:T(8,128)(2,1)S(1)} %get-tuple-element.38.refs_5_.refs_4_.high, bf16[2,64,384]{2,1,0:T(8,128)(2,1)S(1)} %get-tuple-element.43.low, bf16[2,64,384]{2,1,0:T(8,128)(2,1)S(1)} %collective-permute-done.8.other, ...), custom_call_target="tpu_custom_call", output_to_operand_aliasing={{}: (5, {})} | custom-call | flops 2000000000 | tf_op jit(solution)/shard_map/pallas_call | solution.py:28
  26.7 1.0 %collective-permute-done.7.other = bf16[2,64,384]{2,1,0:T(8,128)(2,1)S(1)} collective-permute-done((bf16[2,64,384]{2,1,0:T(8,128)(2,1)S(1)}, bf16[2,64,384]{2,1,0:T(8,128)(2,1)S(1)}, u32[]{:S(2)}, u32[]{:S(2)}) %collective-permute-start.7) | collective-permute-done | bytes 98336 | tf_op jit(solution)/shard_map/ppermute | solution.py:281
  27.7 0.9 %shard_map.84 = f32[2,64,1024]{2,1,0:T(8,128)} custom-call(bf16[2,64,384]{2,1,0:T(8,128)(2,1)S(1)} %get-tuple-element.39.high, bf16[2,64,384]{2,1,0:T(8,128)(2,1)S(1)} %get-tuple-element.40.low, bf16[2,64,384]{2,1,0:T(8,128)(2,1)S(1)} %collective-permute-done.7.other, bf16[2,64,192]{2,1,0:T(8,128)(2,1)S(1)} %get-tuple-element.41.m, ...), custom_call_target="tpu_custom_call", output_to_operand_aliasing={{}: (5, {})} | custom-call | flops 2000000000 | tf_op jit(solution)/shard_map/pallas_call | solution.py:28
Async XLA Ops:
  0.0 1.0 %copy-start = (bf16[2,128,1024]{2,1,0:T(8,128)(2,1)S(1)}, bf16[2,128,1024]{2,1,0:T(8,128)(2,1)}, u32[]{:S(2)}) copy-start(bf16[2,128,1024]{2,1,0:T(8,128)(2,1)} %refs_0_.4) | copy-start | bytes 1572868
  1.2 6.3 %collective-permute-start.1 = (bf16[2,32,1024]{2,1,0:T(8,128)(2,1)S(1)}, bf16[2,32,1024]{2,1,0:T(8,128)(2,1)S(1)}, u32[]{:S(2)}, u32[]{:S(2)}) collective-permute-start(bf16[2,32,1024]{2,1,0:T(8,128)(2,1)S(1)} %get-tuple-element.25), channel_id=1, source_target_pairs={{0,8},{2,0},{4,2},{6,4},{8,6},{10,16},{12,10},{14,12},{16,14},{18,... | collective-permute-start | bytes 393224 | tf_op jit(solution)/shard_map/ppermute | solution.py:263
  4.3 3.2 %collective-permute-start = (bf16[2,32,1024]{2,1,0:T(8,128)(2,1)S(1)}, bf16[2,32,1024]{2,1,0:T(8,128)(2,1)S(1)}, u32[]{:S(2)}, u32[]{:S(2)}) collective-permute-start(bf16[2,32,1024]{2,1,0:T(8,128)(2,1)S(1)} %get-tuple-element.25), channel_id=1, source_target_pairs={{0,2},{2,0},{4,6},{6,4},{8,10},{10,8},{12,14},{14,12},{16,18},{18,... | collective-permute-start | bytes 393224 | tf_op jit(solution)/shard_map/ppermute | solution.py:261
  4.3 2.1 %copy-start.7 = (bf16[2,256]{1,0:T(2,128)(2,1)S(1)}, bf16[2,256]{1,0:T(2,128)(2,1)}, u32[]{:S(2)}) copy-start(bf16[2,256]{1,0:T(2,128)(2,1)} %taps_ref.1) | copy-start | bytes 3076
  4.3 6.6 %collective-permute-start.2 = (bf16[2,128,256]{2,1,0:T(8,128)(2,1)S(1)}, bf16[2,128,256]{2,1,0:T(8,128)(2,1)S(1)}, u32[]{:S(2)}, u32[]{:S(2)}) collective-permute-start(bf16[2,128,256]{2,1,0:T(8,128)(2,1)S(1)} %get-tuple-element.26), channel_id=1, source_target_pairs={{0,1},{1,0},{2,3},{3,2},{4,5},{5,4},{6,7},{7,6},{8,9},{9,8},{10,11... | collective-permute-start | bytes 393224 | tf_op jit(solution)/shard_map/ppermute | solution.py:264
  5.8 0.8 %copy-start.3 = (f32[2,2,128,8]{2,3,1,0:T(8,128)S(1)}, f32[2,2,128,8]{2,3,1,0:T(8,128)}, u32[]{:S(2)}) copy-start(f32[2,2,128,8]{2,3,1,0:T(8,128)} %param.11) | copy-start | bytes 49156
  5.8 0.8 %copy-start.4 = (s32[2,2,128]{2,1,0:T(2,128)S(1)}, s32[2,2,128]{2,1,0:T(2,128)}, u32[]{:S(2)}) copy-start(s32[2,2,128]{2,1,0:T(2,128)} %refs_0_.5) | copy-start | bytes 6148
  5.8 0.8 %copy-start.5 = (f32[2,2,128]{2,1,0:T(2,128)S(1)}, f32[2,2,128]{2,1,0:T(2,128)}, u32[]{:S(2)}) copy-start(f32[2,2,128]{2,1,0:T(2,128)} %refs_2_.1) | copy-start | bytes 6148
  5.8 0.8 %copy-start.6 = (f32[2,2,128]{2,1,0:T(2,128)S(1)}, f32[2,2,128]{2,1,0:T(2,128)}, u32[]{:S(2)}) copy-start(f32[2,2,128]{2,1,0:T(2,128)} %refs_3_.1) | copy-start | bytes 6148
  5.8 1.7 %copy-start.1 = (bf16[2,128,1024]{2,1,0:T(8,128)(2,1)S(1)}, bf16[2,128,1024]{2,1,0:T(8,128)(2,1)}, u32[]{:S(2)}) copy-start(bf16[2,128,1024]{2,1,0:T(8,128)(2,1)} %refs_0_.4) | copy-start | bytes 1572868
  5.8 5.0 %collective-permute-start.3 = (bf16[2,32,256]{2,1,0:T(8,128)(2,1)S(1)}, bf16[2,32,256]{2,1,0:T(8,128)(2,1)S(1)}, u32[]{:S(2)}, u32[]{:S(2)}) collective-permute-start(bf16[2,32,256]{2,1,0:T(8,128)(2,1)S(1)} %get-tuple-element.27), channel_id=1, source_target_pairs={{0,1},{1,3},{2,5},{3,0},{4,7},{5,2},{6,9},{7,4},{8,11},{9,6},{10,1... | collective-permute-start | bytes 98312 | tf_op jit(solution)/shard_map/ppermute | solution.py:266
  6.6 0.9 %copy-start.2 = (bf16[2,64,160]{2,1,0:T(8,128)(2,1)S(1)}, bf16[2,64,160]{2,1,0:T(8,128)(2,1)}, u32[]{:S(2)}) copy-start(bf16[2,64,160]{2,1,0:T(8,128)(2,1)} %refs_6_.1) | copy-start | bytes 122884
  8.0 5.0 %collective-permute-start.4 = (bf16[2,64,256]{2,1,0:T(8,128)(2,1)S(1)}, bf16[2,64,256]{2,1,0:T(8,128)(2,1)S(1)}, u32[]{:S(2)}, u32[]{:S(2)}) collective-permute-start(bf16[2,64,256]{2,1,0:T(8,128)(2,1)S(1)} %get-tuple-element.29.refs_7_.refs_0_), channel_id=1, source_target_pairs={{0,8},{2,10},{4,12},{6,14},{8,0},{10,2},{12,4},{14,6},{16,24},{18,... | collective-permute-start | bytes 196616 | tf_op jit(solution)/shard_map/ppermute | solution.py:281
  11.8 5.4 %collective-permute-start.6 = (bf16[2,64,384]{2,1,0:T(8,128)(2,1)S(1)}, bf16[2,64,384]{2,1,0:T(8,128)(2,1)S(1)}, u32[]{:S(2)}, u32[]{:S(2)}) collective-permute-start(bf16[2,64,384]{2,1,0:T(8,128)(2,1)S(1)} %get-tuple-element.35.refs_0_), channel_id=1, source_target_pairs={{0,8},{2,10},{4,12},{6,14},{8,0},{10,2},{12,4},{14,6},{16,24},{18,... | collective-permute-start | bytes 294920 | tf_op jit(solution)/shard_map/ppermute | solution.py:281
  13.3 7.7 %collective-permute-start.9 = (bf16[2,64,256]{2,1,0:T(8,128)(2,1)S(1)}, bf16[2,64,256]{2,1,0:T(8,128)(2,1)S(1)}, u32[]{:S(2)}, u32[]{:S(2)}) collective-permute-start(bf16[2,64,256]{2,1,0:T(8,128)(2,1)S(1)} %get-tuple-element.37.refs_5_.high), channel_id=1, source_target_pairs={{0,16},{2,18},{4,20},{6,22},{8,24},{10,26},{12,28},{14,30},{16,0},... | collective-permute-start | bytes 196616 | tf_op jit(solution)/shard_map/ppermute | solution.py:281
  15.6 6.3 %collective-permute-start.5 = (bf16[2,64,384]{2,1,0:T(8,128)(2,1)S(1)}, bf16[2,64,384]{2,1,0:T(8,128)(2,1)S(1)}, u32[]{:S(2)}, u32[]{:S(2)}) collective-permute-start(bf16[2,64,384]{2,1,0:T(8,128)(2,1)S(1)} %get-tuple-element.34), channel_id=1, source_target_pairs={{0,8},{2,10},{4,12},{6,14},{8,0},{10,2},{12,4},{14,6},{16,24},{18,... | collective-permute-start | bytes 294920 | tf_op jit(solution)/shard_map/ppermute | solution.py:281
  17.4 8.3 %collective-permute-start.8 = (bf16[2,64,384]{2,1,0:T(8,128)(2,1)S(1)}, bf16[2,64,384]{2,1,0:T(8,128)(2,1)S(1)}, u32[]{:S(2)}, u32[]{:S(2)}) collective-permute-start(bf16[2,64,384]{2,1,0:T(8,128)(2,1)S(1)} %get-tuple-element.38.refs_5_.refs_4_.high), channel_id=1, source_target_pairs={{0,16},{2,18},{4,20},{6,22},{8,24},{10,26},{12,28},{14,30},{16,0},... | collective-permute-start | bytes 294920 | tf_op jit(solution)/shard_map/ppermute | solution.py:281
  22.1 5.6 %collective-permute-start.7 = (bf16[2,64,384]{2,1,0:T(8,128)(2,1)S(1)}, bf16[2,64,384]{2,1,0:T(8,128)(2,1)S(1)}, u32[]{:S(2)}, u32[]{:S(2)}) collective-permute-start(bf16[2,64,384]{2,1,0:T(8,128)(2,1)S(1)} %get-tuple-element.39.high), channel_id=1, source_target_pairs={{0,16},{2,18},{4,20},{6,22},{8,24},{10,26},{12,28},{14,30},{16,0},... | collective-permute-start | bytes 294920 | tf_op jit(solution)/shard_map/ppermute | solution.py:281

commit v5 on v4

--- a/solution.py
+++ b/solution.py
@@ -9,8 +9,7 @@
 from jax.sharding import PartitionSpec as P
 
 LANES = 128
-M0 = 2_000_000_000
-F0 = 2_000_000_000
+WAIT = 2_000_000_000
 VMEM = pltpu.CompilerParams(vmem_limit_bytes=24 * 1024 * 1024)
 
 
@@ -96,7 +95,11 @@
     return c, d
 
 
-def table_kernel(s, level, offsets_ref, coef_ref, slope_ref, base_ref, m_ref, e_ref, turned):
+def table_kernel(s, level, offsets_ref, coef_ref, slope_ref, base_ref, *refs):
+    m_ref, e_ref = refs[-3 - len(refs) // 5 : -1 - len(refs) // 5]
+    turned = refs[-1]
+    if len(refs) == 5:
+        refs[3][...] = refs[0][...]
     beams, bins = e_ref.shape[2:]
     taps = coef_ref.shape[2]
     device = lax.axis_index("aperture")
@@ -132,33 +135,31 @@
             e_ref[side, 1, :, at] = d * fine_cos + c * fine_sin
 
 
-def focus_kernel(first, has_rim, sizes, *refs):
-    if has_rim:
-        raw, near, far, rim, corner, w, steering = refs[:7]
-    else:
-        raw, near, far, w, steering = refs[:5]
+def focus_kernel(first, raw, near, far, w, steering, *refs):
     x = refs[-1]
-    outs = refs[-1 - 2 * len(sizes) : -1]
     pulses, guards = raw.shape[1], near.shape[1]
     width = w.shape[1] // 2
     rows = pulses + guards
-    blocks = sum(sizes) // width
+    blocks = x.shape[0] // rows - 1
+    has_rim = first + blocks * width == raw.shape[2]
+    high_ref, low_ref = refs[-3:-1]
     device = lax.axis_index("aperture")
     even = device % 2 == 0
     followed = device < lax.axis_size("aperture") - 1
     inner = lax.axis_index("tile") < lax.axis_size("tile") - 1
     nought = jnp.zeros((), jnp.bfloat16)
+
     for b in range(blocks + 1):
         at = first + b * width
         for part in range(2):
-            lanes = slice(part * width, (part + 1) * width)
-            if at < raw.shape[2]:
+            if at == raw.shape[2]:
+                own = jnp.where(inner, refs[0][part], nought)
+                other = jnp.where(inner & followed, refs[1][part], nought)
+            else:
                 own = raw[part, :, at : at + width]
                 other = jnp.where(even, near[part, :, at : at + width], far[part, :, at : at + width])
                 other = jnp.where(followed, other, nought)
-            else:
-                own = jnp.where(inner, rim[part], nought)
-                other = jnp.where(inner & followed, corner[part], nought)
+            lanes = slice(part * width, (part + 1) * width)
             x[b * rows : b * rows + pulses, lanes] = own
             x[b * rows + pulses : (b + 1) * rows, lanes] = other
     turned = jnp.concatenate([steering[0], steering[1]], 0)
@@ -167,62 +168,74 @@
     out = jnp.dot(x[: blocks * rows], w[0], preferred_element_type=jnp.float32)
     out += jnp.dot(x[rows:], w[1], preferred_element_type=jnp.float32)
     out = out.astype(jnp.bfloat16)
-    places = [(n, at) for n, size in enumerate(sizes) for at in range(0, size, LANES)]
     for b in range(blocks):
         re = out[b * rows : (b + 1) * rows, :width]
         im = out[b * rows : (b + 1) * rows, width:]
         sub = jnp.dot(turned, re, preferred_element_type=jnp.float32)
         sub += jnp.dot(crossed, im, preferred_element_type=jnp.float32)
-        for k in range(width // LANES):
-            n, at = places[b * (width // LANES) + k]
-            high, low = split(sub[:, k * LANES : (k + 1) * LANES])
-            for ref, value in ((outs[2 * n], high), (outs[2 * n + 1], low)):
-                ref[0, :, at : at + LANES] = value[:beams]
-                ref[1, :, at : at + LANES] = value[beams:]
-
-
-def merged(first, bins, high, low, other, m, e):
-    beams = high.shape[1]
+        high, low = split(sub)
+        at = slice(b * width, (b + 1) * width)
+        high_ref[0, :, at], high_ref[1, :, at] = high[:beams], high[beams:]
+        low_ref[0, :, at], low_ref[1, :, at] = low[:beams], low[beams:]
+
+
+def split_parts(values):
+    high, low = zip(*[split(value) for value in values])
+    return high, low
+
+
+def turned_sum(first, own, other, m, e):
+    bins = own[0][0].shape[1]
+    beams = m.shape[1]
     at = slice(first, first + bins)
-    own_m = m[0]
-    other_m = m[1][:, : 2 * beams]
-    own, got = [], []
-    for part in range(2):
-        x = high[part]
-        x = jnp.concatenate([x, x, low[part]], 0)
-        own.append(jnp.dot(own_m, x, preferred_element_type=jnp.float32))
-        y = other[part]
-        y = jnp.concatenate([y, y], 0)
-        got.append(jnp.dot(other_m, y, preferred_element_type=jnp.float32))
-    c0, s0 = e[0, 0, :, at], e[0, 1, :, at]
-    c1, s1 = e[1, 0, :, at], e[1, 1, :, at]
-    re = c0 * own[0] - s0 * own[1] + c1 * got[0] - s1 * got[1]
-    im = s0 * own[0] + c0 * own[1] + s1 * got[0] + c1 * got[1]
+    re, im = None, None
+    for side, given in enumerate((own, other)):
+        terms = []
+        for part in range(2):
+            high = given[0][part]
+            stacked = [high, high] + ([given[1][part]] if len(given) > 1 else [])
+            weights = m[side][:, : len(stacked) * beams]
+            stacked = jnp.concatenate(stacked, 0)
+            terms.append(jnp.dot(weights, stacked, preferred_element_type=jnp.float32))
+        c, d = e[side, 0, :, at], e[side, 1, :, at]
+        more_re, more_im = c * terms[0] - d * terms[1], d * terms[0] + c * terms[1]
+        re = more_re if re is None else re + more_re
+        im = more_im if im is None else im + more_im
     return re, im
+
+
+def store_split(values, high_ref, low_ref):
+    for part, value in enumerate(values):
+        high_ref[part], low_ref[part] = split(value)
 
 
 def first_merge_kernel(first, high, low, other, m, e, *refs):
     if len(refs) == 4:
         refs[3][...] = refs[0][...]
         refs = refs[1:3]
-    high_ref, low_ref = refs
-    bins = high_ref.shape[2]
-    for part, value in enumerate(merged(first, bins, high, low, other, m, e)):
-        top, rest = split(value)
-        high_ref[part] = top
-        low_ref[part] = rest
-
-
-def last_merge_kernel(first, high, low, other, m, e, *refs):
-    image, held, sem = refs[-3:]
+    store_split(turned_sum(first, (high, low), (other,), m, e), *refs)
+
+
+def write_image(values, first, image, held, sem):
     copies = []
-    for part, value in enumerate(merged(first, held.shape[2], high, low, other, m, e)):
+    for part, value in enumerate(values):
         held[part] = value
         place = image.at[part, :, first : first + held.shape[2]]
         copies.append(pltpu.make_async_copy(held.at[part], place, sem.at[part]))
         copies[-1].start()
     for copy in copies:
         copy.wait()
+
+
+def last_merge_kernel(first, high, low, other, m, e, *refs):
+    image, held, sem = refs[-3:]
+    write_image(turned_sum(first, (high, low), (other,), m, e), first, image, held, sem)
+
+
+def both_merges_kernel(first, high, low, near, over, beyond, m0, e0, m1, e1, _, image, held, sem):
+    own = split_parts(turned_sum(first, (high, low), (near,), m0, e0))
+    other = split_parts(turned_sum(first, (over,), (beyond,), m0, e0))
+    write_image(turned_sum(first, own, other, m1, e1), first, image, held, sem)
 
 
 def cut_kernel(raw, guard, rim, corner, sem):
@@ -265,11 +278,12 @@
     steps = [(d * tiles + t, (d - 1) * tiles + t - 1) for d in range(1, count) for t in range(1, tiles)]
     corner = lax.ppermute(corner, ("aperture", "tile"), completed(steps, count * tiles))
     w = call(toeplitz_kernel, sds((2, 2 * width, 2 * width), bf16), [taps])
-    def tables(s, after=()):
+    def tables(s, after=(), through=()):
+        passed = [sds(x.shape, x.dtype) for x in through]
         return call(
             functools.partial(table_kernel, s, level),
-            [sds((2, beams, 3 * beams), bf16), sds((2, 2, beams, bins), f32)],
-            [offsets, jnp.swapaxes(coef, 2, 3), slope, base],
+            [sds((2, beams, 3 * beams), bf16), sds((2, 2, beams, bins), f32), *passed],
+            [offsets, jnp.swapaxes(coef, 2, 3), slope, base, *through],
             scratch=[pltpu.VMEM((2 * beams, 2 * beams), f32)],
             flops=20_000_000,
             after=after,
@@ -280,59 +294,69 @@
     def partner(value, bit):
         return lax.ppermute(value, "aperture", [(d, d ^ (1 << bit)) for d in range(count)])
 
-    blocks = bins // width
-    plan = [[width], [(bins - width) // 2 // LANES * LANES, bins - width - (bins - width) // 2 // LANES * LANES]] if blocks > 2 else [[bins]]
-    subs = []
-    chunks = []
-    first = 0
-    for sizes in plan:
-        size = sum(sizes)
-        has_rim = first + size == bins
+    def focus(first, size, after, rims=(), flops=0):
         rows = pulses + guards
-        args = [raw, near, far] + ([rim, corner] if has_rim else []) + [w, steering]
-        found = call(
-            functools.partial(focus_kernel, first, has_rim, sizes),
-            [sds((2, beams, part), bf16) for part in sizes for _ in range(2)],
-            args,
+        return call(
+            functools.partial(focus_kernel, first),
+            [sds((2, beams, size), bf16)] * 2,
+            [raw, near, far, w, steering, *rims],
             scratch=[pltpu.VMEM(((size // width + 1) * rows, 2 * width), bf16)],
-            flops=rows * size * 4 * width * 4,
-            after=[subs[-1][0] if subs else first_tables[0]],
-        )
-        for n, part in enumerate(sizes):
-            subs.append(found[2 * n : 2 * n + 2])
-            chunks.append((first, part))
-            first += part
+            flops=flops,
+            after=[after],
+        )
+
+    def first_merge(first, sub, other, after, through=(), flops=0):
+        shape = sds(other.shape, bf16)
+        return call(
+            functools.partial(first_merge_kernel, first),
+            [shape, shape] + [sds(x.shape, bf16) for x in through],
+            [*sub, other, *first_tables, *through],
+            flops=flops,
+            after=[after],
+        )
+
+    def write(body, size, args, image, flops=0):
+        given = [] if image is None else [image]
+        whole_image = sds((2, beams, bins), f32)
+        args = [*args]
+        return call(
+            body,
+            whole_image,
+            args + given,
+            scratch=[pltpu.VMEM((2, beams, size), f32), pltpu.SemaphoreType.DMA((2,))],
+            aliases={len(args): 0} if given else {},
+            in_specs=[whole] * len(args) + [anywhere] * len(given),
+            out_specs=anywhere,
+            flops=flops,
+        )
+
+    assert bins > 2 * width
+    middle, last = width, bins - width
+    subs = [focus(0, width, first_tables[0])]
+    subs.append(focus(middle, last - middle, subs[0][0]))
+    subs.append(focus(last, width, subs[1][0], [rim, corner], WAIT))
     others = [partner(high, level) for high, _ in subs[:2]]
-    seconds = []
-    for n, (first, size) in enumerate(chunks):
-        through = [subs[2][0]] if n == 0 and len(chunks) > 2 else []
-        outs = [sds((2, beams, size), bf16)] * 2 + [sds(x.shape, bf16) for x in through]
-        found = call(
-            functools.partial(first_merge_kernel, first),
-            outs,
-            [*subs[n], others[n], *first_tables, *through],
-            flops=beams * size * beams * 40 if seconds else M0,
-            after=[seconds[-1][0] if seconds else subs[-1][0]],
-        )
-        seconds.append(found[:2])
-        if through:
-            others.append(partner(found[2], level))
-    others = [partner(high, level + 1) for high, _ in seconds]
-    last_tables = tables(1, [seconds[min(1, len(seconds) - 1)][0]])
-    image = None
-    for (first, size), (high, low), other in zip(chunks, seconds, others):
-        args = [high, low, other, *last_tables] + ([] if image is None else [image])
-        image = call(
-            functools.partial(last_merge_kernel, first),
-            sds((2, beams, bins), f32),
-            args,
-            scratch=[pltpu.VMEM((2, beams, size), f32), pltpu.SemaphoreType.DMA((2,))],
-            aliases={} if image is None else {5: 0},
-            in_specs=[whole] * 5 + ([] if image is None else [anywhere]),
-            out_specs=anywhere,
-            flops=F0,
-        )
-    return image
+    over = partner(subs[2][0], level + 1)
+    *second, late = first_merge(0, subs[0], others[0], subs[2][0], [subs[2][0]], WAIT)
+    third = partner(second[0], level + 1)
+    near_last = partner(late, level)
+    middle_second = first_merge(middle, subs[1], others[1], second[0])
+    middle_third = partner(middle_second[0], level + 1)
+    *last_tables, over_late = tables(1, [middle_second[0]], [over])
+    beyond = partner(over_late, level)
+    image = write(functools.partial(last_merge_kernel, 0), width, [*second, third, *last_tables], None, WAIT)
+    image = write(
+        functools.partial(both_merges_kernel, last),
+        width,
+        [*subs[2], near_last, over, beyond, *first_tables, *last_tables],
+        image,
+    )
+    return write(
+        functools.partial(last_merge_kernel, middle),
+        last - middle,
+        [*middle_second, middle_third, *last_tables],
+        image,
+    )
 
 
 def solution(mesh):

time: 28.8 us -> 28.3 us (0.983)
  waiting for transfers between devices: 5.29 us -> 3.88 us
  starting transfers between devices: 15.2 us -> 15.9 us
    ppermute x1, waiting for transfers between devices: 1.02 us -> 0.01 us  [shards(): lax.ppermute(corner, ('aperture', 'tile'), completed(steps, count * tiles))]
    ppermute x6 -> x7, starting transfers between devices: 10.1 us -> 10.7 us  [partner(): lax.ppermute(value, 'aperture', [(d, d ^ 1 << bit) for d in range(count)])]
    ppermute x1, starting transfers between devices: 0.01 us -> 0.52 us  [shards(): lax.ppermute(guard, 'aperture', completed([(d, d - 1) for d in range(1, c...]
    ppermute x1, starting transfers between devices: 3.08 us -> 2.64 us  [shards(): lax.ppermute(guard, 'aperture', completed([(d, d - 1) for d in range(2, c...]
    ppermute x6 -> x7, waiting for transfers between devices: 4.23 us -> 3.87 us  [partner(): lax.ppermute(value, 'aperture', [(d, d ^ 1 << bit) for d in range(count)])]
  transfers between devices with their start and end apart: 10 -> 11, of which waited for: 4 -> 4; matrix products, arithmetic and copies ran while one was open for 0% -> 0% of each run, Pallas kernels for 20% -> 21%
where the time goes in v5:
time: 28.3 us; the launch traced here: 28.2 us
  starting transfers between devices  15.9 us (56%)
  Pallas kernels  7.08 us (25%)
  waiting for transfers between devices  3.88 us (14%)
  local copies, waits for them, and re-layouts  1.07 us (4%)
    ppermute x7, starting transfers between devices, partner(): lax.ppermute(value, 'aperture', [(d, d ^ 1 << bit) for d in range(count)])  10.7 us
    pallas_call x12, Pallas kernels, call(): pl.pallas_call(body, out_shape=outs, in_specs=in_specs or [whole] * len(a...  7.08 us
    ppermute x7, waiting for transfers between devices, partner(): lax.ppermute(value, 'aperture', [(d, d ^ 1 << bit) for d in range(count)])  3.87 us
    ppermute x1, starting transfers between devices, shards(): lax.ppermute(guard, 'aperture', completed([(d, d - 1) for d in range(2, c...  2.64 us
    ppermute x1, starting transfers between devices, shards(): lax.ppermute(rim, 'tile', completed([(t, t - 1) for t in range(1, tiles)]...  1.52 us
    unnamed x16, local copies, waits for them, and re-layouts  1.07 us
  transfers between devices with their start and end apart: 11, of which 4 were waited for; matrix products, arithmetic and copies ran while one was open for 0% of the time, Pallas kernels for 21%

profile of v5, /device:TPU:0, one launch (start us, length us, event | category | flops | bytes accessed | tf_op | source)
XLA Modules:
  0.0 28.2 jit_solution(5398990598425371532)
XLA Ops:
  0.0 0.0 copy-start
  0.0 1.0 %copy-done = bf16[2,128,1024]{2,1,0:T(8,128)(2,1)S(1)} copy-done((bf16[2,128,1024]{2,1,0:T(8,128)(2,1)S(1)}, bf16[2,128,1024]{2,1,0:T(8,128)(2,1)}, u32[]{:S(2)}) %copy-start) | copy-done | bytes 524312
  1.0 0.1 shard_map.73
  1.2 0.5 %collective-permute-start = (bf16[2,32,1024]{2,1,0:T(8,128)(2,1)S(1)}, bf16[2,32,1024]{2,1,0:T(8,128)(2,1)S(1)}, u32[]{:S(2)}, u32[]{:S(2)}) collective-permute-start(bf16[2,32,1024]{2,1,0:T(8,128)(2,1)S(1)} %get-tuple-element.24), channel_id=1, source_target_pairs={{0,2},{2,0},{4,6},{6,4},{8,10},{10,8},{12,14},{14,12},{16,18},{18,... | collective-permute-start | bytes 393224 | tf_op jit(solution)/shard_map/ppermute | solution.py:274
  1.7 2.6 %collective-permute-start.1 = (bf16[2,32,1024]{2,1,0:T(8,128)(2,1)S(1)}, bf16[2,32,1024]{2,1,0:T(8,128)(2,1)S(1)}, u32[]{:S(2)}, u32[]{:S(2)}) collective-permute-start(bf16[2,32,1024]{2,1,0:T(8,128)(2,1)S(1)} %get-tuple-element.24), channel_id=1, source_target_pairs={{0,8},{2,0},{4,2},{6,4},{8,6},{10,16},{12,10},{14,12},{16,14},{18,... | collective-permute-start | bytes 393224 | tf_op jit(solution)/shard_map/ppermute | solution.py:276
  4.3 0.0 copy-start.7
  4.3 1.5 %collective-permute-start.4 = (bf16[2,128,256]{2,1,0:T(8,128)(2,1)S(1)}, bf16[2,128,256]{2,1,0:T(8,128)(2,1)S(1)}, u32[]{:S(2)}, u32[]{:S(2)}) collective-permute-start(bf16[2,128,256]{2,1,0:T(8,128)(2,1)S(1)} %get-tuple-element.31), channel_id=1, source_target_pairs={{0,1},{1,0},{2,3},{3,2},{4,5},{5,4},{6,7},{7,6},{8,9},{9,8},{10,11... | collective-permute-start | bytes 393224 | tf_op jit(solution)/shard_map/ppermute | solution.py:277
  5.9 0.0 copy-start.3
  5.9 0.0 copy-start.4
  5.9 0.0 copy-start.1
  5.9 0.6 %collective-permute-start.5 = (bf16[2,32,256]{2,1,0:T(8,128)(2,1)S(1)}, bf16[2,32,256]{2,1,0:T(8,128)(2,1)S(1)}, u32[]{:S(2)}, u32[]{:S(2)}) collective-permute-start(bf16[2,32,256]{2,1,0:T(8,128)(2,1)S(1)} %get-tuple-element.32), channel_id=1, source_target_pairs={{0,1},{1,3},{2,5},{3,0},{4,7},{5,2},{6,9},{7,4},{8,11},{9,6},{10,1... | collective-permute-start | bytes 98312 | tf_op jit(solution)/shard_map/ppermute | solution.py:279
  6.4 0.0 copy-done.7
  6.4 0.2 shard_map.74.refs_3_
  6.7 0.0 copy-start.2
  6.7 0.0 copy-done.3
  6.7 0.0 copy-done.4
  6.7 0.0 copy-done.5
  6.7 0.0 copy-done.6
  6.7 0.8 %shard_map.75 = (bf16[2,64,192]{2,1,0:T(8,128)(2,1)S(1)}, f32[2,2,64,1024]{3,2,1,0:T(8,128)S(1)}) custom-call(s32[2,2,128]{2,1,0:T(2,128)S(1)} %copy-done.4, f32[2,2,8,128]{3,2,1,0:T(8,128)S(1)} %bitcast.1, f32[2,2,128]{2,1,0:T(2,128)S(1)} %copy-done.5, f32[2,2,128]{2,1,0:T(2,128)S(1)} %copy-done.6), custom_call_target="tpu_custom_call" | custom-call | flops 20000000 | tf_op jit(solution)/shard_map/pallas_call | solution.py:27
  7.5 0.0 collective-permute-done.refs_1_
  7.5 0.0 collective-permute-done.1.refs_2_
  7.6 0.0 copy-done.1
  7.6 0.0 copy-done.2
  7.6 0.5 %shard_map.76 = (bf16[2,64,256]{2,1,0:T(8,128)(2,1)S(1)}, bf16[2,64,256]{2,1,0:T(8,128)(2,1)S(1)}) custom-call(bf16[2,128,1024]{2,1,0:T(8,128)(2,1)S(1)} %copy-done.1, bf16[2,32,1024]{2,1,0:T(8,128)(2,1)S(1)} %collective-permute-done.refs_1_, bf16[2,32,1024]{2,1,0:T(8,128)(2,1)S(1)} %collective-permute-done.1.refs_2_, ...), custom_call_target="tpu_custom_call" | custom-call | tf_op jit(solution)/shard_map/pallas_call | solution.py:27
  8.1 1.8 %collective-permute-start.3 = (bf16[2,64,256]{2,1,0:T(8,128)(2,1)S(1)}, bf16[2,64,256]{2,1,0:T(8,128)(2,1)S(1)}, u32[]{:S(2)}, u32[]{:S(2)}) collective-permute-start(bf16[2,64,256]{2,1,0:T(8,128)(2,1)S(1)} %get-tuple-element.26.refs_5_.refs_0_), channel_id=1, source_target_pairs={{0,8},{2,10},{4,12},{6,14},{8,0},{10,2},{12,4},{14,6},{16,24},{18,... | collective-permute-start | bytes 196616 | tf_op jit(solution)/shard_map/ppermute | solution.py:295
  9.9 0.7 %shard_map.77 = (bf16[2,64,512]{2,1,0:T(8,128)(2,1)S(1)}, bf16[2,64,512]{2,1,0:T(8,128)(2,1)S(1)}) custom-call(bf16[2,128,1024]{2,1,0:T(8,128)(2,1)S(1)} %copy-done.1, bf16[2,32,1024]{2,1,0:T(8,128)(2,1)S(1)} %collective-permute-done.refs_1_, bf16[2,32,1024]{2,1,0:T(8,128)(2,1)S(1)} %collective-permute-done.1.refs_2_, ...), custom_call_target="tpu_custom_call" | custom-call | tf_op jit(solution)/shard_map/pallas_call | solution.py:27
  10.6 0.4 %collective-permute-start.2 = (bf16[2,64,512]{2,1,0:T(8,128)(2,1)S(1)}, bf16[2,64,512]{2,1,0:T(8,128)(2,1)S(1)}, u32[]{:S(2)}, u32[]{:S(2)}) collective-permute-start(bf16[2,64,512]{2,1,0:T(8,128)(2,1)S(1)} %get-tuple-element.27.refs_7_.refs_0_), channel_id=1, source_target_pairs={{0,8},{2,10},{4,12},{6,14},{8,0},{10,2},{12,4},{14,6},{16,24},{18,... | collective-permute-start | bytes 393224 | tf_op jit(solution)/shard_map/ppermute | solution.py:295
  10.9 0.0 collective-permute-done.5.refs_6_
  10.9 0.0 collective-permute-done.4.refs_5_
  11.0 0.5 %shard_map.78 = (bf16[2,64,256]{2,1,0:T(8,128)(2,1)S(1)}, bf16[2,64,256]{2,1,0:T(8,128)(2,1)S(1)}) custom-call(bf16[2,128,1024]{2,1,0:T(8,128)(2,1)S(1)} %copy-done.1, bf16[2,32,1024]{2,1,0:T(8,128)(2,1)S(1)} %collective-permute-done.refs_1_, bf16[2,32,1024]{2,1,0:T(8,128)(2,1)S(1)} %collective-permute-done.1.refs_2_, ...), custom_call_target="tpu_custom_call" | custom-call | flops 2000000000 | tf_op jit(solution)/shard_map/pallas_call | solution.py:27
  11.5 2.4 %collective-permute-start.7 = (bf16[2,64,256]{2,1,0:T(8,128)(2,1)S(1)}, bf16[2,64,256]{2,1,0:T(8,128)(2,1)S(1)}, u32[]{:S(2)}, u32[]{:S(2)}) collective-permute-start(bf16[2,64,256]{2,1,0:T(8,128)(2,1)S(1)} %get-tuple-element.33.refs_5_.refs_6_.high), channel_id=1, source_target_pairs={{0,16},{2,18},{4,20},{6,22},{8,24},{10,26},{12,28},{14,30},{16,0},... | collective-permute-start | bytes 196616 | tf_op jit(solution)/shard_map/ppermute | solution.py:295
  13.8 0.0 collective-permute-done.3.refs_2_
  13.8 0.2 shard_map.79
  14.0 1.3 %collective-permute-start.10 = (bf16[2,64,256]{2,1,0:T(8,128)(2,1)S(1)}, bf16[2,64,256]{2,1,0:T(8,128)(2,1)S(1)}, u32[]{:S(2)}, u32[]{:S(2)}) collective-permute-start(bf16[2,64,256]{2,1,0:T(8,128)(2,1)S(1)} %get-tuple-element.34.refs_5_.high), channel_id=1, source_target_pairs={{0,16},{2,18},{4,20},{6,22},{8,24},{10,26},{12,28},{14,30},{16,0},... | collective-permute-start | bytes 196616 | tf_op jit(solution)/shard_map/ppermute | solution.py:295
  15.3 1.9 %collective-permute-start.8 = (bf16[2,64,256]{2,1,0:T(8,128)(2,1)S(1)}, bf16[2,64,256]{2,1,0:T(8,128)(2,1)S(1)}, u32[]{:S(2)}, u32[]{:S(2)}) collective-permute-start(bf16[2,64,256]{2,1,0:T(8,128)(2,1)S(1)} %get-tuple-element.40), channel_id=1, source_target_pairs={{0,8},{2,10},{4,12},{6,14},{8,0},{10,2},{12,4},{14,6},{16,24},{18,... | collective-permute-start | bytes 196616 | tf_op jit(solution)/shard_map/ppermute | solution.py:295
  17.2 0.2 collective-permute-done.2.refs_2_
  17.3 0.3 %shard_map.80 = (bf16[2,64,512]{2,1,0:T(8,128)(2,1)S(1)}, bf16[2,64,512]{2,1,0:T(8,128)(2,1)S(1)}) custom-call(bf16[2,64,512]{2,1,0:T(8,128)(2,1)S(1)} %get-tuple-element.27.refs_7_.refs_0_, bf16[2,64,512]{2,1,0:T(8,128)(2,1)S(1)} %get-tuple-element.28.refs_1_, bf16[2,64,512]{2,1,0:T(8,128)(2,1)S(1)} %collective-permute-done.2.refs_2_, ...), custom_call_target="tpu_custom_call" | custom-call | tf_op jit(solution)/shard_map/pallas_call | solution.py:27
  17.6 1.8 %collective-permute-start.6 = (bf16[2,64,512]{2,1,0:T(8,128)(2,1)S(1)}, bf16[2,64,512]{2,1,0:T(8,128)(2,1)S(1)}, u32[]{:S(2)}, u32[]{:S(2)}) collective-permute-start(bf16[2,64,512]{2,1,0:T(8,128)(2,1)S(1)} %get-tuple-element.35.refs_5_.high), channel_id=1, source_target_pairs={{0,16},{2,18},{4,20},{6,22},{8,24},{10,26},{12,28},{14,30},{16,0},... | collective-permute-start | bytes 393224 | tf_op jit(solution)/shard_map/ppermute | solution.py:295
  19.5 0.0 collective-permute-done.7.refs_4_.over
  19.5 0.8 %shard_map.81 = (bf16[2,64,192]{2,1,0:T(8,128)(2,1)S(1)}, f32[2,2,64,1024]{3,2,1,0:T(8,128)S(1)}, bf16[2,64,256]{2,1,0:T(8,128)(2,1)S(1)}) custom-call(s32[2,2,128]{2,1,0:T(2,128)S(1)} %copy-done.4, f32[2,2,8,128]{3,2,1,0:T(8,128)S(1)} %bitcast.2, f32[2,2,128]{2,1,0:T(2,128)S(1)} %copy-done.5, f32[2,2,128]{2,1,0:T(2,128)S(1)} %copy-done.6, ...), custom_call_target="tpu_custom_call" | custom-call | flops 20000000 | tf_op jit(solution)/shard_map/pallas_call | solution.py:27
  20.3 1.2 %collective-permute-start.9 = (bf16[2,64,256]{2,1,0:T(8,128)(2,1)S(1)}, bf16[2,64,256]{2,1,0:T(8,128)(2,1)S(1)}, u32[]{:S(2)}, u32[]{:S(2)}) collective-permute-start(bf16[2,64,256]{2,1,0:T(8,128)(2,1)S(1)} %get-tuple-element.41), channel_id=1, source_target_pairs={{0,8},{2,10},{4,12},{6,14},{8,0},{10,2},{12,4},{14,6},{16,24},{18,... | collective-permute-start | bytes 196616 | tf_op jit(solution)/shard_map/ppermute | solution.py:295
  21.5 1.3 %collective-permute-done.10.other = bf16[2,64,256]{2,1,0:T(8,128)(2,1)S(1)} collective-permute-done((bf16[2,64,256]{2,1,0:T(8,128)(2,1)S(1)}, bf16[2,64,256]{2,1,0:T(8,128)(2,1)S(1)}, u32[]{:S(2)}, u32[]{:S(2)}) %collective-permute-start.10) | collective-permute-done | bytes 65568 | tf_op jit(solution)/shard_map/ppermute | solution.py:295
  22.8 0.9 %shard_map.82._ = f32[2,64,1024]{2,1,0:T(8,128)} custom-call(bf16[2,64,256]{2,1,0:T(8,128)(2,1)S(1)} %get-tuple-element.34.refs_5_.high, bf16[2,64,256]{2,1,0:T(8,128)(2,1)S(1)} %get-tuple-element.42.low, bf16[2,64,256]{2,1,0:T(8,128)(2,1)S(1)} %collective-permute-done.10.other, bf16[2,64,192]{2,1,0:T(8,128)(2,1)S(1)} %get-tuple-element.37.m.m1, ...), custom_call_target="tpu_custom_call" | custom-call | flops 2000000000 | tf_op jit(solution)/shard_map/pallas_call | solution.py:27
  23.7 0.0 collective-permute-done.8.near
  23.7 1.2 %collective-permute-done.9.beyond = bf16[2,64,256]{2,1,0:T(8,128)(2,1)S(1)} collective-permute-done((bf16[2,64,256]{2,1,0:T(8,128)(2,1)S(1)}, bf16[2,64,256]{2,1,0:T(8,128)(2,1)S(1)}, u32[]{:S(2)}, u32[]{:S(2)}) %collective-permute-start.9) | collective-permute-done | bytes 65568 | tf_op jit(solution)/shard_map/ppermute | solution.py:295
  24.8 1.1 %shard_map.83.refs_0_ = f32[2,64,1024]{2,1,0:T(8,128)} custom-call(bf16[2,64,256]{2,1,0:T(8,128)(2,1)S(1)} %get-tuple-element.33.refs_5_.refs_6_.high, bf16[2,64,256]{2,1,0:T(8,128)(2,1)S(1)} %get-tuple-element.39.low, bf16[2,64,256]{2,1,0:T(8,128)(2,1)S(1)} %collective-permute-done.8.near, ...), custom_call_target="tpu_custom_call", output_to_operand_aliasing={{}: (9, {})} | custom-call | tf_op jit(solution)/shard_map/pallas_call | solution.py:27
  25.9 1.3 %collective-permute-done.6.other = bf16[2,64,512]{2,1,0:T(8,128)(2,1)S(1)} collective-permute-done((bf16[2,64,512]{2,1,0:T(8,128)(2,1)S(1)}, bf16[2,64,512]{2,1,0:T(8,128)(2,1)S(1)}, u32[]{:S(2)}, u32[]{:S(2)}) %collective-permute-start.6) | collective-permute-done | bytes 131104 | tf_op jit(solution)/shard_map/ppermute | solution.py:295
  27.2 1.0 %shard_map.84 = f32[2,64,1024]{2,1,0:T(8,128)} custom-call(bf16[2,64,512]{2,1,0:T(8,128)(2,1)S(1)} %get-tuple-element.35.refs_5_.high, bf16[2,64,512]{2,1,0:T(8,128)(2,1)S(1)} %get-tuple-element.36.low, bf16[2,64,512]{2,1,0:T(8,128)(2,1)S(1)} %collective-permute-done.6.other, ...), custom_call_target="tpu_custom_call", output_to_operand_aliasing={{}: (5, {})} | custom-call | tf_op jit(solution)/shard_map/pallas_call | solution.py:27
  (2 shorter events, 0.0 us)
Async XLA Ops:
  0.0 1.0 %copy-start = (bf16[2,128,1024]{2,1,0:T(8,128)(2,1)S(1)}, bf16[2,128,1024]{2,1,0:T(8,128)(2,1)}, u32[]{:S(2)}) copy-start(bf16[2,128,1024]{2,1,0:T(8,128)(2,1)} %refs_0_.6) | copy-start | bytes 1572868
  1.2 6.4 %collective-permute-start = (bf16[2,32,1024]{2,1,0:T(8,128)(2,1)S(1)}, bf16[2,32,1024]{2,1,0:T(8,128)(2,1)S(1)}, u32[]{:S(2)}, u32[]{:S(2)}) collective-permute-start(bf16[2,32,1024]{2,1,0:T(8,128)(2,1)S(1)} %get-tuple-element.24), channel_id=1, source_target_pairs={{0,2},{2,0},{4,6},{6,4},{8,10},{10,8},{12,14},{14,12},{16,18},{18,... | collective-permute-start | bytes 393224 | tf_op jit(solution)/shard_map/ppermute | solution.py:274
  1.7 5.9 %collective-permute-start.1 = (bf16[2,32,1024]{2,1,0:T(8,128)(2,1)S(1)}, bf16[2,32,1024]{2,1,0:T(8,128)(2,1)S(1)}, u32[]{:S(2)}, u32[]{:S(2)}) collective-permute-start(bf16[2,32,1024]{2,1,0:T(8,128)(2,1)S(1)} %get-tuple-element.24), channel_id=1, source_target_pairs={{0,8},{2,0},{4,2},{6,4},{8,6},{10,16},{12,10},{14,12},{16,14},{18,... | collective-permute-start | bytes 393224 | tf_op jit(solution)/shard_map/ppermute | solution.py:276
  4.3 2.1 %copy-start.7 = (bf16[2,256]{1,0:T(2,128)(2,1)S(1)}, bf16[2,256]{1,0:T(2,128)(2,1)}, u32[]{:S(2)}) copy-start(bf16[2,256]{1,0:T(2,128)(2,1)} %taps_ref.1) | copy-start | bytes 3076
  4.3 6.6 %collective-permute-start.4 = (bf16[2,128,256]{2,1,0:T(8,128)(2,1)S(1)}, bf16[2,128,256]{2,1,0:T(8,128)(2,1)S(1)}, u32[]{:S(2)}, u32[]{:S(2)}) collective-permute-start(bf16[2,128,256]{2,1,0:T(8,128)(2,1)S(1)} %get-tuple-element.31), channel_id=1, source_target_pairs={{0,1},{1,0},{2,3},{3,2},{4,5},{5,4},{6,7},{7,6},{8,9},{9,8},{10,11... | collective-permute-start | bytes 393224 | tf_op jit(solution)/shard_map/ppermute | solution.py:277
  5.9 0.8 %copy-start.3 = (f32[2,2,128,8]{2,3,1,0:T(8,128)S(1)}, f32[2,2,128,8]{2,3,1,0:T(8,128)}, u32[]{:S(2)}) copy-start(f32[2,2,128,8]{2,3,1,0:T(8,128)} %param.11) | copy-start | bytes 49156
  5.9 0.8 %copy-start.4 = (s32[2,2,128]{2,1,0:T(2,128)S(1)}, s32[2,2,128]{2,1,0:T(2,128)}, u32[]{:S(2)}) copy-start(s32[2,2,128]{2,1,0:T(2,128)} %refs_0_.7) | copy-start | bytes 6148
  5.9 0.8 %copy-start.5 = (f32[2,2,128]{2,1,0:T(2,128)S(1)}, f32[2,2,128]{2,1,0:T(2,128)}, u32[]{:S(2)}) copy-start(f32[2,2,128]{2,1,0:T(2,128)} %refs_2_.1) | copy-start | bytes 6148
  5.9 0.8 %copy-start.6 = (f32[2,2,128]{2,1,0:T(2,128)S(1)}, f32[2,2,128]{2,1,0:T(2,128)}, u32[]{:S(2)}) copy-start(f32[2,2,128]{2,1,0:T(2,128)} %refs_3_.1) | copy-start | bytes 6148
  5.9 1.7 %copy-start.1 = (bf16[2,128,1024]{2,1,0:T(8,128)(2,1)S(1)}, bf16[2,128,1024]{2,1,0:T(8,128)(2,1)}, u32[]{:S(2)}) copy-start(bf16[2,128,1024]{2,1,0:T(8,128)(2,1)} %refs_0_.6) | copy-start | bytes 1572868
  5.9 5.1 %collective-permute-start.5 = (bf16[2,32,256]{2,1,0:T(8,128)(2,1)S(1)}, bf16[2,32,256]{2,1,0:T(8,128)(2,1)S(1)}, u32[]{:S(2)}, u32[]{:S(2)}) collective-permute-start(bf16[2,32,256]{2,1,0:T(8,128)(2,1)S(1)} %get-tuple-element.32), channel_id=1, source_target_pairs={{0,1},{1,3},{2,5},{3,0},{4,7},{5,2},{6,9},{7,4},{8,11},{9,6},{10,1... | collective-permute-start | bytes 98312 | tf_op jit(solution)/shard_map/ppermute | solution.py:279
  6.7 0.9 %copy-start.2 = (bf16[2,64,160]{2,1,0:T(8,128)(2,1)S(1)}, bf16[2,64,160]{2,1,0:T(8,128)(2,1)}, u32[]{:S(2)}) copy-start(bf16[2,64,160]{2,1,0:T(8,128)(2,1)} %refs_4_.5) | copy-start | bytes 122884
  8.1 5.7 %collective-permute-start.3 = (bf16[2,64,256]{2,1,0:T(8,128)(2,1)S(1)}, bf16[2,64,256]{2,1,0:T(8,128)(2,1)S(1)}, u32[]{:S(2)}, u32[]{:S(2)}) collective-permute-start(bf16[2,64,256]{2,1,0:T(8,128)(2,1)S(1)} %get-tuple-element.26.refs_5_.refs_0_), channel_id=1, source_target_pairs={{0,8},{2,10},{4,12},{6,14},{8,0},{10,2},{12,4},{14,6},{16,24},{18,... | collective-permute-start | bytes 196616 | tf_op jit(solution)/shard_map/ppermute | solution.py:295
  10.6 6.7 %collective-permute-start.2 = (bf16[2,64,512]{2,1,0:T(8,128)(2,1)S(1)}, bf16[2,64,512]{2,1,0:T(8,128)(2,1)S(1)}, u32[]{:S(2)}, u32[]{:S(2)}) collective-permute-start(bf16[2,64,512]{2,1,0:T(8,128)(2,1)S(1)} %get-tuple-element.27.refs_7_.refs_0_), channel_id=1, source_target_pairs={{0,8},{2,10},{4,12},{6,14},{8,0},{10,2},{12,4},{14,6},{16,24},{18,... | collective-permute-start | bytes 393224 | tf_op jit(solution)/shard_map/ppermute | solution.py:295
  11.5 8.0 %collective-permute-start.7 = (bf16[2,64,256]{2,1,0:T(8,128)(2,1)S(1)}, bf16[2,64,256]{2,1,0:T(8,128)(2,1)S(1)}, u32[]{:S(2)}, u32[]{:S(2)}) collective-permute-start(bf16[2,64,256]{2,1,0:T(8,128)(2,1)S(1)} %get-tuple-element.33.refs_5_.refs_6_.high), channel_id=1, source_target_pairs={{0,16},{2,18},{4,20},{6,22},{8,24},{10,26},{12,28},{14,30},{16,0},... | collective-permute-start | bytes 196616 | tf_op jit(solution)/shard_map/ppermute | solution.py:295
  14.0 8.7 %collective-permute-start.10 = (bf16[2,64,256]{2,1,0:T(8,128)(2,1)S(1)}, bf16[2,64,256]{2,1,0:T(8,128)(2,1)S(1)}, u32[]{:S(2)}, u32[]{:S(2)}) collective-permute-start(bf16[2,64,256]{2,1,0:T(8,128)(2,1)S(1)} %get-tuple-element.34.refs_5_.high), channel_id=1, source_target_pairs={{0,16},{2,18},{4,20},{6,22},{8,24},{10,26},{12,28},{14,30},{16,0},... | collective-permute-start | bytes 196616 | tf_op jit(solution)/shard_map/ppermute | solution.py:295
  15.3 8.3 %collective-permute-start.8 = (bf16[2,64,256]{2,1,0:T(8,128)(2,1)S(1)}, bf16[2,64,256]{2,1,0:T(8,128)(2,1)S(1)}, u32[]{:S(2)}, u32[]{:S(2)}) collective-permute-start(bf16[2,64,256]{2,1,0:T(8,128)(2,1)S(1)} %get-tuple-element.40), channel_id=1, source_target_pairs={{0,8},{2,10},{4,12},{6,14},{8,0},{10,2},{12,4},{14,6},{16,24},{18,... | collective-permute-start | bytes 196616 | tf_op jit(solution)/shard_map/ppermute | solution.py:295
  17.6 9.6 %collective-permute-start.6 = (bf16[2,64,512]{2,1,0:T(8,128)(2,1)S(1)}, bf16[2,64,512]{2,1,0:T(8,128)(2,1)S(1)}, u32[]{:S(2)}, u32[]{:S(2)}) collective-permute-start(bf16[2,64,512]{2,1,0:T(8,128)(2,1)S(1)} %get-tuple-element.35.refs_5_.high), channel_id=1, source_target_pairs={{0,16},{2,18},{4,20},{6,22},{8,24},{10,26},{12,28},{14,30},{16,0},... | collective-permute-start | bytes 393224 | tf_op jit(solution)/shard_map/ppermute | solution.py:295
  20.3 4.5 %collective-permute-start.9 = (bf16[2,64,256]{2,1,0:T(8,128)(2,1)S(1)}, bf16[2,64,256]{2,1,0:T(8,128)(2,1)S(1)}, u32[]{:S(2)}, u32[]{:S(2)}) collective-permute-start(bf16[2,64,256]{2,1,0:T(8,128)(2,1)S(1)} %get-tuple-element.41), channel_id=1, source_target_pairs={{0,8},{2,10},{4,12},{6,14},{8,0},{10,2},{12,4},{14,6},{16,24},{18,... | collective-permute-start | bytes 196616 | tf_op jit(solution)/shard_map/ppermute | solution.py:295

commit v6 on v5

--- a/solution.py
+++ b/solution.py
@@ -10,7 +10,7 @@
 
 LANES = 128
 WAIT = 2_000_000_000
-VMEM = pltpu.CompilerParams(vmem_limit_bytes=24 * 1024 * 1024)
+VMEM = pltpu.CompilerParams(vmem_limit_bytes=12 * 1024 * 1024)
 
 
 def call(body, outs, args, scratch=(), flops=0, aliases=None, in_specs=None, out_specs=None, after=()):
@@ -95,44 +95,57 @@
     return c, d
 
 
-def table_kernel(s, level, offsets_ref, coef_ref, slope_ref, base_ref, *refs):
-    m_ref, e_ref = refs[-3 - len(refs) // 5 : -1 - len(refs) // 5]
-    turned = refs[-1]
-    if len(refs) == 5:
-        refs[3][...] = refs[0][...]
+def side_table(s, q, start, first_bin, total, operands, turned, m_out, e_out):
+    offsets_ref, coef_ref, slope_ref, base_ref = operands
+    beams, bins = e_out.shape[1:]
+    fine_bin = lax.broadcasted_iota(jnp.int32, (beams, LANES), 1)
+    coarse_bin = fine_bin * LANES + first_bin
+    rows = lax.broadcasted_iota(jnp.int32, (beams, 2 * beams), 0)
+    lag = rows - offsets_ref[s, q : q + 1, :]
+    matrix = jnp.zeros((beams, 2 * beams), jnp.float32)
+    for t in range(coef_ref.shape[2]):
+        matrix += jnp.where(lag == t, coef_ref[s, q, t : t + 1, :], 0.0)
+    pad = jnp.zeros((beams - 2, 2 * beams), jnp.float32)
+    stacked = jnp.concatenate([matrix, slope_ref[s, q : q + 1, :], base_ref[s, q : q + 1, :], pad], 0)
+    turned[...] = stacked.T
+    mine = turned[pl.ds(start, beams), :]
+    high, low = split(mine[:, :beams])
+    m_out[...] = jnp.concatenate([high, low, high], 1)
+    slope = mine[:, beams : beams + 1]
+    base = mine[:, beams + 1 : beams + 2]
+    fine_cos, fine_sin = turn(slope * (fine_bin.astype(jnp.float32) / total))
+    coarse_cos, coarse_sin = turn(slope * (coarse_bin.astype(jnp.float32) / total) + base)
+    for k in range(bins // LANES):
+        c, d = coarse_cos[:, k : k + 1], coarse_sin[:, k : k + 1]
+        at = slice(k * LANES, (k + 1) * LANES)
+        e_out[0, :, at] = c * fine_cos - d * fine_sin
+        e_out[1, :, at] = d * fine_cos + c * fine_sin
+
+
+def table_kernel(s, level, *refs):
+    *operands, m_ref, e_ref, turned = refs
     beams, bins = e_ref.shape[2:]
-    taps = coef_ref.shape[2]
-    device = lax.axis_index("aperture")
-    tile = lax.axis_index("tile")
+    first_bin = lax.axis_index("tile") * bins
     total = float(bins * lax.axis_size("tile"))
-    fine_bin = lax.broadcasted_iota(jnp.int32, (beams, LANES), 1)
-    coarse_bin = fine_bin * LANES + tile * bins
-    upper = (device >> (level + s)) & 1
+    upper = (lax.axis_index("aperture") >> (level + s)) & 1
     start = pl.multiple_of(upper * beams, beams)
     for q in range(2):
         side = jnp.where(upper == q, 0, 1)
-        rows = lax.broadcasted_iota(jnp.int32, (beams, 2 * beams), 0)
-        lag = rows - offsets_ref[s, q : q + 1, :]
-        matrix = jnp.zeros((beams, 2 * beams), jnp.float32)
-        for t in range(taps):
-            matrix += jnp.where(lag == t, coef_ref[s, q, t : t + 1, :], 0.0)
-        pad = jnp.zeros((beams - 2, 2 * beams), jnp.float32)
-        stacked = jnp.concatenate(
-            [matrix, slope_ref[s, q : q + 1, :], base_ref[s, q : q + 1, :], pad], 0
-        )
-        turned[...] = stacked.T
-        mine = turned[pl.ds(start, beams), :]
-        high, low = split(mine[:, :beams])
-        m_ref[side, :, :] = jnp.concatenate([high, low, high], 1)
-        slope = mine[:, beams : beams + 1]
-        base = mine[:, beams + 1 : beams + 2]
-        fine_cos, fine_sin = turn(slope * (fine_bin.astype(jnp.float32) / total))
-        coarse_cos, coarse_sin = turn(slope * (coarse_bin.astype(jnp.float32) / total) + base)
-        for k in range(bins // LANES):
-            c, d = coarse_cos[:, k : k + 1], coarse_sin[:, k : k + 1]
-            at = slice(k * LANES, (k + 1) * LANES)
-            e_ref[side, 0, :, at] = c * fine_cos - d * fine_sin
-            e_ref[side, 1, :, at] = d * fine_cos + c * fine_sin
+        side_table(s, q, start, first_bin, total, operands, turned, m_ref.at[side], e_ref.at[side])
+
+
+def cross_table_kernel(level, first, bins, *refs):
+    *operands, m_ref, e_ref, turned = refs
+    beams = e_ref.shape[2]
+    first_bin = lax.axis_index("tile") * bins + first
+    total = float(bins * lax.axis_size("tile"))
+    upper = (lax.axis_index("aperture") >> level) & 1
+    start = pl.multiple_of((1 - upper) * beams, beams)
+    for q in range(2):
+
+        @pl.when(upper == q)
+        def _(q=q):
+            side_table(0, q, start, first_bin, total, operands, turned, m_ref.at[0], e_ref.at[0])
 
 
 def focus_kernel(first, raw, near, far, w, steering, *refs):
@@ -184,24 +197,24 @@
     return high, low
 
 
-def turned_sum(first, own, other, m, e):
-    bins = own[0][0].shape[1]
+def turned_term(first, side, given, m, e):
+    bins = given[0][0].shape[1]
     beams = m.shape[1]
     at = slice(first, first + bins)
-    re, im = None, None
-    for side, given in enumerate((own, other)):
-        terms = []
-        for part in range(2):
-            high = given[0][part]
-            stacked = [high, high] + ([given[1][part]] if len(given) > 1 else [])
-            weights = m[side][:, : len(stacked) * beams]
-            stacked = jnp.concatenate(stacked, 0)
-            terms.append(jnp.dot(weights, stacked, preferred_element_type=jnp.float32))
-        c, d = e[side, 0, :, at], e[side, 1, :, at]
-        more_re, more_im = c * terms[0] - d * terms[1], d * terms[0] + c * terms[1]
-        re = more_re if re is None else re + more_re
-        im = more_im if im is None else im + more_im
-    return re, im
+    terms = []
+    for part in range(2):
+        high = given[0][part]
+        stacked = [high, high] + ([given[1][part]] if len(given) > 1 else [])
+        weights = m[side][:, : len(stacked) * beams]
+        stacked = jnp.concatenate(stacked, 0)
+        terms.append(jnp.dot(weights, stacked, preferred_element_type=jnp.float32))
+    c, d = e[side, 0, :, at], e[side, 1, :, at]
+    return c * terms[0] - d * terms[1], d * terms[0] + c * terms[1]
+
+
+def turned_sum(first, own, other, m, e):
+    left, right = turned_term(first, 0, own, m, e), turned_term(first, 1, other, m, e)
+    return left[0] + right[0], left[1] + right[1]
 
 
 def store_split(values, high_ref, low_ref):
@@ -209,11 +222,8 @@
         high_ref[part], low_ref[part] = split(value)
 
 
-def first_merge_kernel(first, high, low, other, m, e, *refs):
-    if len(refs) == 4:
-        refs[3][...] = refs[0][...]
-        refs = refs[1:3]
-    store_split(turned_sum(first, (high, low), (other,), m, e), *refs)
+def first_merge_kernel(first, high, low, other, m, e, high_ref, low_ref):
+    store_split(turned_sum(first, (high, low), (other,), m, e), high_ref, low_ref)
 
 
 def write_image(values, first, image, held, sem):
@@ -223,19 +233,34 @@
         place = image.at[part, :, first : first + held.shape[2]]
         copies.append(pltpu.make_async_copy(held.at[part], place, sem.at[part]))
         copies[-1].start()
+    return copies
+
+
+def start_image_kernel(first, high, low, other, m, e, image, held, sem):
+    for copy in write_image(turned_sum(first, (high, low), (other,), m, e), first, image, held, sem):
+        copy.wait()
+
+
+def own_term_kernel(first, high, low, m, e, out):
+    out[0], out[1] = turned_term(first, 0, (high, low), m, e)
+
+
+def both_terms_kernel(first, high, low, over, m0, e0, mx, ex, m1, e1, out, sent):
+    given = ((high, low), (over,))
+    for m, e, at, ref in ((m0, e0, first, out), (mx, ex, 0, sent)):
+        own, other = [split_parts(turned_term(at, 0, parts, m, e)) for parts in given]
+        for part, value in enumerate(turned_sum(first, own, other, m1, e1)):
+            ref[part] = value.astype(ref.dtype)
+
+
+def end_image_kernel(first, own, other, m, e, out, got, _, image, held, held_last, sem):
+    bins = own.shape[2]
+    values = [out[part] + got[part].astype(jnp.float32) for part in range(2)]
+    copies = write_image(values, first + bins, image, held_last, sem.at[2:4])
+    term = turned_term(first, 1, (other,), m, e)
+    copies += write_image((own[0] + term[0], own[1] + term[1]), first, image, held, sem)
     for copy in copies:
         copy.wait()
-
-
-def last_merge_kernel(first, high, low, other, m, e, *refs):
-    image, held, sem = refs[-3:]
-    write_image(turned_sum(first, (high, low), (other,), m, e), first, image, held, sem)
-
-
-def both_merges_kernel(first, high, low, near, over, beyond, m0, e0, m1, e1, _, image, held, sem):
-    own = split_parts(turned_sum(first, (high, low), (near,), m0, e0))
-    other = split_parts(turned_sum(first, (over,), (beyond,), m0, e0))
-    write_image(turned_sum(first, own, other, m1, e1), first, image, held, sem)
 
 
 def cut_kernel(raw, guard, rim, corner, sem):
@@ -278,18 +303,17 @@
     steps = [(d * tiles + t, (d - 1) * tiles + t - 1) for d in range(1, count) for t in range(1, tiles)]
     corner = lax.ppermute(corner, ("aperture", "tile"), completed(steps, count * tiles))
     w = call(toeplitz_kernel, sds((2, 2 * width, 2 * width), bf16), [taps])
-    def tables(s, after=(), through=()):
-        passed = [sds(x.shape, x.dtype) for x in through]
+    def tables(body, sides, size, after=()):
         return call(
-            functools.partial(table_kernel, s, level),
-            [sds((2, beams, 3 * beams), bf16), sds((2, 2, beams, bins), f32), *passed],
-            [offsets, jnp.swapaxes(coef, 2, 3), slope, base, *through],
+            body,
+            [sds((sides, beams, 3 * beams), bf16), sds((sides, 2, beams, size), f32)],
+            [offsets, jnp.swapaxes(coef, 2, 3), slope, base],
             scratch=[pltpu.VMEM((2 * beams, 2 * beams), f32)],
             flops=20_000_000,
             after=after,
         )
 
-    first_tables = tables(0)
+    first_tables = tables(functools.partial(table_kernel, 0, level), 2, bins)
 
     def partner(value, bit):
         return lax.ppermute(value, "aperture", [(d, d ^ (1 << bit)) for d in range(count)])
@@ -305,29 +329,27 @@
             after=[after],
         )
 
-    def first_merge(first, sub, other, after, through=(), flops=0):
+    def first_merge(first, sub, other, after, flops=0):
         shape = sds(other.shape, bf16)
         return call(
             functools.partial(first_merge_kernel, first),
-            [shape, shape] + [sds(x.shape, bf16) for x in through],
-            [*sub, other, *first_tables, *through],
+            [shape, shape],
+            [*sub, other, *first_tables],
             flops=flops,
             after=[after],
         )
 
-    def write(body, size, args, image, flops=0):
+    def write(body, sizes, args, image=None):
         given = [] if image is None else [image]
-        whole_image = sds((2, beams, bins), f32)
-        args = [*args]
         return call(
             body,
-            whole_image,
-            args + given,
-            scratch=[pltpu.VMEM((2, beams, size), f32), pltpu.SemaphoreType.DMA((2,))],
+            sds((2, beams, bins), f32),
+            [*args, *given],
+            scratch=[*[pltpu.VMEM((2, beams, size), f32) for size in sizes], pltpu.SemaphoreType.DMA((4,))],
             aliases={len(args): 0} if given else {},
             in_specs=[whole] * len(args) + [anywhere] * len(given),
             out_specs=anywhere,
-            flops=flops,
+            flops=0 if given else WAIT,
         )
 
     assert bins > 2 * width
@@ -337,24 +359,29 @@
     subs.append(focus(last, width, subs[1][0], [rim, corner], WAIT))
     others = [partner(high, level) for high, _ in subs[:2]]
     over = partner(subs[2][0], level + 1)
-    *second, late = first_merge(0, subs[0], others[0], subs[2][0], [subs[2][0]], WAIT)
+    second = first_merge(0, subs[0], others[0], subs[2][0], WAIT)
     third = partner(second[0], level + 1)
-    near_last = partner(late, level)
     middle_second = first_merge(middle, subs[1], others[1], second[0])
     middle_third = partner(middle_second[0], level + 1)
-    *last_tables, over_late = tables(1, [middle_second[0]], [over])
-    beyond = partner(over_late, level)
-    image = write(functools.partial(last_merge_kernel, 0), width, [*second, third, *last_tables], None, WAIT)
-    image = write(
-        functools.partial(both_merges_kernel, last),
-        width,
-        [*subs[2], near_last, over, beyond, *first_tables, *last_tables],
-        image,
+    last_tables = tables(functools.partial(table_kernel, 1, level), 2, bins, [second[0]])
+    cross = tables(functools.partial(cross_table_kernel, level, last, bins), 1, width, [second[0]])
+    out, sent = call(
+        functools.partial(both_terms_kernel, last),
+        [sds((2, beams, width), f32), sds((2, beams, width), bf16)],
+        [*subs[2], over, *first_tables, *cross, *last_tables],
+        after=[middle_second[0]],
+    )
+    got = partner(sent, level)
+    image = write(functools.partial(start_image_kernel, 0), [width], [*second, third, *last_tables])
+    own = call(
+        functools.partial(own_term_kernel, middle),
+        sds((2, beams, last - middle), f32),
+        [*middle_second, *last_tables],
     )
     return write(
-        functools.partial(last_merge_kernel, middle),
-        last - middle,
-        [*middle_second, middle_third, *last_tables],
+        functools.partial(end_image_kernel, middle),
+        [last - middle, width],
+        [own, middle_third, *last_tables, out, got],
         image,
     )
 

time: 28.3 us -> 28.1 us (level)
  starting transfers between devices: 15.9 us -> 14.9 us
  waiting for transfers between devices: 3.88 us -> 4.59 us
    ppermute x7 -> x6, starting transfers between devices: 10.7 us -> 9.76 us  [partner(): lax.ppermute(value, 'aperture', [(d, d ^ 1 << bit) for d in range(count)])]
    ppermute x7 -> x6, waiting for transfers between devices: 3.87 us -> 4.58 us  [partner(): lax.ppermute(value, 'aperture', [(d, d ^ 1 << bit) for d in range(count)])]
    ppermute x1, starting transfers between devices: 0.52 us -> 0.01 us  [shards(): lax.ppermute(guard, 'aperture', completed([(d, d - 1) for d in range(1, c...]
    ppermute x1, starting transfers between devices: 2.64 us -> 3.08 us  [shards(): lax.ppermute(guard, 'aperture', completed([(d, d - 1) for d in range(2, c...]
    pallas_call x12 -> x14, Pallas kernels: 7.08 us -> 7.12 us  [call(): pl.pallas_call(body, out_shape=outs, in_specs=in_specs or [whole] * len(a...]
  transfers between devices with their start and end apart: 11 -> 10, of which waited for: 4 -> 3; matrix products, arithmetic and copies ran while one was open for 0% -> 0% of each run, Pallas kernels for 21% -> 22%
where the time goes in v6:
time: 28.1 us; the launch traced here: 27.9 us
  starting transfers between devices  14.9 us (53%)
  Pallas kernels  7.12 us (25%)
  waiting for transfers between devices  4.59 us (16%)
  local copies, waits for them, and re-layouts  1.07 us (4%)
    ppermute x6, starting transfers between devices, partner(): lax.ppermute(value, 'aperture', [(d, d ^ 1 << bit) for d in range(count)])  9.76 us
    pallas_call x14, Pallas kernels, call(): pl.pallas_call(body, out_shape=outs, in_specs=in_specs or [whole] * len(a...  7.12 us
    ppermute x6, waiting for transfers between devices, partner(): lax.ppermute(value, 'aperture', [(d, d ^ 1 << bit) for d in range(count)])  4.58 us
    ppermute x1, starting transfers between devices, shards(): lax.ppermute(guard, 'aperture', completed([(d, d - 1) for d in range(2, c...  3.08 us
    ppermute x1, starting transfers between devices, shards(): lax.ppermute(rim, 'tile', completed([(t, t - 1) for t in range(1, tiles)]...  1.52 us
    unnamed x16, local copies, waits for them, and re-layouts  1.07 us
  transfers between devices with their start and end apart: 10, of which 3 were waited for; matrix products, arithmetic and copies ran while one was open for 0% of the time, Pallas kernels for 22%

profile of v6, /device:TPU:0, one launch (start us, length us, event | category | flops | bytes accessed | tf_op | source)
XLA Modules:
  0.0 27.9 jit_solution(17622409856653691717)
XLA Ops:
  0.0 1.0 %copy-done = bf16[2,128,1024]{2,1,0:T(8,128)(2,1)S(1)} copy-done((bf16[2,128,1024]{2,1,0:T(8,128)(2,1)S(1)}, bf16[2,128,1024]{2,1,0:T(8,128)(2,1)}, u32[]{:S(2)}) %copy-start) | copy-done | bytes 524312
  1.0 0.1 shard_map.73
  1.2 3.1 %collective-permute-start.1 = (bf16[2,32,1024]{2,1,0:T(8,128)(2,1)S(1)}, bf16[2,32,1024]{2,1,0:T(8,128)(2,1)S(1)}, u32[]{:S(2)}, u32[]{:S(2)}) collective-permute-start(bf16[2,32,1024]{2,1,0:T(8,128)(2,1)S(1)} %get-tuple-element.26), channel_id=1, source_target_pairs={{0,8},{2,0},{4,2},{6,4},{8,6},{10,16},{12,10},{14,12},{16,14},{18,... | collective-permute-start | bytes 393224 | tf_op jit(solution)/shard_map/ppermute | solution.py:301
  4.3 0.0 collective-permute-start
  4.3 0.0 copy-start.7
  4.3 1.5 %collective-permute-start.4 = (bf16[2,128,256]{2,1,0:T(8,128)(2,1)S(1)}, bf16[2,128,256]{2,1,0:T(8,128)(2,1)S(1)}, u32[]{:S(2)}, u32[]{:S(2)}) collective-permute-start(bf16[2,128,256]{2,1,0:T(8,128)(2,1)S(1)} %get-tuple-element.33), channel_id=1, source_target_pairs={{0,1},{1,0},{2,3},{3,2},{4,5},{5,4},{6,7},{7,6},{8,9},{9,8},{10,11... | collective-permute-start | bytes 393224 | tf_op jit(solution)/shard_map/ppermute | solution.py:302
  5.8 0.0 copy-start.3
  5.8 0.0 copy-start.4
  5.8 0.0 copy-start.5
  5.8 0.0 copy-start.1
  5.8 0.6 %collective-permute-start.5 = (bf16[2,32,256]{2,1,0:T(8,128)(2,1)S(1)}, bf16[2,32,256]{2,1,0:T(8,128)(2,1)S(1)}, u32[]{:S(2)}, u32[]{:S(2)}) collective-permute-start(bf16[2,32,256]{2,1,0:T(8,128)(2,1)S(1)} %get-tuple-element.34), channel_id=1, source_target_pairs={{0,1},{1,3},{2,5},{3,0},{4,7},{5,2},{6,9},{7,4},{8,11},{9,6},{10,1... | collective-permute-start | bytes 98312 | tf_op jit(solution)/shard_map/ppermute | solution.py:304
  6.4 0.0 copy-done.7
  6.4 0.2 shard_map.74.refs_3_
  6.6 0.0 copy-start.2
  6.6 0.0 copy-done.3
  6.6 0.0 copy-done.4
  6.6 0.0 copy-done.5
  6.6 0.0 copy-done.6
  6.6 0.8 %shard_map.75 = (bf16[2,64,192]{2,1,0:T(8,128)(2,1)S(1)}, f32[2,2,64,1024]{3,2,1,0:T(8,128)S(1)}) custom-call(s32[2,2,128]{2,1,0:T(2,128)S(1)} %copy-done.4, f32[2,2,8,128]{3,2,1,0:T(8,128)S(1)} %bitcast.1, f32[2,2,128]{2,1,0:T(2,128)S(1)} %copy-done.5, f32[2,2,128]{2,1,0:T(2,128)S(1)} %copy-done.6), custom_call_target="tpu_custom_call" | custom-call | flops 20000000 | tf_op jit(solution)/shard_map/pallas_call | solution.py:27
  7.5 0.0 collective-permute-done.1.refs_2_
  7.5 0.0 collective-permute-done.refs_1_
  7.5 0.0 copy-done.1
  7.5 0.0 copy-done.2
  7.5 0.5 %shard_map.76 = (bf16[2,64,256]{2,1,0:T(8,128)(2,1)S(1)}, bf16[2,64,256]{2,1,0:T(8,128)(2,1)S(1)}) custom-call(bf16[2,128,1024]{2,1,0:T(8,128)(2,1)S(1)} %copy-done.1, bf16[2,32,1024]{2,1,0:T(8,128)(2,1)S(1)} %collective-permute-done.refs_1_, bf16[2,32,1024]{2,1,0:T(8,128)(2,1)S(1)} %collective-permute-done.1.refs_2_, ...), custom_call_target="tpu_custom_call" | custom-call | tf_op jit(solution)/shard_map/pallas_call | solution.py:27
  8.0 1.8 %collective-permute-start.3 = (bf16[2,64,256]{2,1,0:T(8,128)(2,1)S(1)}, bf16[2,64,256]{2,1,0:T(8,128)(2,1)S(1)}, u32[]{:S(2)}, u32[]{:S(2)}) collective-permute-start(bf16[2,64,256]{2,1,0:T(8,128)(2,1)S(1)} %get-tuple-element.28.refs_5_.refs_0_), channel_id=1, source_target_pairs={{0,8},{2,10},{4,12},{6,14},{8,0},{10,2},{12,4},{14,6},{16,24},{18,... | collective-permute-start | bytes 196616 | tf_op jit(solution)/shard_map/ppermute | solution.py:319
  9.8 0.7 %shard_map.77 = (bf16[2,64,512]{2,1,0:T(8,128)(2,1)S(1)}, bf16[2,64,512]{2,1,0:T(8,128)(2,1)S(1)}) custom-call(bf16[2,128,1024]{2,1,0:T(8,128)(2,1)S(1)} %copy-done.1, bf16[2,32,1024]{2,1,0:T(8,128)(2,1)S(1)} %collective-permute-done.refs_1_, bf16[2,32,1024]{2,1,0:T(8,128)(2,1)S(1)} %collective-permute-done.1.refs_2_, ...), custom_call_target="tpu_custom_call" | custom-call | tf_op jit(solution)/shard_map/pallas_call | solution.py:27
  10.5 0.4 %collective-permute-start.2 = (bf16[2,64,512]{2,1,0:T(8,128)(2,1)S(1)}, bf16[2,64,512]{2,1,0:T(8,128)(2,1)S(1)}, u32[]{:S(2)}, u32[]{:S(2)}) collective-permute-start(bf16[2,64,512]{2,1,0:T(8,128)(2,1)S(1)} %get-tuple-element.29.refs_7_.refs_0_), channel_id=1, source_target_pairs={{0,8},{2,10},{4,12},{6,14},{8,0},{10,2},{12,4},{14,6},{16,24},{18,... | collective-permute-start | bytes 393224 | tf_op jit(solution)/shard_map/ppermute | solution.py:319
  10.9 0.0 collective-permute-done.5.refs_6_
  10.9 0.0 collective-permute-done.4.refs_5_
  10.9 0.5 %shard_map.78 = (bf16[2,64,256]{2,1,0:T(8,128)(2,1)S(1)}, bf16[2,64,256]{2,1,0:T(8,128)(2,1)S(1)}) custom-call(bf16[2,128,1024]{2,1,0:T(8,128)(2,1)S(1)} %copy-done.1, bf16[2,32,1024]{2,1,0:T(8,128)(2,1)S(1)} %collective-permute-done.refs_1_, bf16[2,32,1024]{2,1,0:T(8,128)(2,1)S(1)} %collective-permute-done.1.refs_2_, ...), custom_call_target="tpu_custom_call" | custom-call | flops 2000000000 | tf_op jit(solution)/shard_map/pallas_call | solution.py:27
  11.4 2.6 %collective-permute-start.7 = (bf16[2,64,256]{2,1,0:T(8,128)(2,1)S(1)}, bf16[2,64,256]{2,1,0:T(8,128)(2,1)S(1)}, u32[]{:S(2)}, u32[]{:S(2)}) collective-permute-start(bf16[2,64,256]{2,1,0:T(8,128)(2,1)S(1)} %get-tuple-element.35.refs_5_.refs_0_), channel_id=1, source_target_pairs={{0,16},{2,18},{4,20},{6,22},{8,24},{10,26},{12,28},{14,30},{16,0},... | collective-permute-start | bytes 196616 | tf_op jit(solution)/shard_map/ppermute | solution.py:319
  14.0 0.0 collective-permute-done.3.refs_2_
  14.0 0.2 shard_map.79
  14.2 0.9 %collective-permute-start.9 = (bf16[2,64,256]{2,1,0:T(8,128)(2,1)S(1)}, bf16[2,64,256]{2,1,0:T(8,128)(2,1)S(1)}, u32[]{:S(2)}, u32[]{:S(2)}) collective-permute-start(bf16[2,64,256]{2,1,0:T(8,128)(2,1)S(1)} %get-tuple-element.36.refs_5_.refs_4_.high), channel_id=1, source_target_pairs={{0,16},{2,18},{4,20},{6,22},{8,24},{10,26},{12,28},{14,30},{16,0},... | collective-permute-start | bytes 196616 | tf_op jit(solution)/shard_map/ppermute | solution.py:319
  15.2 0.3 %shard_map.83 = (bf16[1,64,192]{2,1,0:T(8,128)(2,1)S(1)}, f32[1,2,64,256]{3,2,1,0:T(8,128)S(1)}) custom-call(s32[2,2,128]{2,1,0:T(2,128)S(1)} %copy-done.4, f32[2,2,8,128]{3,2,1,0:T(8,128)S(1)} %bitcast.2, f32[2,2,128]{2,1,0:T(2,128)S(1)} %copy-done.5, f32[2,2,128]{2,1,0:T(2,128)S(1)} %copy-done.6, bf16[2,64,256]{2,1,0:T(8,128)(2,1)S(1)} %get-tuple-element.36.refs_5_.refs_4_.high), custom_call_target="tpu_custom_call" | custom-call | flops 20000000 | tf_op jit(solution)/shard_map/pallas_call | solution.py:27
  15.5 0.8 %shard_map.81 = (bf16[2,64,192]{2,1,0:T(8,128)(2,1)S(1)}, f32[2,2,64,1024]{3,2,1,0:T(8,128)S(1)}) custom-call(s32[2,2,128]{2,1,0:T(2,128)S(1)} %copy-done.4, f32[2,2,8,128]{3,2,1,0:T(8,128)S(1)} %bitcast.3, f32[2,2,128]{2,1,0:T(2,128)S(1)} %copy-done.5, f32[2,2,128]{2,1,0:T(2,128)S(1)} %copy-done.6, ...), custom_call_target="tpu_custom_call" | custom-call | flops 20000000 | tf_op jit(solution)/shard_map/pallas_call | solution.py:27
  16.4 0.6 %collective-permute-done.2.refs_2_ = bf16[2,64,512]{2,1,0:T(8,128)(2,1)S(1)} collective-permute-done((bf16[2,64,512]{2,1,0:T(8,128)(2,1)S(1)}, bf16[2,64,512]{2,1,0:T(8,128)(2,1)S(1)}, u32[]{:S(2)}, u32[]{:S(2)}) %collective-permute-start.2) | collective-permute-done | bytes 131104 | tf_op jit(solution)/shard_map/ppermute | solution.py:319
  17.0 0.3 %shard_map.80 = (bf16[2,64,512]{2,1,0:T(8,128)(2,1)S(1)}, bf16[2,64,512]{2,1,0:T(8,128)(2,1)S(1)}) custom-call(bf16[2,64,512]{2,1,0:T(8,128)(2,1)S(1)} %get-tuple-element.29.refs_7_.refs_0_, bf16[2,64,512]{2,1,0:T(8,128)(2,1)S(1)} %get-tuple-element.30.refs_1_, bf16[2,64,512]{2,1,0:T(8,128)(2,1)S(1)} %collective-permute-done.2.refs_2_, ...), custom_call_target="tpu_custom_call" | custom-call | tf_op jit(solution)/shard_map/pallas_call | solution.py:27
  17.2 2.1 %collective-permute-start.6 = (bf16[2,64,512]{2,1,0:T(8,128)(2,1)S(1)}, bf16[2,64,512]{2,1,0:T(8,128)(2,1)S(1)}, u32[]{:S(2)}, u32[]{:S(2)}) collective-permute-start(bf16[2,64,512]{2,1,0:T(8,128)(2,1)S(1)} %get-tuple-element.37.high.refs_9_), channel_id=1, source_target_pairs={{0,16},{2,18},{4,20},{6,22},{8,24},{10,26},{12,28},{14,30},{16,0},... | collective-permute-start | bytes 393224 | tf_op jit(solution)/shard_map/ppermute | solution.py:319
  19.3 0.0 collective-permute-done.7.refs_2_
  19.3 0.6 %shard_map.84 = (f32[2,64,256]{2,1,0:T(8,128)S(1)}, bf16[2,64,256]{2,1,0:T(8,128)(2,1)S(1)}) custom-call(bf16[2,64,256]{2,1,0:T(8,128)(2,1)S(1)} %get-tuple-element.35.refs_5_.refs_0_, bf16[2,64,256]{2,1,0:T(8,128)(2,1)S(1)} %get-tuple-element.41.refs_1_, bf16[2,64,256]{2,1,0:T(8,128)(2,1)S(1)} %collective-permute-done.7.refs_2_, ...), custom_call_target="tpu_custom_call" | custom-call | tf_op jit(solution)/shard_map/pallas_call | solution.py:27
  20.0 1.9 %collective-permute-start.8 = (bf16[2,64,256]{2,1,0:T(8,128)(2,1)S(1)}, bf16[2,64,256]{2,1,0:T(8,128)(2,1)S(1)}, u32[]{:S(2)}, u32[]{:S(2)}) collective-permute-start(bf16[2,64,256]{2,1,0:T(8,128)(2,1)S(1)} %get-tuple-element.45), channel_id=1, source_target_pairs={{0,8},{2,10},{4,12},{6,14},{8,0},{10,2},{12,4},{14,6},{16,24},{18,... | collective-permute-start | bytes 196616 | tf_op jit(solution)/shard_map/ppermute | solution.py:319
  21.9 2.8 %collective-permute-done.9.other = bf16[2,64,256]{2,1,0:T(8,128)(2,1)S(1)} collective-permute-done((bf16[2,64,256]{2,1,0:T(8,128)(2,1)S(1)}, bf16[2,64,256]{2,1,0:T(8,128)(2,1)S(1)}, u32[]{:S(2)}, u32[]{:S(2)}) %collective-permute-start.9) | collective-permute-done | bytes 65568 | tf_op jit(solution)/shard_map/ppermute | solution.py:319
  24.7 0.9 %shard_map.85._ = f32[2,64,1024]{2,1,0:T(8,128)} custom-call(bf16[2,64,256]{2,1,0:T(8,128)(2,1)S(1)} %get-tuple-element.36.refs_5_.refs_4_.high, bf16[2,64,256]{2,1,0:T(8,128)(2,1)S(1)} %get-tuple-element.46.low, bf16[2,64,256]{2,1,0:T(8,128)(2,1)S(1)} %collective-permute-done.9.other, bf16[2,64,192]{2,1,0:T(8,128)(2,1)S(1)} %get-tuple-element.39.m.refs_7_, ...), custom_call_target="tpu_custom_call" | custom-call | flops 2000000000 | tf_op jit(solution)/shard_map/pallas_call | solution.py:27
  25.5 0.2 shard_map.82.own
  25.7 1.2 %collective-permute-done.8.got = bf16[2,64,256]{2,1,0:T(8,128)(2,1)S(1)} collective-permute-done((bf16[2,64,256]{2,1,0:T(8,128)(2,1)S(1)}, bf16[2,64,256]{2,1,0:T(8,128)(2,1)S(1)}, u32[]{:S(2)}, u32[]{:S(2)}) %collective-permute-start.8) | collective-permute-done | bytes 65568 | tf_op jit(solution)/shard_map/ppermute | solution.py:319
  27.0 0.0 collective-permute-done.6.other
  27.0 0.9 %shard_map.86 = f32[2,64,1024]{2,1,0:T(8,128)} custom-call(f32[2,64,512]{2,1,0:T(8,128)S(1)} %shard_map.82.own, bf16[2,64,512]{2,1,0:T(8,128)(2,1)S(1)} %collective-permute-done.6.other, bf16[2,64,192]{2,1,0:T(8,128)(2,1)S(1)} %get-tuple-element.39.m.refs_7_, f32[2,2,64,1024]{3,2,1,0:T(8,128)S(1)} %get-tuple-element.40.e.refs_8_, ...), custom_call_target="tpu_custom_call", output_to_operand_aliasing={{}: (6, {})} | custom-call | tf_op jit(solution)/shard_map/pallas_call | solution.py:27
  (2 shorter events, 0.0 us)
Async XLA Ops:
  0.0 1.0 %copy-start = (bf16[2,128,1024]{2,1,0:T(8,128)(2,1)S(1)}, bf16[2,128,1024]{2,1,0:T(8,128)(2,1)}, u32[]{:S(2)}) copy-start(bf16[2,128,1024]{2,1,0:T(8,128)(2,1)} %refs_0_.9) | copy-start | bytes 1572868
  1.2 6.3 %collective-permute-start.1 = (bf16[2,32,1024]{2,1,0:T(8,128)(2,1)S(1)}, bf16[2,32,1024]{2,1,0:T(8,128)(2,1)S(1)}, u32[]{:S(2)}, u32[]{:S(2)}) collective-permute-start(bf16[2,32,1024]{2,1,0:T(8,128)(2,1)S(1)} %get-tuple-element.26), channel_id=1, source_target_pairs={{0,8},{2,0},{4,2},{6,4},{8,6},{10,16},{12,10},{14,12},{16,14},{18,... | collective-permute-start | bytes 393224 | tf_op jit(solution)/shard_map/ppermute | solution.py:301
  4.3 3.2 %collective-permute-start = (bf16[2,32,1024]{2,1,0:T(8,128)(2,1)S(1)}, bf16[2,32,1024]{2,1,0:T(8,128)(2,1)S(1)}, u32[]{:S(2)}, u32[]{:S(2)}) collective-permute-start(bf16[2,32,1024]{2,1,0:T(8,128)(2,1)S(1)} %get-tuple-element.26), channel_id=1, source_target_pairs={{0,2},{2,0},{4,6},{6,4},{8,10},{10,8},{12,14},{14,12},{16,18},{18,... | collective-permute-start | bytes 393224 | tf_op jit(solution)/shard_map/ppermute | solution.py:299
  4.3 2.1 %copy-start.7 = (bf16[2,256]{1,0:T(2,128)(2,1)S(1)}, bf16[2,256]{1,0:T(2,128)(2,1)}, u32[]{:S(2)}) copy-start(bf16[2,256]{1,0:T(2,128)(2,1)} %taps_ref.1) | copy-start | bytes 3076
  4.3 6.6 %collective-permute-start.4 = (bf16[2,128,256]{2,1,0:T(8,128)(2,1)S(1)}, bf16[2,128,256]{2,1,0:T(8,128)(2,1)S(1)}, u32[]{:S(2)}, u32[]{:S(2)}) collective-permute-start(bf16[2,128,256]{2,1,0:T(8,128)(2,1)S(1)} %get-tuple-element.33), channel_id=1, source_target_pairs={{0,1},{1,0},{2,3},{3,2},{4,5},{5,4},{6,7},{7,6},{8,9},{9,8},{10,11... | collective-permute-start | bytes 393224 | tf_op jit(solution)/shard_map/ppermute | solution.py:302
  5.8 0.8 %copy-start.3 = (f32[2,2,128,8]{2,3,1,0:T(8,128)S(1)}, f32[2,2,128,8]{2,3,1,0:T(8,128)}, u32[]{:S(2)}) copy-start(f32[2,2,128,8]{2,3,1,0:T(8,128)} %param.11) | copy-start | bytes 49156
  5.8 0.8 %copy-start.4 = (s32[2,2,128]{2,1,0:T(2,128)S(1)}, s32[2,2,128]{2,1,0:T(2,128)}, u32[]{:S(2)}) copy-start(s32[2,2,128]{2,1,0:T(2,128)} %refs_0_.11) | copy-start | bytes 6148
  5.8 0.8 %copy-start.5 = (f32[2,2,128]{2,1,0:T(2,128)S(1)}, f32[2,2,128]{2,1,0:T(2,128)}, u32[]{:S(2)}) copy-start(f32[2,2,128]{2,1,0:T(2,128)} %refs_2_.5) | copy-start | bytes 6148
  5.8 0.8 %copy-start.6 = (f32[2,2,128]{2,1,0:T(2,128)S(1)}, f32[2,2,128]{2,1,0:T(2,128)}, u32[]{:S(2)}) copy-start(f32[2,2,128]{2,1,0:T(2,128)} %refs_3_.5) | copy-start | bytes 6148
  5.8 1.7 %copy-start.1 = (bf16[2,128,1024]{2,1,0:T(8,128)(2,1)S(1)}, bf16[2,128,1024]{2,1,0:T(8,128)(2,1)}, u32[]{:S(2)}) copy-start(bf16[2,128,1024]{2,1,0:T(8,128)(2,1)} %refs_0_.9) | copy-start | bytes 1572868
  5.8 5.1 %collective-permute-start.5 = (bf16[2,32,256]{2,1,0:T(8,128)(2,1)S(1)}, bf16[2,32,256]{2,1,0:T(8,128)(2,1)S(1)}, u32[]{:S(2)}, u32[]{:S(2)}) collective-permute-start(bf16[2,32,256]{2,1,0:T(8,128)(2,1)S(1)} %get-tuple-element.34), channel_id=1, source_target_pairs={{0,1},{1,3},{2,5},{3,0},{4,7},{5,2},{6,9},{7,4},{8,11},{9,6},{10,1... | collective-permute-start | bytes 98312 | tf_op jit(solution)/shard_map/ppermute | solution.py:304
  6.6 0.9 %copy-start.2 = (bf16[2,64,160]{2,1,0:T(8,128)(2,1)S(1)}, bf16[2,64,160]{2,1,0:T(8,128)(2,1)}, u32[]{:S(2)}) copy-start(bf16[2,64,160]{2,1,0:T(8,128)(2,1)} %refs_4_.5) | copy-start | bytes 122884
  8.0 6.0 %collective-permute-start.3 = (bf16[2,64,256]{2,1,0:T(8,128)(2,1)S(1)}, bf16[2,64,256]{2,1,0:T(8,128)(2,1)S(1)}, u32[]{:S(2)}, u32[]{:S(2)}) collective-permute-start(bf16[2,64,256]{2,1,0:T(8,128)(2,1)S(1)} %get-tuple-element.28.refs_5_.refs_0_), channel_id=1, source_target_pairs={{0,8},{2,10},{4,12},{6,14},{8,0},{10,2},{12,4},{14,6},{16,24},{18,... | collective-permute-start | bytes 196616 | tf_op jit(solution)/shard_map/ppermute | solution.py:319
  10.5 6.4 %collective-permute-start.2 = (bf16[2,64,512]{2,1,0:T(8,128)(2,1)S(1)}, bf16[2,64,512]{2,1,0:T(8,128)(2,1)S(1)}, u32[]{:S(2)}, u32[]{:S(2)}) collective-permute-start(bf16[2,64,512]{2,1,0:T(8,128)(2,1)S(1)} %get-tuple-element.29.refs_7_.refs_0_), channel_id=1, source_target_pairs={{0,8},{2,10},{4,12},{6,14},{8,0},{10,2},{12,4},{14,6},{16,24},{18,... | collective-permute-start | bytes 393224 | tf_op jit(solution)/shard_map/ppermute | solution.py:319
  11.4 7.9 %collective-permute-start.7 = (bf16[2,64,256]{2,1,0:T(8,128)(2,1)S(1)}, bf16[2,64,256]{2,1,0:T(8,128)(2,1)S(1)}, u32[]{:S(2)}, u32[]{:S(2)}) collective-permute-start(bf16[2,64,256]{2,1,0:T(8,128)(2,1)S(1)} %get-tuple-element.35.refs_5_.refs_0_), channel_id=1, source_target_pairs={{0,16},{2,18},{4,20},{6,22},{8,24},{10,26},{12,28},{14,30},{16,0},... | collective-permute-start | bytes 196616 | tf_op jit(solution)/shard_map/ppermute | solution.py:319
  14.2 10.4 %collective-permute-start.9 = (bf16[2,64,256]{2,1,0:T(8,128)(2,1)S(1)}, bf16[2,64,256]{2,1,0:T(8,128)(2,1)S(1)}, u32[]{:S(2)}, u32[]{:S(2)}) collective-permute-start(bf16[2,64,256]{2,1,0:T(8,128)(2,1)S(1)} %get-tuple-element.36.refs_5_.refs_4_.high), channel_id=1, source_target_pairs={{0,16},{2,18},{4,20},{6,22},{8,24},{10,26},{12,28},{14,30},{16,0},... | collective-permute-start | bytes 196616 | tf_op jit(solution)/shard_map/ppermute | solution.py:319
  17.2 9.7 %collective-permute-start.6 = (bf16[2,64,512]{2,1,0:T(8,128)(2,1)S(1)}, bf16[2,64,512]{2,1,0:T(8,128)(2,1)S(1)}, u32[]{:S(2)}, u32[]{:S(2)}) collective-permute-start(bf16[2,64,512]{2,1,0:T(8,128)(2,1)S(1)} %get-tuple-element.37.high.refs_9_), channel_id=1, source_target_pairs={{0,16},{2,18},{4,20},{6,22},{8,24},{10,26},{12,28},{14,30},{16,0},... | collective-permute-start | bytes 393224 | tf_op jit(solution)/shard_map/ppermute | solution.py:319
  20.0 7.0 %collective-permute-start.8 = (bf16[2,64,256]{2,1,0:T(8,128)(2,1)S(1)}, bf16[2,64,256]{2,1,0:T(8,128)(2,1)S(1)}, u32[]{:S(2)}, u32[]{:S(2)}) collective-permute-start(bf16[2,64,256]{2,1,0:T(8,128)(2,1)S(1)} %get-tuple-element.45), channel_id=1, source_target_pairs={{0,8},{2,10},{4,12},{6,14},{8,0},{10,2},{12,4},{14,6},{16,24},{18,... | collective-permute-start | bytes 196616 | tf_op jit(solution)/shard_map/ppermute | solution.py:319

commit v7 on v6

--- a/solution.py
+++ b/solution.py
@@ -148,14 +148,14 @@
             side_table(0, q, start, first_bin, total, operands, turned, m_ref.at[0], e_ref.at[0])
 
 
-def focus_kernel(first, raw, near, far, w, steering, *refs):
+def focus_kernel(first, cuts, raw, near, far, w, steering, *refs):
     x = refs[-1]
     pulses, guards = raw.shape[1], near.shape[1]
     width = w.shape[1] // 2
     rows = pulses + guards
     blocks = x.shape[0] // rows - 1
-    has_rim = first + blocks * width == raw.shape[2]
-    high_ref, low_ref = refs[-3:-1]
+    outs = refs[-1 - 2 * len(cuts) : -1]
+    ahead = refs[: len(refs) - 1 - len(outs)] if first + blocks * width < raw.shape[2] else ()
     device = lax.axis_index("aperture")
     even = device % 2 == 0
     followed = device < lax.axis_size("aperture") - 1
@@ -181,15 +181,21 @@
     out = jnp.dot(x[: blocks * rows], w[0], preferred_element_type=jnp.float32)
     out += jnp.dot(x[rows:], w[1], preferred_element_type=jnp.float32)
     out = out.astype(jnp.bfloat16)
+    places = [(n, at) for n, size in enumerate(cuts) for at in range(0, size, LANES)]
+    if ahead:
+        places = places[ahead[0].shape[2] // LANES :]
+        for ref, value in zip(outs, ahead):
+            ref[:, :, : value.shape[2]] = value[...]
     for b in range(blocks):
         re = out[b * rows : (b + 1) * rows, :width]
         im = out[b * rows : (b + 1) * rows, width:]
         sub = jnp.dot(turned, re, preferred_element_type=jnp.float32)
         sub += jnp.dot(crossed, im, preferred_element_type=jnp.float32)
-        high, low = split(sub)
-        at = slice(b * width, (b + 1) * width)
-        high_ref[0, :, at], high_ref[1, :, at] = high[:beams], high[beams:]
-        low_ref[0, :, at], low_ref[1, :, at] = low[:beams], low[beams:]
+        for k in range(width // LANES):
+            n, at = places[b * (width // LANES) + k]
+            for ref, value in zip(outs[2 * n : 2 * n + 2], split(sub[:, k * LANES : (k + 1) * LANES])):
+                ref[0, :, at : at + LANES] = value[:beams]
+                ref[1, :, at : at + LANES] = value[beams:]
 
 
 def split_parts(values):
@@ -253,10 +259,9 @@
             ref[part] = value.astype(ref.dtype)
 
 
-def end_image_kernel(first, own, other, m, e, out, got, _, image, held, held_last, sem):
-    bins = own.shape[2]
+def end_image_kernel(first, first_out, own, other, m, e, out, got, _, image, held, held_out, sem):
     values = [out[part] + got[part].astype(jnp.float32) for part in range(2)]
-    copies = write_image(values, first + bins, image, held_last, sem.at[2:4])
+    copies = write_image(values, first_out, image, held_out, sem.at[2:4])
     term = turned_term(first, 1, (other,), m, e)
     copies += write_image((own[0] + term[0], own[1] + term[1]), first, image, held, sem)
     for copy in copies:
@@ -318,13 +323,13 @@
     def partner(value, bit):
         return lax.ppermute(value, "aperture", [(d, d ^ (1 << bit)) for d in range(count)])
 
-    def focus(first, size, after, rims=(), flops=0):
+    def focus(first, cuts, blocks, after, more=(), flops=0):
         rows = pulses + guards
         return call(
-            functools.partial(focus_kernel, first),
-            [sds((2, beams, size), bf16)] * 2,
-            [raw, near, far, w, steering, *rims],
-            scratch=[pltpu.VMEM(((size // width + 1) * rows, 2 * width), bf16)],
+            functools.partial(focus_kernel, first, cuts),
+            [sds((2, beams, size), bf16) for size in cuts for _ in range(2)],
+            [raw, near, far, w, steering, *more],
+            scratch=[pltpu.VMEM(((blocks + 1) * rows, 2 * width), bf16)],
             flops=flops,
             after=[after],
         )
@@ -336,7 +341,7 @@
             [shape, shape],
             [*sub, other, *first_tables],
             flops=flops,
-            after=[after],
+            after=after,
         )
 
     def write(body, sizes, args, image=None):
@@ -352,36 +357,37 @@
             flops=0 if given else WAIT,
         )
 
-    assert bins > 2 * width
-    middle, last = width, bins - width
-    subs = [focus(0, width, first_tables[0])]
-    subs.append(focus(middle, last - middle, subs[0][0]))
-    subs.append(focus(last, width, subs[1][0], [rim, corner], WAIT))
-    others = [partner(high, level) for high, _ in subs[:2]]
-    over = partner(subs[2][0], level + 1)
-    second = first_merge(0, subs[0], others[0], subs[2][0], WAIT)
+    assert bins >= 4 * width and bins % width == 0
+    middle, last = width + LANES, bins - width
+    *sub, high, low = focus(0, [middle, 2 * width - middle], 2, first_tables[0])
+    crossing = focus(2 * width, [last - middle], (last - 2 * width) // width, sub[0], [high, low])
+    last_sub = focus(last, [width], 1, crossing[0], [rim, corner], WAIT)
+    other = partner(sub[0], level)
+    over = partner(crossing[0], level + 1)
+    last_other = partner(last_sub[0], level)
+    second = first_merge(0, sub, other, [last_sub[0]], WAIT)
     third = partner(second[0], level + 1)
-    middle_second = first_merge(middle, subs[1], others[1], second[0])
-    middle_third = partner(middle_second[0], level + 1)
     last_tables = tables(functools.partial(table_kernel, 1, level), 2, bins, [second[0]])
-    cross = tables(functools.partial(cross_table_kernel, level, last, bins), 1, width, [second[0]])
+    cross = tables(functools.partial(cross_table_kernel, level, middle, bins), 1, last - middle, [second[0]])
+    last_second = first_merge(last, last_sub, last_other, [last_tables[0], cross[0]], WAIT)
+    last_third = partner(last_second[0], level + 1)
     out, sent = call(
-        functools.partial(both_terms_kernel, last),
-        [sds((2, beams, width), f32), sds((2, beams, width), bf16)],
-        [*subs[2], over, *first_tables, *cross, *last_tables],
-        after=[middle_second[0]],
+        functools.partial(both_terms_kernel, middle),
+        [sds((2, beams, last - middle), f32), sds((2, beams, last - middle), bf16)],
+        [*crossing, over, *first_tables, *cross, *last_tables],
+        after=[last_second[0]],
     )
     got = partner(sent, level)
-    image = write(functools.partial(start_image_kernel, 0), [width], [*second, third, *last_tables])
+    image = write(functools.partial(start_image_kernel, 0), [middle], [*second, third, *last_tables])
     own = call(
-        functools.partial(own_term_kernel, middle),
-        sds((2, beams, last - middle), f32),
-        [*middle_second, *last_tables],
+        functools.partial(own_term_kernel, last),
+        sds((2, beams, width), f32),
+        [*last_second, *last_tables],
     )
     return write(
-        functools.partial(end_image_kernel, middle),
-        [last - middle, width],
-        [own, middle_third, *last_tables, out, got],
+        functools.partial(end_image_kernel, last, middle),
+        [width, last - middle],
+        [own, last_third, *last_tables, out, got],
         image,
     )
 

time: 28.1 us -> 27.1 us (0.964)
  waiting for transfers between devices: 4.59 us -> 3.96 us
  starting transfers between devices: 14.9 us -> 14.4 us
    ppermute x6, waiting for transfers between devices: 4.58 us -> 3.95 us  [partner(): lax.ppermute(value, 'aperture', [(d, d ^ 1 << bit) for d in range(count)])]
    ppermute x6, starting transfers between devices: 9.76 us -> 9.28 us  [partner(): lax.ppermute(value, 'aperture', [(d, d ^ 1 << bit) for d in range(count)])]
  transfers between devices with their start and end apart: 10 -> 10, of which waited for: 3 -> 3; matrix products, arithmetic and copies ran while one was open for 0% -> 0% of each run, Pallas kernels for 22% -> 23%
where the time goes in v7:
time: 27.1 us; the launch traced here: 26.9 us
  starting transfers between devices  14.4 us (53%)
  Pallas kernels  7.26 us (27%)
  waiting for transfers between devices  3.96 us (15%)
  local copies, waits for them, and re-layouts  1.07 us (4%)
    ppermute x6, starting transfers between devices, partner(): lax.ppermute(value, 'aperture', [(d, d ^ 1 << bit) for d in range(count)])  9.28 us
    pallas_call x14, Pallas kernels, call(): pl.pallas_call(body, out_shape=outs, in_specs=in_specs or [whole] * len(a...  7.26 us
    ppermute x6, waiting for transfers between devices, partner(): lax.ppermute(value, 'aperture', [(d, d ^ 1 << bit) for d in range(count)])  3.95 us
    ppermute x1, starting transfers between devices, shards(): lax.ppermute(guard, 'aperture', completed([(d, d - 1) for d in range(2, c...  3.08 us
    ppermute x1, starting transfers between devices, shards(): lax.ppermute(rim, 'tile', completed([(t, t - 1) for t in range(1, tiles)]...  1.52 us
    unnamed x16, local copies, waits for them, and re-layouts  1.07 us
    ppermute x1, starting transfers between devices, shards(): lax.ppermute(corner, ('aperture', 'tile'), completed(steps, count * tiles))  0.56 us
  transfers between devices with their start and end apart: 10, of which 3 were waited for; matrix products, arithmetic and copies ran while one was open for 0% of the time, Pallas kernels for 23%

profile of v7, /device:TPU:0, one launch (start us, length us, event | category | flops | bytes accessed | tf_op | source)
XLA Modules:
  0.0 26.9 jit_solution(5674059581267554989)
XLA Ops:
  0.0 1.0 %copy-done = bf16[2,128,1024]{2,1,0:T(8,128)(2,1)S(1)} copy-done((bf16[2,128,1024]{2,1,0:T(8,128)(2,1)S(1)}, bf16[2,128,1024]{2,1,0:T(8,128)(2,1)}, u32[]{:S(2)}) %copy-start) | copy-done | bytes 524312
  1.0 0.1 shard_map.73
  1.2 3.1 %collective-permute-start.1 = (bf16[2,32,1024]{2,1,0:T(8,128)(2,1)S(1)}, bf16[2,32,1024]{2,1,0:T(8,128)(2,1)S(1)}, u32[]{:S(2)}, u32[]{:S(2)}) collective-permute-start(bf16[2,32,1024]{2,1,0:T(8,128)(2,1)S(1)} %get-tuple-element.28), channel_id=1, source_target_pairs={{0,8},{2,0},{4,2},{6,4},{8,6},{10,16},{12,10},{14,12},{16,14},{18,... | collective-permute-start | bytes 393224 | tf_op jit(solution)/shard_map/ppermute | solution.py:306
  4.3 0.0 collective-permute-start
  4.3 0.0 copy-start.7
  4.3 1.5 %collective-permute-start.2 = (bf16[2,128,256]{2,1,0:T(8,128)(2,1)S(1)}, bf16[2,128,256]{2,1,0:T(8,128)(2,1)S(1)}, u32[]{:S(2)}, u32[]{:S(2)}) collective-permute-start(bf16[2,128,256]{2,1,0:T(8,128)(2,1)S(1)} %get-tuple-element.29), channel_id=1, source_target_pairs={{0,1},{1,0},{2,3},{3,2},{4,5},{5,4},{6,7},{7,6},{8,9},{9,8},{10,11... | collective-permute-start | bytes 393224 | tf_op jit(solution)/shard_map/ppermute | solution.py:307
  5.8 0.0 copy-start.3
  5.8 0.0 copy-start.4
  5.8 0.0 copy-start.5
  5.8 0.0 copy-start.1
  5.8 0.6 %collective-permute-start.3 = (bf16[2,32,256]{2,1,0:T(8,128)(2,1)S(1)}, bf16[2,32,256]{2,1,0:T(8,128)(2,1)S(1)}, u32[]{:S(2)}, u32[]{:S(2)}) collective-permute-start(bf16[2,32,256]{2,1,0:T(8,128)(2,1)S(1)} %get-tuple-element.30), channel_id=1, source_target_pairs={{0,1},{1,3},{2,5},{3,0},{4,7},{5,2},{6,9},{7,4},{8,11},{9,6},{10,1... | collective-permute-start | bytes 98312 | tf_op jit(solution)/shard_map/ppermute | solution.py:309
  6.4 0.0 copy-done.7
  6.4 0.2 shard_map.74.refs_3_
  6.6 0.0 copy-start.2
  6.6 0.0 copy-done.3
  6.6 0.0 copy-done.4
  6.6 0.0 copy-done.5
  6.6 0.0 copy-done.6
  6.6 0.8 %shard_map.75 = (bf16[2,64,192]{2,1,0:T(8,128)(2,1)S(1)}, f32[2,2,64,1024]{3,2,1,0:T(8,128)S(1)}) custom-call(s32[2,2,128]{2,1,0:T(2,128)S(1)} %copy-done.4, f32[2,2,8,128]{3,2,1,0:T(8,128)S(1)} %bitcast.1, f32[2,2,128]{2,1,0:T(2,128)S(1)} %copy-done.5, f32[2,2,128]{2,1,0:T(2,128)S(1)} %copy-done.6), custom_call_target="tpu_custom_call" | custom-call | flops 20000000 | tf_op jit(solution)/shard_map/pallas_call | solution.py:27
  7.5 0.0 collective-permute-done.1.refs_2_
  7.5 0.0 collective-permute-done.refs_1_
  7.5 0.0 copy-done.1
  7.5 0.0 copy-done.2
  7.5 0.7 %shard_map.76 = (bf16[2,64,384]{2,1,0:T(8,128)(2,1)S(1)}, bf16[2,64,384]{2,1,0:T(8,128)(2,1)S(1)}, bf16[2,64,128]{2,1,0:T(8,128)(2,1)S(1)}, bf16[2,64,128]{2,1,0:T(8,128)(2,1)S(1)}) custom-call(bf16[2,128,1024]{2,1,0:T(8,128)(2,1)S(1)} %copy-done.1, bf16[2,32,1024]{2,1,0:T(8,128)(2,1)S(1)} %collective-permute-done.refs_1_, ...), custom_call_target="tpu_custom_call" | custom-call | tf_op jit(solution)/shard_map/pallas_call | solution.py:27
  8.2 1.8 %collective-permute-start.5 = (bf16[2,64,384]{2,1,0:T(8,128)(2,1)S(1)}, bf16[2,64,384]{2,1,0:T(8,128)(2,1)S(1)}, u32[]{:S(2)}, u32[]{:S(2)}) collective-permute-start(bf16[2,64,384]{2,1,0:T(8,128)(2,1)S(1)} %get-tuple-element.34.refs_7_.refs_0_), channel_id=1, source_target_pairs={{0,8},{2,10},{4,12},{6,14},{8,0},{10,2},{12,4},{14,6},{16,24},{18,... | collective-permute-start | bytes 294920 | tf_op jit(solution)/shard_map/ppermute | solution.py:324
  10.0 0.5 %shard_map.77 = (bf16[2,64,384]{2,1,0:T(8,128)(2,1)S(1)}, bf16[2,64,384]{2,1,0:T(8,128)(2,1)S(1)}) custom-call(bf16[2,128,1024]{2,1,0:T(8,128)(2,1)S(1)} %copy-done.1, bf16[2,32,1024]{2,1,0:T(8,128)(2,1)S(1)} %collective-permute-done.refs_1_, bf16[2,32,1024]{2,1,0:T(8,128)(2,1)S(1)} %collective-permute-done.1.refs_2_, ...), custom_call_target="tpu_custom_call" | custom-call | tf_op jit(solution)/shard_map/pallas_call | solution.py:27
  10.5 2.1 %collective-permute-start.7 = (bf16[2,64,384]{2,1,0:T(8,128)(2,1)S(1)}, bf16[2,64,384]{2,1,0:T(8,128)(2,1)S(1)}, u32[]{:S(2)}, u32[]{:S(2)}) collective-permute-start(bf16[2,64,384]{2,1,0:T(8,128)(2,1)S(1)} %get-tuple-element.35.refs_7_.refs_0_), channel_id=1, source_target_pairs={{0,16},{2,18},{4,20},{6,22},{8,24},{10,26},{12,28},{14,30},{16,0},... | collective-permute-start | bytes 294920 | tf_op jit(solution)/shard_map/ppermute | solution.py:324
  12.6 0.0 collective-permute-done.3.refs_6_
  12.6 0.0 collective-permute-done.2.refs_5_
  12.6 0.5 %shard_map.78 = (bf16[2,64,256]{2,1,0:T(8,128)(2,1)S(1)}, bf16[2,64,256]{2,1,0:T(8,128)(2,1)S(1)}) custom-call(bf16[2,128,1024]{2,1,0:T(8,128)(2,1)S(1)} %copy-done.1, bf16[2,32,1024]{2,1,0:T(8,128)(2,1)S(1)} %collective-permute-done.refs_1_, bf16[2,32,1024]{2,1,0:T(8,128)(2,1)S(1)} %collective-permute-done.1.refs_2_, ...), custom_call_target="tpu_custom_call" | custom-call | flops 2000000000 | tf_op jit(solution)/shard_map/pallas_call | solution.py:27
  13.1 0.9 %collective-permute-start.4 = (bf16[2,64,256]{2,1,0:T(8,128)(2,1)S(1)}, bf16[2,64,256]{2,1,0:T(8,128)(2,1)S(1)}, u32[]{:S(2)}, u32[]{:S(2)}) collective-permute-start(bf16[2,64,256]{2,1,0:T(8,128)(2,1)S(1)} %get-tuple-element.36.refs_5_.refs_0_), channel_id=1, source_target_pairs={{0,8},{2,10},{4,12},{6,14},{8,0},{10,2},{12,4},{14,6},{16,24},{18,... | collective-permute-start | bytes 196616 | tf_op jit(solution)/shard_map/ppermute | solution.py:324
  14.0 0.0 collective-permute-done.5.refs_2_
  14.0 0.3 shard_map.79
  14.3 2.5 %collective-permute-start.9 = (bf16[2,64,384]{2,1,0:T(8,128)(2,1)S(1)}, bf16[2,64,384]{2,1,0:T(8,128)(2,1)S(1)}, u32[]{:S(2)}, u32[]{:S(2)}) collective-permute-start(bf16[2,64,384]{2,1,0:T(8,128)(2,1)S(1)} %get-tuple-element.40.refs_4_.high), channel_id=1, source_target_pairs={{0,16},{2,18},{4,20},{6,22},{8,24},{10,26},{12,28},{14,30},{16,0},... | collective-permute-start | bytes 294920 | tf_op jit(solution)/shard_map/ppermute | solution.py:324
  16.8 0.3 %shard_map.81 = (bf16[1,64,192]{2,1,0:T(8,128)(2,1)S(1)}, f32[1,2,64,384]{3,2,1,0:T(8,128)S(1)}) custom-call(s32[2,2,128]{2,1,0:T(2,128)S(1)} %copy-done.4, f32[2,2,8,128]{3,2,1,0:T(8,128)S(1)} %bitcast.2, f32[2,2,128]{2,1,0:T(2,128)S(1)} %copy-done.5, f32[2,2,128]{2,1,0:T(2,128)S(1)} %copy-done.6, bf16[2,64,384]{2,1,0:T(8,128)(2,1)S(1)} %get-tuple-element.40.refs_4_.high), custom_call_target="tpu_custom_call" | custom-call | flops 20000000 | tf_op jit(solution)/shard_map/pallas_call | solution.py:27
  17.2 0.8 %shard_map.80 = (bf16[2,64,192]{2,1,0:T(8,128)(2,1)S(1)}, f32[2,2,64,1024]{3,2,1,0:T(8,128)S(1)}) custom-call(s32[2,2,128]{2,1,0:T(2,128)S(1)} %copy-done.4, f32[2,2,8,128]{3,2,1,0:T(8,128)S(1)} %bitcast.3, f32[2,2,128]{2,1,0:T(2,128)S(1)} %copy-done.5, f32[2,2,128]{2,1,0:T(2,128)S(1)} %copy-done.6, bf16[2,64,384]{2,1,0:T(8,128)(2,1)S(1)} %get-tuple-element.40.refs_4_.high), custom_call_target="tpu_custom_call" | custom-call | flops 20000000 | tf_op jit(solution)/shard_map/pallas_call | solution.py:27
  18.0 0.3 %collective-permute-done.4.refs_2_ = bf16[2,64,256]{2,1,0:T(8,128)(2,1)S(1)} collective-permute-done((bf16[2,64,256]{2,1,0:T(8,128)(2,1)S(1)}, bf16[2,64,256]{2,1,0:T(8,128)(2,1)S(1)}, u32[]{:S(2)}, u32[]{:S(2)}) %collective-permute-start.4) | collective-permute-done | bytes 65568 | tf_op jit(solution)/shard_map/ppermute | solution.py:324
  18.3 0.2 shard_map.82
  18.5 1.2 %collective-permute-start.6 = (bf16[2,64,256]{2,1,0:T(8,128)(2,1)S(1)}, bf16[2,64,256]{2,1,0:T(8,128)(2,1)S(1)}, u32[]{:S(2)}, u32[]{:S(2)}) collective-permute-start(bf16[2,64,256]{2,1,0:T(8,128)(2,1)S(1)} %get-tuple-element.43.high.refs_9_), channel_id=1, source_target_pairs={{0,16},{2,18},{4,20},{6,22},{8,24},{10,26},{12,28},{14,30},{16,0},... | collective-permute-start | bytes 196616 | tf_op jit(solution)/shard_map/ppermute | solution.py:324
  19.7 0.2 shard_map.83.own
  19.9 0.0 collective-permute-done.7.refs_2_
  19.9 0.8 %shard_map.84 = (f32[2,64,384]{2,1,0:T(8,128)S(1)}, bf16[2,64,384]{2,1,0:T(8,128)(2,1)S(1)}) custom-call(bf16[2,64,384]{2,1,0:T(8,128)(2,1)S(1)} %get-tuple-element.35.refs_7_.refs_0_, bf16[2,64,384]{2,1,0:T(8,128)(2,1)S(1)} %get-tuple-element.46.refs_1_, bf16[2,64,384]{2,1,0:T(8,128)(2,1)S(1)} %collective-permute-done.7.refs_2_, ...), custom_call_target="tpu_custom_call" | custom-call | tf_op jit(solution)/shard_map/pallas_call | solution.py:27
  20.7 0.8 %collective-permute-start.8 = (bf16[2,64,384]{2,1,0:T(8,128)(2,1)S(1)}, bf16[2,64,384]{2,1,0:T(8,128)(2,1)S(1)}, u32[]{:S(2)}, u32[]{:S(2)}) collective-permute-start(bf16[2,64,384]{2,1,0:T(8,128)(2,1)S(1)} %get-tuple-element.49), channel_id=1, source_target_pairs={{0,8},{2,10},{4,12},{6,14},{8,0},{10,2},{12,4},{14,6},{16,24},{18,... | collective-permute-start | bytes 294920 | tf_op jit(solution)/shard_map/ppermute | solution.py:324
  21.4 2.1 %collective-permute-done.9.other = bf16[2,64,384]{2,1,0:T(8,128)(2,1)S(1)} collective-permute-done((bf16[2,64,384]{2,1,0:T(8,128)(2,1)S(1)}, bf16[2,64,384]{2,1,0:T(8,128)(2,1)S(1)}, u32[]{:S(2)}, u32[]{:S(2)}) %collective-permute-start.9) | collective-permute-done | bytes 98336 | tf_op jit(solution)/shard_map/ppermute | solution.py:324
  23.5 1.0 %shard_map.85._ = f32[2,64,1024]{2,1,0:T(8,128)} custom-call(bf16[2,64,384]{2,1,0:T(8,128)(2,1)S(1)} %get-tuple-element.40.refs_4_.high, bf16[2,64,384]{2,1,0:T(8,128)(2,1)S(1)} %get-tuple-element.50.low, bf16[2,64,384]{2,1,0:T(8,128)(2,1)S(1)} %collective-permute-done.9.other, bf16[2,64,192]{2,1,0:T(8,128)(2,1)S(1)} %get-tuple-element.41.refs_5_.m.refs_7_, ...), custom_call_target="tpu_custom_call" | custom-call | flops 2000000000 | tf_op jit(solution)/shard_map/pallas_call | solution.py:27
  24.5 0.0 collective-permute-done.6.other
  24.5 1.6 %collective-permute-done.8.got = bf16[2,64,384]{2,1,0:T(8,128)(2,1)S(1)} collective-permute-done((bf16[2,64,384]{2,1,0:T(8,128)(2,1)S(1)}, bf16[2,64,384]{2,1,0:T(8,128)(2,1)S(1)}, u32[]{:S(2)}, u32[]{:S(2)}) %collective-permute-start.8) | collective-permute-done | bytes 98336 | tf_op jit(solution)/shard_map/ppermute | solution.py:324
  26.1 0.8 %shard_map.86 = f32[2,64,1024]{2,1,0:T(8,128)} custom-call(f32[2,64,256]{2,1,0:T(8,128)S(1)} %shard_map.83.own, bf16[2,64,256]{2,1,0:T(8,128)(2,1)S(1)} %collective-permute-done.6.other, bf16[2,64,192]{2,1,0:T(8,128)(2,1)S(1)} %get-tuple-element.41.refs_5_.m.refs_7_, ...), custom_call_target="tpu_custom_call", output_to_operand_aliasing={{}: (6, {})} | custom-call | tf_op jit(solution)/shard_map/pallas_call | solution.py:27
  (2 shorter events, 0.0 us)
Async XLA Ops:
  0.0 1.0 %copy-start = (bf16[2,128,1024]{2,1,0:T(8,128)(2,1)S(1)}, bf16[2,128,1024]{2,1,0:T(8,128)(2,1)}, u32[]{:S(2)}) copy-start(bf16[2,128,1024]{2,1,0:T(8,128)(2,1)} %refs_0_.9) | copy-start | bytes 1572868
  1.2 6.3 %collective-permute-start.1 = (bf16[2,32,1024]{2,1,0:T(8,128)(2,1)S(1)}, bf16[2,32,1024]{2,1,0:T(8,128)(2,1)S(1)}, u32[]{:S(2)}, u32[]{:S(2)}) collective-permute-start(bf16[2,32,1024]{2,1,0:T(8,128)(2,1)S(1)} %get-tuple-element.28), channel_id=1, source_target_pairs={{0,8},{2,0},{4,2},{6,4},{8,6},{10,16},{12,10},{14,12},{16,14},{18,... | collective-permute-start | bytes 393224 | tf_op jit(solution)/shard_map/ppermute | solution.py:306
  4.3 3.2 %collective-permute-start = (bf16[2,32,1024]{2,1,0:T(8,128)(2,1)S(1)}, bf16[2,32,1024]{2,1,0:T(8,128)(2,1)S(1)}, u32[]{:S(2)}, u32[]{:S(2)}) collective-permute-start(bf16[2,32,1024]{2,1,0:T(8,128)(2,1)S(1)} %get-tuple-element.28), channel_id=1, source_target_pairs={{0,2},{2,0},{4,6},{6,4},{8,10},{10,8},{12,14},{14,12},{16,18},{18,... | collective-permute-start | bytes 393224 | tf_op jit(solution)/shard_map/ppermute | solution.py:304
  4.3 2.1 %copy-start.7 = (bf16[2,256]{1,0:T(2,128)(2,1)S(1)}, bf16[2,256]{1,0:T(2,128)(2,1)}, u32[]{:S(2)}) copy-start(bf16[2,256]{1,0:T(2,128)(2,1)} %taps_ref.1) | copy-start | bytes 3076
  4.3 8.4 %collective-permute-start.2 = (bf16[2,128,256]{2,1,0:T(8,128)(2,1)S(1)}, bf16[2,128,256]{2,1,0:T(8,128)(2,1)S(1)}, u32[]{:S(2)}, u32[]{:S(2)}) collective-permute-start(bf16[2,128,256]{2,1,0:T(8,128)(2,1)S(1)} %get-tuple-element.29), channel_id=1, source_target_pairs={{0,1},{1,0},{2,3},{3,2},{4,5},{5,4},{6,7},{7,6},{8,9},{9,8},{10,11... | collective-permute-start | bytes 393224 | tf_op jit(solution)/shard_map/ppermute | solution.py:307
  5.8 0.8 %copy-start.3 = (f32[2,2,128,8]{2,3,1,0:T(8,128)S(1)}, f32[2,2,128,8]{2,3,1,0:T(8,128)}, u32[]{:S(2)}) copy-start(f32[2,2,128,8]{2,3,1,0:T(8,128)} %param.11) | copy-start | bytes 49156
  5.8 0.8 %copy-start.4 = (s32[2,2,128]{2,1,0:T(2,128)S(1)}, s32[2,2,128]{2,1,0:T(2,128)}, u32[]{:S(2)}) copy-start(s32[2,2,128]{2,1,0:T(2,128)} %refs_0_.11) | copy-start | bytes 6148
  5.8 0.8 %copy-start.5 = (f32[2,2,128]{2,1,0:T(2,128)S(1)}, f32[2,2,128]{2,1,0:T(2,128)}, u32[]{:S(2)}) copy-start(f32[2,2,128]{2,1,0:T(2,128)} %refs_2_.5) | copy-start | bytes 6148
  5.8 0.8 %copy-start.6 = (f32[2,2,128]{2,1,0:T(2,128)S(1)}, f32[2,2,128]{2,1,0:T(2,128)}, u32[]{:S(2)}) copy-start(f32[2,2,128]{2,1,0:T(2,128)} %refs_3_.5) | copy-start | bytes 6148
  5.8 1.7 %copy-start.1 = (bf16[2,128,1024]{2,1,0:T(8,128)(2,1)S(1)}, bf16[2,128,1024]{2,1,0:T(8,128)(2,1)}, u32[]{:S(2)}) copy-start(bf16[2,128,1024]{2,1,0:T(8,128)(2,1)} %refs_0_.9) | copy-start | bytes 1572868
  5.8 6.8 %collective-permute-start.3 = (bf16[2,32,256]{2,1,0:T(8,128)(2,1)S(1)}, bf16[2,32,256]{2,1,0:T(8,128)(2,1)S(1)}, u32[]{:S(2)}, u32[]{:S(2)}) collective-permute-start(bf16[2,32,256]{2,1,0:T(8,128)(2,1)S(1)} %get-tuple-element.30), channel_id=1, source_target_pairs={{0,1},{1,3},{2,5},{3,0},{4,7},{5,2},{6,9},{7,4},{8,11},{9,6},{10,1... | collective-permute-start | bytes 98312 | tf_op jit(solution)/shard_map/ppermute | solution.py:309
  6.6 0.9 %copy-start.2 = (bf16[2,64,160]{2,1,0:T(8,128)(2,1)S(1)}, bf16[2,64,160]{2,1,0:T(8,128)(2,1)}, u32[]{:S(2)}) copy-start(bf16[2,64,160]{2,1,0:T(8,128)(2,1)} %refs_4_.5) | copy-start | bytes 122884
  8.2 5.8 %collective-permute-start.5 = (bf16[2,64,384]{2,1,0:T(8,128)(2,1)S(1)}, bf16[2,64,384]{2,1,0:T(8,128)(2,1)S(1)}, u32[]{:S(2)}, u32[]{:S(2)}) collective-permute-start(bf16[2,64,384]{2,1,0:T(8,128)(2,1)S(1)} %get-tuple-element.34.refs_7_.refs_0_), channel_id=1, source_target_pairs={{0,8},{2,10},{4,12},{6,14},{8,0},{10,2},{12,4},{14,6},{16,24},{18,... | collective-permute-start | bytes 294920 | tf_op jit(solution)/shard_map/ppermute | solution.py:324
  10.5 9.4 %collective-permute-start.7 = (bf16[2,64,384]{2,1,0:T(8,128)(2,1)S(1)}, bf16[2,64,384]{2,1,0:T(8,128)(2,1)S(1)}, u32[]{:S(2)}, u32[]{:S(2)}) collective-permute-start(bf16[2,64,384]{2,1,0:T(8,128)(2,1)S(1)} %get-tuple-element.35.refs_7_.refs_0_), channel_id=1, source_target_pairs={{0,16},{2,18},{4,20},{6,22},{8,24},{10,26},{12,28},{14,30},{16,0},... | collective-permute-start | bytes 294920 | tf_op jit(solution)/shard_map/ppermute | solution.py:324
  13.1 5.2 %collective-permute-start.4 = (bf16[2,64,256]{2,1,0:T(8,128)(2,1)S(1)}, bf16[2,64,256]{2,1,0:T(8,128)(2,1)S(1)}, u32[]{:S(2)}, u32[]{:S(2)}) collective-permute-start(bf16[2,64,256]{2,1,0:T(8,128)(2,1)S(1)} %get-tuple-element.36.refs_5_.refs_0_), channel_id=1, source_target_pairs={{0,8},{2,10},{4,12},{6,14},{8,0},{10,2},{12,4},{14,6},{16,24},{18,... | collective-permute-start | bytes 196616 | tf_op jit(solution)/shard_map/ppermute | solution.py:324
  14.3 9.2 %collective-permute-start.9 = (bf16[2,64,384]{2,1,0:T(8,128)(2,1)S(1)}, bf16[2,64,384]{2,1,0:T(8,128)(2,1)S(1)}, u32[]{:S(2)}, u32[]{:S(2)}) collective-permute-start(bf16[2,64,384]{2,1,0:T(8,128)(2,1)S(1)} %get-tuple-element.40.refs_4_.high), channel_id=1, source_target_pairs={{0,16},{2,18},{4,20},{6,22},{8,24},{10,26},{12,28},{14,30},{16,0},... | collective-permute-start | bytes 294920 | tf_op jit(solution)/shard_map/ppermute | solution.py:324
  18.5 6.0 %collective-permute-start.6 = (bf16[2,64,256]{2,1,0:T(8,128)(2,1)S(1)}, bf16[2,64,256]{2,1,0:T(8,128)(2,1)S(1)}, u32[]{:S(2)}, u32[]{:S(2)}) collective-permute-start(bf16[2,64,256]{2,1,0:T(8,128)(2,1)S(1)} %get-tuple-element.43.high.refs_9_), channel_id=1, source_target_pairs={{0,16},{2,18},{4,20},{6,22},{8,24},{10,26},{12,28},{14,30},{16,0},... | collective-permute-start | bytes 196616 | tf_op jit(solution)/shard_map/ppermute | solution.py:324
  20.7 5.4 %collective-permute-start.8 = (bf16[2,64,384]{2,1,0:T(8,128)(2,1)S(1)}, bf16[2,64,384]{2,1,0:T(8,128)(2,1)S(1)}, u32[]{:S(2)}, u32[]{:S(2)}) collective-permute-start(bf16[2,64,384]{2,1,0:T(8,128)(2,1)S(1)} %get-tuple-element.49), channel_id=1, source_target_pairs={{0,8},{2,10},{4,12},{6,14},{8,0},{10,2},{12,4},{14,6},{16,24},{18,... | collective-permute-start | bytes 294920 | tf_op jit(solution)/shard_map/ppermute | solution.py:324

commit v8 on v7

--- a/solution.py
+++ b/solution.py
@@ -148,7 +148,7 @@
             side_table(0, q, start, first_bin, total, operands, turned, m_ref.at[0], e_ref.at[0])
 
 
-def focus_kernel(first, cuts, raw, near, far, w, steering, *refs):
+def focus_kernel(first, cuts, raw, far, near, w, steering, *refs):
     x = refs[-1]
     pulses, guards = raw.shape[1], near.shape[1]
     width = w.shape[1] // 2
@@ -251,12 +251,10 @@
     out[0], out[1] = turned_term(first, 0, (high, low), m, e)
 
 
-def both_terms_kernel(first, high, low, over, m0, e0, mx, ex, m1, e1, out, sent):
-    given = ((high, low), (over,))
-    for m, e, at, ref in ((m0, e0, first, out), (mx, ex, 0, sent)):
-        own, other = [split_parts(turned_term(at, 0, parts, m, e)) for parts in given]
-        for part, value in enumerate(turned_sum(first, own, other, m1, e1)):
-            ref[part] = value.astype(ref.dtype)
+def both_terms_kernel(first, place, high, low, over, m0, e0, m1, e1, out):
+    own, other = [split_parts(turned_term(place, 0, parts, m0, e0)) for parts in ((high, low), (over,))]
+    for part, value in enumerate(turned_sum(first, own, other, m1, e1)):
+        out[part] = value.astype(out.dtype)
 
 
 def end_image_kernel(first, first_out, own, other, m, e, out, got, _, image, held, held_out, sem):
@@ -328,7 +326,7 @@
         return call(
             functools.partial(focus_kernel, first, cuts),
             [sds((2, beams, size), bf16) for size in cuts for _ in range(2)],
-            [raw, near, far, w, steering, *more],
+            [raw, far, near, w, steering, *more],
             scratch=[pltpu.VMEM(((blocks + 1) * rows, 2 * width), bf16)],
             flops=flops,
             after=[after],
@@ -371,18 +369,23 @@
     cross = tables(functools.partial(cross_table_kernel, level, middle, bins), 1, last - middle, [second[0]])
     last_second = first_merge(last, last_sub, last_other, [last_tables[0], cross[0]], WAIT)
     last_third = partner(last_second[0], level + 1)
-    out, sent = call(
-        functools.partial(both_terms_kernel, middle),
-        [sds((2, beams, last - middle), f32), sds((2, beams, last - middle), bf16)],
-        [*crossing, over, *first_tables, *cross, *last_tables],
-        after=[last_second[0]],
-    )
+    def both_terms(place, used, dtype, after):
+        return call(
+            functools.partial(both_terms_kernel, middle, place),
+            sds((2, beams, last - middle), dtype),
+            [*crossing, over, *used, *last_tables],
+            after=[after],
+        )
+
+    sent = both_terms(0, cross, bf16, last_second[0])
     got = partner(sent, level)
+    out = both_terms(middle, first_tables, f32, sent)
     image = write(functools.partial(start_image_kernel, 0), [middle], [*second, third, *last_tables])
     own = call(
         functools.partial(own_term_kernel, last),
         sds((2, beams, width), f32),
         [*last_second, *last_tables],
+        after=[sent],
     )
     return write(
         functools.partial(end_image_kernel, last, middle),

time: 27.1 us -> 26.6 us (0.982)
  waiting for transfers between devices: 3.96 us -> 3.32 us
    ppermute x6, waiting for transfers between devices: 3.95 us -> 3.31 us  [partner(): lax.ppermute(value, 'aperture', [(d, d ^ 1 << bit) for d in range(count)])]
    pallas_call x14 -> x15, Pallas kernels: 7.26 us -> 7.41 us  [call(): pl.pallas_call(body, out_shape=outs, in_specs=in_specs or [whole] * len(a...]
  transfers between devices with their start and end apart: 10 -> 10, of which waited for: 3 -> 3; matrix products, arithmetic and copies ran while one was open for 0% -> 0% of each run, Pallas kernels for 23% -> 24%
where the time goes in v8:
time: 26.6 us; the launch traced here: 26.4 us
  starting transfers between devices  14.4 us (54%)
  Pallas kernels  7.41 us (28%)
  waiting for transfers between devices  3.32 us (12%)
  local copies, waits for them, and re-layouts  1.07 us (4%)
    ppermute x6, starting transfers between devices, partner(): lax.ppermute(value, 'aperture', [(d, d ^ 1 << bit) for d in range(count)])  9.27 us
    pallas_call x15, Pallas kernels, call(): pl.pallas_call(body, out_shape=outs, in_specs=in_specs or [whole] * len(a...  7.41 us
    ppermute x6, waiting for transfers between devices, partner(): lax.ppermute(value, 'aperture', [(d, d ^ 1 << bit) for d in range(count)])  3.31 us
    ppermute x1, starting transfers between devices, shards(): lax.ppermute(guard, 'aperture', completed([(d, d - 1) for d in range(2, c...  3.08 us
    ppermute x1, starting transfers between devices, shards(): lax.ppermute(rim, 'tile', completed([(t, t - 1) for t in range(1, tiles)]...  1.52 us
    unnamed x16, local copies, waits for them, and re-layouts  1.07 us
    ppermute x1, starting transfers between devices, shards(): lax.ppermute(corner, ('aperture', 'tile'), completed(steps, count * tiles))  0.56 us
  transfers between devices with their start and end apart: 10, of which 3 were waited for; matrix products, arithmetic and copies ran while one was open for 0% of the time, Pallas kernels for 24%

profile of v8, /device:TPU:0, one launch (start us, length us, event | category | flops | bytes accessed | tf_op | source)
XLA Modules:
  0.0 26.4 jit_solution(7250397949535259011)
XLA Ops:
  0.0 0.0 copy-start
  0.0 1.0 %copy-done = bf16[2,128,1024]{2,1,0:T(8,128)(2,1)S(1)} copy-done((bf16[2,128,1024]{2,1,0:T(8,128)(2,1)S(1)}, bf16[2,128,1024]{2,1,0:T(8,128)(2,1)}, u32[]{:S(2)}) %copy-start) | copy-done | bytes 524312
  1.0 0.1 shard_map.73
  1.2 3.1 %collective-permute-start = (bf16[2,32,1024]{2,1,0:T(8,128)(2,1)S(1)}, bf16[2,32,1024]{2,1,0:T(8,128)(2,1)S(1)}, u32[]{:S(2)}, u32[]{:S(2)}) collective-permute-start(bf16[2,32,1024]{2,1,0:T(8,128)(2,1)S(1)} %get-tuple-element.26), channel_id=1, source_target_pairs={{0,8},{2,0},{4,2},{6,4},{8,6},{10,16},{12,10},{14,12},{16,14},{18,... | collective-permute-start | bytes 393224 | tf_op jit(solution)/shard_map/ppermute | solution.py:304
  4.3 0.0 collective-permute-start.1
  4.3 0.0 copy-start.7
  4.3 1.5 %collective-permute-start.2 = (bf16[2,128,256]{2,1,0:T(8,128)(2,1)S(1)}, bf16[2,128,256]{2,1,0:T(8,128)(2,1)S(1)}, u32[]{:S(2)}, u32[]{:S(2)}) collective-permute-start(bf16[2,128,256]{2,1,0:T(8,128)(2,1)S(1)} %get-tuple-element.27), channel_id=1, source_target_pairs={{0,1},{1,0},{2,3},{3,2},{4,5},{5,4},{6,7},{7,6},{8,9},{9,8},{10,11... | collective-permute-start | bytes 393224 | tf_op jit(solution)/shard_map/ppermute | solution.py:305
  5.8 0.0 copy-start.3
  5.8 0.0 copy-start.1
  5.8 0.6 %collective-permute-start.3 = (bf16[2,32,256]{2,1,0:T(8,128)(2,1)S(1)}, bf16[2,32,256]{2,1,0:T(8,128)(2,1)S(1)}, u32[]{:S(2)}, u32[]{:S(2)}) collective-permute-start(bf16[2,32,256]{2,1,0:T(8,128)(2,1)S(1)} %get-tuple-element.28), channel_id=1, source_target_pairs={{0,1},{1,3},{2,5},{3,0},{4,7},{5,2},{6,9},{7,4},{8,11},{9,6},{10,1... | collective-permute-start | bytes 98312 | tf_op jit(solution)/shard_map/ppermute | solution.py:307
  6.4 0.0 copy-done.7
  6.4 0.2 shard_map.74.refs_3_
  6.6 0.0 copy-start.2
  6.6 0.0 copy-done.3
  6.6 0.0 copy-done.4
  6.6 0.0 copy-done.5
  6.6 0.0 copy-done.6
  6.6 0.8 %shard_map.75 = (bf16[2,64,192]{2,1,0:T(8,128)(2,1)S(1)}, f32[2,2,64,1024]{3,2,1,0:T(8,128)S(1)}) custom-call(s32[2,2,128]{2,1,0:T(2,128)S(1)} %copy-done.4, f32[2,2,8,128]{3,2,1,0:T(8,128)S(1)} %bitcast.1, f32[2,2,128]{2,1,0:T(2,128)S(1)} %copy-done.5, f32[2,2,128]{2,1,0:T(2,128)S(1)} %copy-done.6), custom_call_target="tpu_custom_call" | custom-call | flops 20000000 | tf_op jit(solution)/shard_map/pallas_call | solution.py:27
  7.5 0.0 collective-permute-done.refs_1_
  7.5 0.0 collective-permute-done.1.refs_2_
  7.5 0.0 copy-done.1
  7.5 0.0 copy-done.2
  7.5 0.7 %shard_map.76 = (bf16[2,64,384]{2,1,0:T(8,128)(2,1)S(1)}, bf16[2,64,384]{2,1,0:T(8,128)(2,1)S(1)}, bf16[2,64,128]{2,1,0:T(8,128)(2,1)S(1)}, bf16[2,64,128]{2,1,0:T(8,128)(2,1)S(1)}) custom-call(bf16[2,128,1024]{2,1,0:T(8,128)(2,1)S(1)} %copy-done.1, bf16[2,32,1024]{2,1,0:T(8,128)(2,1)S(1)} %collective-permute-done.refs_1_, ...), custom_call_target="tpu_custom_call" | custom-call | tf_op jit(solution)/shard_map/pallas_call | solution.py:27
  8.2 1.8 %collective-permute-start.5 = (bf16[2,64,384]{2,1,0:T(8,128)(2,1)S(1)}, bf16[2,64,384]{2,1,0:T(8,128)(2,1)S(1)}, u32[]{:S(2)}, u32[]{:S(2)}) collective-permute-start(bf16[2,64,384]{2,1,0:T(8,128)(2,1)S(1)} %get-tuple-element.32.refs_7_.refs_0_), channel_id=1, source_target_pairs={{0,8},{2,10},{4,12},{6,14},{8,0},{10,2},{12,4},{14,6},{16,24},{18,... | collective-permute-start | bytes 294920 | tf_op jit(solution)/shard_map/ppermute | solution.py:322
  10.0 0.5 %shard_map.77 = (bf16[2,64,384]{2,1,0:T(8,128)(2,1)S(1)}, bf16[2,64,384]{2,1,0:T(8,128)(2,1)S(1)}) custom-call(bf16[2,128,1024]{2,1,0:T(8,128)(2,1)S(1)} %copy-done.1, bf16[2,32,1024]{2,1,0:T(8,128)(2,1)S(1)} %collective-permute-done.refs_1_, bf16[2,32,1024]{2,1,0:T(8,128)(2,1)S(1)} %collective-permute-done.1.refs_2_, ...), custom_call_target="tpu_custom_call" | custom-call | tf_op jit(solution)/shard_map/pallas_call | solution.py:27
  10.5 2.1 %collective-permute-start.6 = (bf16[2,64,384]{2,1,0:T(8,128)(2,1)S(1)}, bf16[2,64,384]{2,1,0:T(8,128)(2,1)S(1)}, u32[]{:S(2)}, u32[]{:S(2)}) collective-permute-start(bf16[2,64,384]{2,1,0:T(8,128)(2,1)S(1)} %get-tuple-element.33.refs_7_.refs_0_), channel_id=1, source_target_pairs={{0,16},{2,18},{4,20},{6,22},{8,24},{10,26},{12,28},{14,30},{16,0},... | collective-permute-start | bytes 294920 | tf_op jit(solution)/shard_map/ppermute | solution.py:322
  12.6 0.0 collective-permute-done.3.refs_6_
  12.6 0.0 collective-permute-done.2.refs_5_
  12.6 0.5 %shard_map.78 = (bf16[2,64,256]{2,1,0:T(8,128)(2,1)S(1)}, bf16[2,64,256]{2,1,0:T(8,128)(2,1)S(1)}) custom-call(bf16[2,128,1024]{2,1,0:T(8,128)(2,1)S(1)} %copy-done.1, bf16[2,32,1024]{2,1,0:T(8,128)(2,1)S(1)} %collective-permute-done.refs_1_, bf16[2,32,1024]{2,1,0:T(8,128)(2,1)S(1)} %collective-permute-done.1.refs_2_, ...), custom_call_target="tpu_custom_call" | custom-call | flops 2000000000 | tf_op jit(solution)/shard_map/pallas_call | solution.py:27
  13.1 0.9 %collective-permute-start.4 = (bf16[2,64,256]{2,1,0:T(8,128)(2,1)S(1)}, bf16[2,64,256]{2,1,0:T(8,128)(2,1)S(1)}, u32[]{:S(2)}, u32[]{:S(2)}) collective-permute-start(bf16[2,64,256]{2,1,0:T(8,128)(2,1)S(1)} %get-tuple-element.34.refs_5_.refs_0_), channel_id=1, source_target_pairs={{0,8},{2,10},{4,12},{6,14},{8,0},{10,2},{12,4},{14,6},{16,24},{18,... | collective-permute-start | bytes 196616 | tf_op jit(solution)/shard_map/ppermute | solution.py:322
  14.0 0.0 collective-permute-done.5.refs_2_
  14.0 0.3 %shard_map.79 = (bf16[2,64,384]{2,1,0:T(8,128)(2,1)S(1)}, bf16[2,64,384]{2,1,0:T(8,128)(2,1)S(1)}) custom-call(bf16[2,64,384]{2,1,0:T(8,128)(2,1)S(1)} %get-tuple-element.32.refs_7_.refs_0_, bf16[2,64,384]{2,1,0:T(8,128)(2,1)S(1)} %get-tuple-element.37.refs_1_, bf16[2,64,384]{2,1,0:T(8,128)(2,1)S(1)} %collective-permute-done.5.refs_2_, ...), custom_call_target="tpu_custom_call" | custom-call | flops 2000000000 | tf_op jit(solution)/shard_map/pallas_call | solution.py:27
  14.3 2.5 %collective-permute-start.9 = (bf16[2,64,384]{2,1,0:T(8,128)(2,1)S(1)}, bf16[2,64,384]{2,1,0:T(8,128)(2,1)S(1)}, u32[]{:S(2)}, u32[]{:S(2)}) collective-permute-start(bf16[2,64,384]{2,1,0:T(8,128)(2,1)S(1)} %get-tuple-element.38.refs_4_.high), channel_id=1, source_target_pairs={{0,16},{2,18},{4,20},{6,22},{8,24},{10,26},{12,28},{14,30},{16,0},... | collective-permute-start | bytes 294920 | tf_op jit(solution)/shard_map/ppermute | solution.py:322
  16.8 0.8 %shard_map.80 = (bf16[2,64,192]{2,1,0:T(8,128)(2,1)S(1)}, f32[2,2,64,1024]{3,2,1,0:T(8,128)S(1)}) custom-call(s32[2,2,128]{2,1,0:T(2,128)S(1)} %copy-done.4, f32[2,2,8,128]{3,2,1,0:T(8,128)S(1)} %bitcast.2, f32[2,2,128]{2,1,0:T(2,128)S(1)} %copy-done.5, f32[2,2,128]{2,1,0:T(2,128)S(1)} %copy-done.6, bf16[2,64,384]{2,1,0:T(8,128)(2,1)S(1)} %get-tuple-element.38.refs_4_.high), custom_call_target="tpu_custom_call" | custom-call | flops 20000000 | tf_op jit(solution)/shard_map/pallas_call | solution.py:27
  17.7 0.4 %shard_map.81 = (bf16[1,64,192]{2,1,0:T(8,128)(2,1)S(1)}, f32[1,2,64,384]{3,2,1,0:T(8,128)S(1)}) custom-call(s32[2,2,128]{2,1,0:T(2,128)S(1)} %copy-done.4, f32[2,2,8,128]{3,2,1,0:T(8,128)S(1)} %bitcast.3, f32[2,2,128]{2,1,0:T(2,128)S(1)} %copy-done.5, f32[2,2,128]{2,1,0:T(2,128)S(1)} %copy-done.6, bf16[2,64,384]{2,1,0:T(8,128)(2,1)S(1)} %get-tuple-element.38.refs_4_.high), custom_call_target="tpu_custom_call" | custom-call | flops 20000000 | tf_op jit(solution)/shard_map/pallas_call | solution.py:27
  18.0 0.3 %collective-permute-done.4.refs_2_ = bf16[2,64,256]{2,1,0:T(8,128)(2,1)S(1)} collective-permute-done((bf16[2,64,256]{2,1,0:T(8,128)(2,1)S(1)}, bf16[2,64,256]{2,1,0:T(8,128)(2,1)S(1)}, u32[]{:S(2)}, u32[]{:S(2)}) %collective-permute-start.4) | collective-permute-done | bytes 65568 | tf_op jit(solution)/shard_map/ppermute | solution.py:322
  18.3 0.2 shard_map.82
  18.5 1.2 %collective-permute-start.7 = (bf16[2,64,256]{2,1,0:T(8,128)(2,1)S(1)}, bf16[2,64,256]{2,1,0:T(8,128)(2,1)S(1)}, u32[]{:S(2)}, u32[]{:S(2)}) collective-permute-start(bf16[2,64,256]{2,1,0:T(8,128)(2,1)S(1)} %get-tuple-element.41.refs_7_.refs_0_), channel_id=1, source_target_pairs={{0,16},{2,18},{4,20},{6,22},{8,24},{10,26},{12,28},{14,30},{16,0},... | collective-permute-start | bytes 196616 | tf_op jit(solution)/shard_map/ppermute | solution.py:322
  19.7 0.0 collective-permute-done.6.refs_2_
  19.7 0.5 %shard_map.83.refs_4_.refs_7_ = bf16[2,64,384]{2,1,0:T(8,128)(2,1)S(1)} custom-call(bf16[2,64,384]{2,1,0:T(8,128)(2,1)S(1)} %get-tuple-element.33.refs_7_.refs_0_, bf16[2,64,384]{2,1,0:T(8,128)(2,1)S(1)} %get-tuple-element.44.refs_1_, bf16[2,64,384]{2,1,0:T(8,128)(2,1)S(1)} %collective-permute-done.6.refs_2_, ...), custom_call_target="tpu_custom_call" | custom-call | tf_op jit(solution)/shard_map/pallas_call | solution.py:27
  20.2 0.8 %collective-permute-start.8 = (bf16[2,64,384]{2,1,0:T(8,128)(2,1)S(1)}, bf16[2,64,384]{2,1,0:T(8,128)(2,1)S(1)}, u32[]{:S(2)}, u32[]{:S(2)}) collective-permute-start(bf16[2,64,384]{2,1,0:T(8,128)(2,1)S(1)} %shard_map.83.refs_4_.refs_7_), channel_id=1, source_target_pairs={{0,8},{2,10},{4,12},{6,14},{8,0},{10,2},{12,4},{14,6},{16,24},{18,... | collective-permute-start | bytes 294920 | tf_op jit(solution)/shard_map/ppermute | solution.py:322
  20.9 0.2 shard_map.84.own
  21.1 0.5 %shard_map.85.out = f32[2,64,384]{2,1,0:T(8,128)S(1)} custom-call(bf16[2,64,384]{2,1,0:T(8,128)(2,1)S(1)} %get-tuple-element.33.refs_7_.refs_0_, bf16[2,64,384]{2,1,0:T(8,128)(2,1)S(1)} %get-tuple-element.44.refs_1_, bf16[2,64,384]{2,1,0:T(8,128)(2,1)S(1)} %collective-permute-done.6.refs_2_, bf16[2,64,192]{2,1,0:T(8,128)(2,1)S(1)} %get-tuple-element.29.refs_5_.refs_3_, ...), custom_call_target="tpu_custom_call" | custom-call | tf_op jit(solution)/shard_map/pallas_call | solution.py:27
  21.6 2.0 %collective-permute-done.9.other = bf16[2,64,384]{2,1,0:T(8,128)(2,1)S(1)} collective-permute-done((bf16[2,64,384]{2,1,0:T(8,128)(2,1)S(1)}, bf16[2,64,384]{2,1,0:T(8,128)(2,1)S(1)}, u32[]{:S(2)}, u32[]{:S(2)}) %collective-permute-start.9) | collective-permute-done | bytes 98336 | tf_op jit(solution)/shard_map/ppermute | solution.py:322
  23.5 1.0 %shard_map.86._ = f32[2,64,1024]{2,1,0:T(8,128)} custom-call(bf16[2,64,384]{2,1,0:T(8,128)(2,1)S(1)} %get-tuple-element.38.refs_4_.high, bf16[2,64,384]{2,1,0:T(8,128)(2,1)S(1)} %get-tuple-element.46.low, bf16[2,64,384]{2,1,0:T(8,128)(2,1)S(1)} %collective-permute-done.9.other, bf16[2,64,192]{2,1,0:T(8,128)(2,1)S(1)} %get-tuple-element.39.refs_5_.refs_2_.m, ...), custom_call_target="tpu_custom_call" | custom-call | flops 2000000000 | tf_op jit(solution)/shard_map/pallas_call | solution.py:27
  24.5 0.0 collective-permute-done.7.other
  24.5 1.1 %collective-permute-done.8.got = bf16[2,64,384]{2,1,0:T(8,128)(2,1)S(1)} collective-permute-done((bf16[2,64,384]{2,1,0:T(8,128)(2,1)S(1)}, bf16[2,64,384]{2,1,0:T(8,128)(2,1)S(1)}, u32[]{:S(2)}, u32[]{:S(2)}) %collective-permute-start.8) | collective-permute-done | bytes 98336 | tf_op jit(solution)/shard_map/ppermute | solution.py:322
  25.6 0.8 %shard_map.87 = f32[2,64,1024]{2,1,0:T(8,128)} custom-call(f32[2,64,256]{2,1,0:T(8,128)S(1)} %shard_map.84.own, bf16[2,64,256]{2,1,0:T(8,128)(2,1)S(1)} %collective-permute-done.7.other, bf16[2,64,192]{2,1,0:T(8,128)(2,1)S(1)} %get-tuple-element.39.refs_5_.refs_2_.m, ...), custom_call_target="tpu_custom_call", output_to_operand_aliasing={{}: (6, {})} | custom-call | tf_op jit(solution)/shard_map/pallas_call | solution.py:27
  (3 shorter events, 0.0 us)
Async XLA Ops:
  0.0 1.0 %copy-start = (bf16[2,128,1024]{2,1,0:T(8,128)(2,1)S(1)}, bf16[2,128,1024]{2,1,0:T(8,128)(2,1)}, u32[]{:S(2)}) copy-start(bf16[2,128,1024]{2,1,0:T(8,128)(2,1)} %refs_0_.9) | copy-start | bytes 1572868
  1.2 6.3 %collective-permute-start = (bf16[2,32,1024]{2,1,0:T(8,128)(2,1)S(1)}, bf16[2,32,1024]{2,1,0:T(8,128)(2,1)S(1)}, u32[]{:S(2)}, u32[]{:S(2)}) collective-permute-start(bf16[2,32,1024]{2,1,0:T(8,128)(2,1)S(1)} %get-tuple-element.26), channel_id=1, source_target_pairs={{0,8},{2,0},{4,2},{6,4},{8,6},{10,16},{12,10},{14,12},{16,14},{18,... | collective-permute-start | bytes 393224 | tf_op jit(solution)/shard_map/ppermute | solution.py:304
  4.3 3.2 %collective-permute-start.1 = (bf16[2,32,1024]{2,1,0:T(8,128)(2,1)S(1)}, bf16[2,32,1024]{2,1,0:T(8,128)(2,1)S(1)}, u32[]{:S(2)}, u32[]{:S(2)}) collective-permute-start(bf16[2,32,1024]{2,1,0:T(8,128)(2,1)S(1)} %get-tuple-element.26), channel_id=1, source_target_pairs={{0,2},{2,0},{4,6},{6,4},{8,10},{10,8},{12,14},{14,12},{16,18},{18,... | collective-permute-start | bytes 393224 | tf_op jit(solution)/shard_map/ppermute | solution.py:302
  4.3 2.1 %copy-start.7 = (bf16[2,256]{1,0:T(2,128)(2,1)S(1)}, bf16[2,256]{1,0:T(2,128)(2,1)}, u32[]{:S(2)}) copy-start(bf16[2,256]{1,0:T(2,128)(2,1)} %taps_ref.1) | copy-start | bytes 3076
  4.3 8.4 %collective-permute-start.2 = (bf16[2,128,256]{2,1,0:T(8,128)(2,1)S(1)}, bf16[2,128,256]{2,1,0:T(8,128)(2,1)S(1)}, u32[]{:S(2)}, u32[]{:S(2)}) collective-permute-start(bf16[2,128,256]{2,1,0:T(8,128)(2,1)S(1)} %get-tuple-element.27), channel_id=1, source_target_pairs={{0,1},{1,0},{2,3},{3,2},{4,5},{5,4},{6,7},{7,6},{8,9},{9,8},{10,11... | collective-permute-start | bytes 393224 | tf_op jit(solution)/shard_map/ppermute | solution.py:305
  5.8 0.8 %copy-start.3 = (f32[2,2,128,8]{2,3,1,0:T(8,128)S(1)}, f32[2,2,128,8]{2,3,1,0:T(8,128)}, u32[]{:S(2)}) copy-start(f32[2,2,128,8]{2,3,1,0:T(8,128)} %param.11) | copy-start | bytes 49156
  5.8 0.8 %copy-start.4 = (s32[2,2,128]{2,1,0:T(2,128)S(1)}, s32[2,2,128]{2,1,0:T(2,128)}, u32[]{:S(2)}) copy-start(s32[2,2,128]{2,1,0:T(2,128)} %refs_0_.11) | copy-start | bytes 6148
  5.8 0.8 %copy-start.5 = (f32[2,2,128]{2,1,0:T(2,128)S(1)}, f32[2,2,128]{2,1,0:T(2,128)}, u32[]{:S(2)}) copy-start(f32[2,2,128]{2,1,0:T(2,128)} %refs_2_.5) | copy-start | bytes 6148
  5.8 0.8 %copy-start.6 = (f32[2,2,128]{2,1,0:T(2,128)S(1)}, f32[2,2,128]{2,1,0:T(2,128)}, u32[]{:S(2)}) copy-start(f32[2,2,128]{2,1,0:T(2,128)} %refs_3_.5) | copy-start | bytes 6148
  5.8 1.7 %copy-start.1 = (bf16[2,128,1024]{2,1,0:T(8,128)(2,1)S(1)}, bf16[2,128,1024]{2,1,0:T(8,128)(2,1)}, u32[]{:S(2)}) copy-start(bf16[2,128,1024]{2,1,0:T(8,128)(2,1)} %refs_0_.9) | copy-start | bytes 1572868
  5.8 6.8 %collective-permute-start.3 = (bf16[2,32,256]{2,1,0:T(8,128)(2,1)S(1)}, bf16[2,32,256]{2,1,0:T(8,128)(2,1)S(1)}, u32[]{:S(2)}, u32[]{:S(2)}) collective-permute-start(bf16[2,32,256]{2,1,0:T(8,128)(2,1)S(1)} %get-tuple-element.28), channel_id=1, source_target_pairs={{0,1},{1,3},{2,5},{3,0},{4,7},{5,2},{6,9},{7,4},{8,11},{9,6},{10,1... | collective-permute-start | bytes 98312 | tf_op jit(solution)/shard_map/ppermute | solution.py:307
  6.6 0.9 %copy-start.2 = (bf16[2,64,160]{2,1,0:T(8,128)(2,1)S(1)}, bf16[2,64,160]{2,1,0:T(8,128)(2,1)}, u32[]{:S(2)}) copy-start(bf16[2,64,160]{2,1,0:T(8,128)(2,1)} %refs_4_.5) | copy-start | bytes 122884
  8.2 5.8 %collective-permute-start.5 = (bf16[2,64,384]{2,1,0:T(8,128)(2,1)S(1)}, bf16[2,64,384]{2,1,0:T(8,128)(2,1)S(1)}, u32[]{:S(2)}, u32[]{:S(2)}) collective-permute-start(bf16[2,64,384]{2,1,0:T(8,128)(2,1)S(1)} %get-tuple-element.32.refs_7_.refs_0_), channel_id=1, source_target_pairs={{0,8},{2,10},{4,12},{6,14},{8,0},{10,2},{12,4},{14,6},{16,24},{18,... | collective-permute-start | bytes 294920 | tf_op jit(solution)/shard_map/ppermute | solution.py:322
  10.5 9.2 %collective-permute-start.6 = (bf16[2,64,384]{2,1,0:T(8,128)(2,1)S(1)}, bf16[2,64,384]{2,1,0:T(8,128)(2,1)S(1)}, u32[]{:S(2)}, u32[]{:S(2)}) collective-permute-start(bf16[2,64,384]{2,1,0:T(8,128)(2,1)S(1)} %get-tuple-element.33.refs_7_.refs_0_), channel_id=1, source_target_pairs={{0,16},{2,18},{4,20},{6,22},{8,24},{10,26},{12,28},{14,30},{16,0},... | collective-permute-start | bytes 294920 | tf_op jit(solution)/shard_map/ppermute | solution.py:322
  13.1 5.2 %collective-permute-start.4 = (bf16[2,64,256]{2,1,0:T(8,128)(2,1)S(1)}, bf16[2,64,256]{2,1,0:T(8,128)(2,1)S(1)}, u32[]{:S(2)}, u32[]{:S(2)}) collective-permute-start(bf16[2,64,256]{2,1,0:T(8,128)(2,1)S(1)} %get-tuple-element.34.refs_5_.refs_0_), channel_id=1, source_target_pairs={{0,8},{2,10},{4,12},{6,14},{8,0},{10,2},{12,4},{14,6},{16,24},{18,... | collective-permute-start | bytes 196616 | tf_op jit(solution)/shard_map/ppermute | solution.py:322
  14.3 9.2 %collective-permute-start.9 = (bf16[2,64,384]{2,1,0:T(8,128)(2,1)S(1)}, bf16[2,64,384]{2,1,0:T(8,128)(2,1)S(1)}, u32[]{:S(2)}, u32[]{:S(2)}) collective-permute-start(bf16[2,64,384]{2,1,0:T(8,128)(2,1)S(1)} %get-tuple-element.38.refs_4_.high), channel_id=1, source_target_pairs={{0,16},{2,18},{4,20},{6,22},{8,24},{10,26},{12,28},{14,30},{16,0},... | collective-permute-start | bytes 294920 | tf_op jit(solution)/shard_map/ppermute | solution.py:322
  18.5 6.0 %collective-permute-start.7 = (bf16[2,64,256]{2,1,0:T(8,128)(2,1)S(1)}, bf16[2,64,256]{2,1,0:T(8,128)(2,1)S(1)}, u32[]{:S(2)}, u32[]{:S(2)}) collective-permute-start(bf16[2,64,256]{2,1,0:T(8,128)(2,1)S(1)} %get-tuple-element.41.refs_7_.refs_0_), channel_id=1, source_target_pairs={{0,16},{2,18},{4,20},{6,22},{8,24},{10,26},{12,28},{14,30},{16,0},... | collective-permute-start | bytes 196616 | tf_op jit(solution)/shard_map/ppermute | solution.py:322
  20.2 5.4 %collective-permute-start.8 = (bf16[2,64,384]{2,1,0:T(8,128)(2,1)S(1)}, bf16[2,64,384]{2,1,0:T(8,128)(2,1)S(1)}, u32[]{:S(2)}, u32[]{:S(2)}) collective-permute-start(bf16[2,64,384]{2,1,0:T(8,128)(2,1)S(1)} %shard_map.83.refs_4_.refs_7_), channel_id=1, source_target_pairs={{0,8},{2,10},{4,12},{6,14},{8,0},{10,2},{12,4},{14,6},{16,24},{18,... | collective-permute-start | bytes 294920 | tf_op jit(solution)/shard_map/ppermute | solution.py:322

commit v9 on v8

--- a/solution.py
+++ b/solution.py
@@ -56,8 +56,9 @@
 def toeplitz_kernel(taps_ref, w_ref):
     count = taps_ref.shape[1]
     halves = []
+    taps = taps_ref[...].astype(jnp.float32)
     for part in range(2):
-        row = taps_ref[part : part + 1, :].astype(jnp.float32)
+        row = taps[part : part + 1, :]
         row = jnp.concatenate([row, jnp.zeros_like(row)], 1)
         rows = jnp.broadcast_to(row, (count, 2 * count))
         rolled = pltpu.roll(rows, 0, 1, stride=1, stride_axis=0)
@@ -257,12 +258,15 @@
         out[part] = value.astype(out.dtype)
 
 
-def end_image_kernel(first, first_out, own, other, m, e, out, got, _, image, held, held_out, sem):
+def next_image_kernel(first, own, other, m, e, _, image, held, sem):
+    term = turned_term(first, 1, (other,), m, e)
+    for copy in write_image((own[0] + term[0], own[1] + term[1]), first, image, held, sem):
+        copy.wait()
+
+
+def end_image_kernel(first, out, got, _, image, held, sem):
     values = [out[part] + got[part].astype(jnp.float32) for part in range(2)]
-    copies = write_image(values, first_out, image, held_out, sem.at[2:4])
-    term = turned_term(first, 1, (other,), m, e)
-    copies += write_image((own[0] + term[0], own[1] + term[1]), first, image, held, sem)
-    for copy in copies:
+    for copy in write_image(values, first, image, held, sem):
         copy.wait()
 
 
@@ -342,13 +346,13 @@
             after=after,
         )
 
-    def write(body, sizes, args, image=None):
+    def write(body, size, args, image=None):
         given = [] if image is None else [image]
         return call(
             body,
             sds((2, beams, bins), f32),
             [*args, *given],
-            scratch=[*[pltpu.VMEM((2, beams, size), f32) for size in sizes], pltpu.SemaphoreType.DMA((4,))],
+            scratch=[pltpu.VMEM((2, beams, size), f32), pltpu.SemaphoreType.DMA((2,))],
             aliases={len(args): 0} if given else {},
             in_specs=[whole] * len(args) + [anywhere] * len(given),
             out_specs=anywhere,
@@ -380,19 +384,17 @@
     sent = both_terms(0, cross, bf16, last_second[0])
     got = partner(sent, level)
     out = both_terms(middle, first_tables, f32, sent)
-    image = write(functools.partial(start_image_kernel, 0), [middle], [*second, third, *last_tables])
+    image = write(functools.partial(start_image_kernel, 0), middle, [*second, third, *last_tables])
     own = call(
         functools.partial(own_term_kernel, last),
         sds((2, beams, width), f32),
         [*last_second, *last_tables],
         after=[sent],
     )
-    return write(
-        functools.partial(end_image_kernel, last, middle),
-        [width, last - middle],
-        [own, last_third, *last_tables, out, got],
-        image,
+    image = write(
+        functools.partial(next_image_kernel, last), width, [own, last_third, *last_tables], image
     )
+    return write(functools.partial(end_image_kernel, middle), last - middle, [out, got], image)
 
 
 def solution(mesh):

time: 26.6 us -> 26.5 us (level)
  waiting for transfers between devices: 3.32 us -> 2.5 us
  Pallas kernels: 7.41 us -> 8.08 us
    ppermute x6, waiting for transfers between devices: 3.31 us -> 2.49 us  [partner(): lax.ppermute(value, 'aperture', [(d, d ^ 1 << bit) for d in range(count)])]
    pallas_call x15 -> x16, Pallas kernels: 7.41 us -> 8.08 us  [call(): pl.pallas_call(body, out_shape=outs, in_specs=in_specs or [whole] * len(a...]
  transfers between devices with their start and end apart: 10 -> 10, of which waited for: 3 -> 3; matrix products, arithmetic and copies ran while one was open for 0% -> 0% of each run, Pallas kernels for 24% -> 28%
where the time goes in v9:
time: 26.5 us; the launch traced here: 26.3 us
  starting transfers between devices  14.4 us (54%)
  Pallas kernels  8.08 us (30%)
  waiting for transfers between devices  2.5 us (9%)
  local copies, waits for them, and re-layouts  1.07 us (4%)
    ppermute x6, starting transfers between devices, partner(): lax.ppermute(value, 'aperture', [(d, d ^ 1 << bit) for d in range(count)])  9.27 us
    pallas_call x16, Pallas kernels, call(): pl.pallas_call(body, out_shape=outs, in_specs=in_specs or [whole] * len(a...  8.08 us
    ppermute x1, starting transfers between devices, shards(): lax.ppermute(guard, 'aperture', completed([(d, d - 1) for d in range(2, c...  3.08 us
    ppermute x6, waiting for transfers between devices, partner(): lax.ppermute(value, 'aperture', [(d, d ^ 1 << bit) for d in range(count)])  2.49 us
    ppermute x1, starting transfers between devices, shards(): lax.ppermute(rim, 'tile', completed([(t, t - 1) for t in range(1, tiles)]...  1.52 us
    unnamed x16, local copies, waits for them, and re-layouts  1.07 us
    ppermute x1, starting transfers between devices, shards(): lax.ppermute(corner, ('aperture', 'tile'), completed(steps, count * tiles))  0.56 us
  transfers between devices with their start and end apart: 10, of which 3 were waited for; matrix products, arithmetic and copies ran while one was open for 0% of the time, Pallas kernels for 28%

profile of v9, /device:TPU:0, one launch (start us, length us, event | category | flops | bytes accessed | tf_op | source)
XLA Modules:
  0.0 26.3 jit_solution(3890734112949159221)
XLA Ops:
  0.0 0.0 copy-start
  0.0 1.0 %copy-done = bf16[2,128,1024]{2,1,0:T(8,128)(2,1)S(1)} copy-done((bf16[2,128,1024]{2,1,0:T(8,128)(2,1)S(1)}, bf16[2,128,1024]{2,1,0:T(8,128)(2,1)}, u32[]{:S(2)}) %copy-start) | copy-done | bytes 524312
  1.0 0.1 shard_map.73
  1.2 3.1 %collective-permute-start = (bf16[2,32,1024]{2,1,0:T(8,128)(2,1)S(1)}, bf16[2,32,1024]{2,1,0:T(8,128)(2,1)S(1)}, u32[]{:S(2)}, u32[]{:S(2)}) collective-permute-start(bf16[2,32,1024]{2,1,0:T(8,128)(2,1)S(1)} %get-tuple-element.26), channel_id=1, source_target_pairs={{0,8},{2,0},{4,2},{6,4},{8,6},{10,16},{12,10},{14,12},{16,14},{18,... | collective-permute-start | bytes 393224 | tf_op jit(solution)/shard_map/ppermute | solution.py:308
  4.3 0.0 collective-permute-start.1
  4.3 0.0 copy-start.7
  4.3 1.5 %collective-permute-start.4 = (bf16[2,128,256]{2,1,0:T(8,128)(2,1)S(1)}, bf16[2,128,256]{2,1,0:T(8,128)(2,1)S(1)}, u32[]{:S(2)}, u32[]{:S(2)}) collective-permute-start(bf16[2,128,256]{2,1,0:T(8,128)(2,1)S(1)} %get-tuple-element.35), channel_id=1, source_target_pairs={{0,1},{1,0},{2,3},{3,2},{4,5},{5,4},{6,7},{7,6},{8,9},{9,8},{10,11... | collective-permute-start | bytes 393224 | tf_op jit(solution)/shard_map/ppermute | solution.py:309
  5.8 0.0 copy-start.1
  5.8 0.6 %collective-permute-start.5 = (bf16[2,32,256]{2,1,0:T(8,128)(2,1)S(1)}, bf16[2,32,256]{2,1,0:T(8,128)(2,1)S(1)}, u32[]{:S(2)}, u32[]{:S(2)}) collective-permute-start(bf16[2,32,256]{2,1,0:T(8,128)(2,1)S(1)} %get-tuple-element.36), channel_id=1, source_target_pairs={{0,1},{1,3},{2,5},{3,0},{4,7},{5,2},{6,9},{7,4},{8,11},{9,6},{10,1... | collective-permute-start | bytes 98312 | tf_op jit(solution)/shard_map/ppermute | solution.py:311
  6.4 0.0 copy-done.7
  6.4 0.2 shard_map.74.refs_3_
  6.6 0.0 copy-start.2
  6.6 0.0 copy-done.3
  6.6 0.0 copy-done.4
  6.6 0.0 copy-done.5
  6.6 0.0 copy-done.6
  6.6 0.8 %shard_map.75 = (bf16[2,64,192]{2,1,0:T(8,128)(2,1)S(1)}, f32[2,2,64,1024]{3,2,1,0:T(8,128)S(1)}) custom-call(s32[2,2,128]{2,1,0:T(2,128)S(1)} %copy-done.4, f32[2,2,8,128]{3,2,1,0:T(8,128)S(1)} %bitcast.1, f32[2,2,128]{2,1,0:T(2,128)S(1)} %copy-done.5, f32[2,2,128]{2,1,0:T(2,128)S(1)} %copy-done.6), custom_call_target="tpu_custom_call" | custom-call | flops 20000000 | tf_op jit(solution)/shard_map/pallas_call | solution.py:27
  7.5 0.0 collective-permute-done.refs_1_
  7.5 0.0 collective-permute-done.1.refs_2_
  7.5 0.0 copy-done.1
  7.5 0.0 copy-done.2
  7.5 0.7 %shard_map.76 = (bf16[2,64,384]{2,1,0:T(8,128)(2,1)S(1)}, bf16[2,64,384]{2,1,0:T(8,128)(2,1)S(1)}, bf16[2,64,128]{2,1,0:T(8,128)(2,1)S(1)}, bf16[2,64,128]{2,1,0:T(8,128)(2,1)S(1)}) custom-call(bf16[2,128,1024]{2,1,0:T(8,128)(2,1)S(1)} %copy-done.1, bf16[2,32,1024]{2,1,0:T(8,128)(2,1)S(1)} %collective-permute-done.refs_1_, ...), custom_call_target="tpu_custom_call" | custom-call | tf_op jit(solution)/shard_map/pallas_call | solution.py:27
  8.2 1.8 %collective-permute-start.3 = (bf16[2,64,384]{2,1,0:T(8,128)(2,1)S(1)}, bf16[2,64,384]{2,1,0:T(8,128)(2,1)S(1)}, u32[]{:S(2)}, u32[]{:S(2)}) collective-permute-start(bf16[2,64,384]{2,1,0:T(8,128)(2,1)S(1)} %get-tuple-element.30.refs_7_.refs_0_), channel_id=1, source_target_pairs={{0,8},{2,10},{4,12},{6,14},{8,0},{10,2},{12,4},{14,6},{16,24},{18,... | collective-permute-start | bytes 294920 | tf_op jit(solution)/shard_map/ppermute | solution.py:326
  10.0 0.5 %shard_map.77 = (bf16[2,64,384]{2,1,0:T(8,128)(2,1)S(1)}, bf16[2,64,384]{2,1,0:T(8,128)(2,1)S(1)}) custom-call(bf16[2,128,1024]{2,1,0:T(8,128)(2,1)S(1)} %copy-done.1, bf16[2,32,1024]{2,1,0:T(8,128)(2,1)S(1)} %collective-permute-done.refs_1_, bf16[2,32,1024]{2,1,0:T(8,128)(2,1)S(1)} %collective-permute-done.1.refs_2_, ...), custom_call_target="tpu_custom_call" | custom-call | tf_op jit(solution)/shard_map/pallas_call | solution.py:27
  10.5 2.1 %collective-permute-start.2 = (bf16[2,64,384]{2,1,0:T(8,128)(2,1)S(1)}, bf16[2,64,384]{2,1,0:T(8,128)(2,1)S(1)}, u32[]{:S(2)}, u32[]{:S(2)}) collective-permute-start(bf16[2,64,384]{2,1,0:T(8,128)(2,1)S(1)} %get-tuple-element.31.refs_7_.refs_0_), channel_id=1, source_target_pairs={{0,16},{2,18},{4,20},{6,22},{8,24},{10,26},{12,28},{14,30},{16,0},... | collective-permute-start | bytes 294920 | tf_op jit(solution)/shard_map/ppermute | solution.py:326
  12.6 0.0 collective-permute-done.5.refs_6_
  12.6 0.0 collective-permute-done.4.refs_5_
  12.6 0.5 %shard_map.78 = (bf16[2,64,256]{2,1,0:T(8,128)(2,1)S(1)}, bf16[2,64,256]{2,1,0:T(8,128)(2,1)S(1)}) custom-call(bf16[2,128,1024]{2,1,0:T(8,128)(2,1)S(1)} %copy-done.1, bf16[2,32,1024]{2,1,0:T(8,128)(2,1)S(1)} %collective-permute-done.refs_1_, bf16[2,32,1024]{2,1,0:T(8,128)(2,1)S(1)} %collective-permute-done.1.refs_2_, ...), custom_call_target="tpu_custom_call" | custom-call | flops 2000000000 | tf_op jit(solution)/shard_map/pallas_call | solution.py:27
  13.1 0.9 %collective-permute-start.6 = (bf16[2,64,256]{2,1,0:T(8,128)(2,1)S(1)}, bf16[2,64,256]{2,1,0:T(8,128)(2,1)S(1)}, u32[]{:S(2)}, u32[]{:S(2)}) collective-permute-start(bf16[2,64,256]{2,1,0:T(8,128)(2,1)S(1)} %get-tuple-element.37.refs_5_.refs_0_), channel_id=1, source_target_pairs={{0,8},{2,10},{4,12},{6,14},{8,0},{10,2},{12,4},{14,6},{16,24},{18,... | collective-permute-start | bytes 196616 | tf_op jit(solution)/shard_map/ppermute | solution.py:326
  14.0 0.0 collective-permute-done.3.refs_2_
  14.0 0.3 %shard_map.79 = (bf16[2,64,384]{2,1,0:T(8,128)(2,1)S(1)}, bf16[2,64,384]{2,1,0:T(8,128)(2,1)S(1)}) custom-call(bf16[2,64,384]{2,1,0:T(8,128)(2,1)S(1)} %get-tuple-element.30.refs_7_.refs_0_, bf16[2,64,384]{2,1,0:T(8,128)(2,1)S(1)} %get-tuple-element.34.refs_1_, bf16[2,64,384]{2,1,0:T(8,128)(2,1)S(1)} %collective-permute-done.3.refs_2_, ...), custom_call_target="tpu_custom_call" | custom-call | flops 2000000000 | tf_op jit(solution)/shard_map/pallas_call | solution.py:27
  14.3 2.5 %collective-permute-start.9 = (bf16[2,64,384]{2,1,0:T(8,128)(2,1)S(1)}, bf16[2,64,384]{2,1,0:T(8,128)(2,1)S(1)}, u32[]{:S(2)}, u32[]{:S(2)}) collective-permute-start(bf16[2,64,384]{2,1,0:T(8,128)(2,1)S(1)} %get-tuple-element.38.refs_4_.high), channel_id=1, source_target_pairs={{0,16},{2,18},{4,20},{6,22},{8,24},{10,26},{12,28},{14,30},{16,0},... | collective-permute-start | bytes 294920 | tf_op jit(solution)/shard_map/ppermute | solution.py:326
  16.8 0.8 %shard_map.80 = (bf16[2,64,192]{2,1,0:T(8,128)(2,1)S(1)}, f32[2,2,64,1024]{3,2,1,0:T(8,128)S(1)}) custom-call(s32[2,2,128]{2,1,0:T(2,128)S(1)} %copy-done.4, f32[2,2,8,128]{3,2,1,0:T(8,128)S(1)} %bitcast.2, f32[2,2,128]{2,1,0:T(2,128)S(1)} %copy-done.5, f32[2,2,128]{2,1,0:T(2,128)S(1)} %copy-done.6, bf16[2,64,384]{2,1,0:T(8,128)(2,1)S(1)} %get-tuple-element.38.refs_4_.high), custom_call_target="tpu_custom_call" | custom-call | flops 20000000 | tf_op jit(solution)/shard_map/pallas_call | solution.py:27
  17.7 0.4 %shard_map.81 = (bf16[1,64,192]{2,1,0:T(8,128)(2,1)S(1)}, f32[1,2,64,384]{3,2,1,0:T(8,128)S(1)}) custom-call(s32[2,2,128]{2,1,0:T(2,128)S(1)} %copy-done.4, f32[2,2,8,128]{3,2,1,0:T(8,128)S(1)} %bitcast.3, f32[2,2,128]{2,1,0:T(2,128)S(1)} %copy-done.5, f32[2,2,128]{2,1,0:T(2,128)S(1)} %copy-done.6, bf16[2,64,384]{2,1,0:T(8,128)(2,1)S(1)} %get-tuple-element.38.refs_4_.high), custom_call_target="tpu_custom_call" | custom-call | flops 20000000 | tf_op jit(solution)/shard_map/pallas_call | solution.py:27
  18.0 0.3 %collective-permute-done.6.refs_2_ = bf16[2,64,256]{2,1,0:T(8,128)(2,1)S(1)} collective-permute-done((bf16[2,64,256]{2,1,0:T(8,128)(2,1)S(1)}, bf16[2,64,256]{2,1,0:T(8,128)(2,1)S(1)}, u32[]{:S(2)}, u32[]{:S(2)}) %collective-permute-start.6) | collective-permute-done | bytes 65568 | tf_op jit(solution)/shard_map/ppermute | solution.py:326
  18.3 0.2 shard_map.82
  18.5 1.2 %collective-permute-start.8 = (bf16[2,64,256]{2,1,0:T(8,128)(2,1)S(1)}, bf16[2,64,256]{2,1,0:T(8,128)(2,1)S(1)}, u32[]{:S(2)}, u32[]{:S(2)}) collective-permute-start(bf16[2,64,256]{2,1,0:T(8,128)(2,1)S(1)} %get-tuple-element.44.refs_7_.refs_0_), channel_id=1, source_target_pairs={{0,16},{2,18},{4,20},{6,22},{8,24},{10,26},{12,28},{14,30},{16,0},... | collective-permute-start | bytes 196616 | tf_op jit(solution)/shard_map/ppermute | solution.py:326
  19.7 0.0 collective-permute-done.2.refs_2_
  19.7 0.5 %shard_map.83.refs_7_.refs_4_ = bf16[2,64,384]{2,1,0:T(8,128)(2,1)S(1)} custom-call(bf16[2,64,384]{2,1,0:T(8,128)(2,1)S(1)} %get-tuple-element.31.refs_7_.refs_0_, bf16[2,64,384]{2,1,0:T(8,128)(2,1)S(1)} %get-tuple-element.32.refs_1_, bf16[2,64,384]{2,1,0:T(8,128)(2,1)S(1)} %collective-permute-done.2.refs_2_, ...), custom_call_target="tpu_custom_call" | custom-call | tf_op jit(solution)/shard_map/pallas_call | solution.py:27
  20.2 0.8 %collective-permute-start.7 = (bf16[2,64,384]{2,1,0:T(8,128)(2,1)S(1)}, bf16[2,64,384]{2,1,0:T(8,128)(2,1)S(1)}, u32[]{:S(2)}, u32[]{:S(2)}) collective-permute-start(bf16[2,64,384]{2,1,0:T(8,128)(2,1)S(1)} %shard_map.83.refs_7_.refs_4_), channel_id=1, source_target_pairs={{0,8},{2,10},{4,12},{6,14},{8,0},{10,2},{12,4},{14,6},{16,24},{18,... | collective-permute-start | bytes 294920 | tf_op jit(solution)/shard_map/ppermute | solution.py:326
  20.9 0.2 shard_map.85.own
  21.1 0.5 %shard_map.84.out = f32[2,64,384]{2,1,0:T(8,128)S(1)} custom-call(bf16[2,64,384]{2,1,0:T(8,128)(2,1)S(1)} %get-tuple-element.31.refs_7_.refs_0_, bf16[2,64,384]{2,1,0:T(8,128)(2,1)S(1)} %get-tuple-element.32.refs_1_, bf16[2,64,384]{2,1,0:T(8,128)(2,1)S(1)} %collective-permute-done.2.refs_2_, bf16[2,64,192]{2,1,0:T(8,128)(2,1)S(1)} %get-tuple-element.27.refs_5_.refs_3_, ...), custom_call_target="tpu_custom_call" | custom-call | tf_op jit(solution)/shard_map/pallas_call | solution.py:27
  21.6 2.0 %collective-permute-done.9.other = bf16[2,64,384]{2,1,0:T(8,128)(2,1)S(1)} collective-permute-done((bf16[2,64,384]{2,1,0:T(8,128)(2,1)S(1)}, bf16[2,64,384]{2,1,0:T(8,128)(2,1)S(1)}, u32[]{:S(2)}, u32[]{:S(2)}) %collective-permute-start.9) | collective-permute-done | bytes 98336 | tf_op jit(solution)/shard_map/ppermute | solution.py:326
  23.5 0.9 %shard_map.86._ = f32[2,64,1024]{2,1,0:T(8,128)} custom-call(bf16[2,64,384]{2,1,0:T(8,128)(2,1)S(1)} %get-tuple-element.38.refs_4_.high, bf16[2,64,384]{2,1,0:T(8,128)(2,1)S(1)} %get-tuple-element.46.low, bf16[2,64,384]{2,1,0:T(8,128)(2,1)S(1)} %collective-permute-done.9.other, bf16[2,64,192]{2,1,0:T(8,128)(2,1)S(1)} %get-tuple-element.39.refs_5_.refs_2_.m, ...), custom_call_target="tpu_custom_call" | custom-call | flops 2000000000 | tf_op jit(solution)/shard_map/pallas_call | solution.py:27
  24.5 0.0 collective-permute-done.8.other
  24.5 0.8 %shard_map.87._ = f32[2,64,1024]{2,1,0:T(8,128)} custom-call(f32[2,64,256]{2,1,0:T(8,128)S(1)} %shard_map.85.own, bf16[2,64,256]{2,1,0:T(8,128)(2,1)S(1)} %collective-permute-done.8.other, bf16[2,64,192]{2,1,0:T(8,128)(2,1)S(1)} %get-tuple-element.39.refs_5_.refs_2_.m, ...), custom_call_target="tpu_custom_call", output_to_operand_aliasing={{}: (4, {})} | custom-call | tf_op jit(solution)/shard_map/pallas_call | solution.py:27
  25.3 0.2 collective-permute-done.7.got
  25.6 0.7 %shard_map.88 = f32[2,64,1024]{2,1,0:T(8,128)} custom-call(f32[2,64,384]{2,1,0:T(8,128)S(1)} %shard_map.84.out, bf16[2,64,384]{2,1,0:T(8,128)(2,1)S(1)} %collective-permute-done.7.got, f32[2,64,1024]{2,1,0:T(8,128)} %shard_map.87._), custom_call_target="tpu_custom_call", output_to_operand_aliasing={{}: (2, {})} | custom-call | tf_op jit(solution)/shard_map/pallas_call | solution.py:27
  (4 shorter events, 0.0 us)
Async XLA Ops:
  0.0 1.0 %copy-start = (bf16[2,128,1024]{2,1,0:T(8,128)(2,1)S(1)}, bf16[2,128,1024]{2,1,0:T(8,128)(2,1)}, u32[]{:S(2)}) copy-start(bf16[2,128,1024]{2,1,0:T(8,128)(2,1)} %refs_0_.9) | copy-start | bytes 1572868
  1.2 6.3 %collective-permute-start = (bf16[2,32,1024]{2,1,0:T(8,128)(2,1)S(1)}, bf16[2,32,1024]{2,1,0:T(8,128)(2,1)S(1)}, u32[]{:S(2)}, u32[]{:S(2)}) collective-permute-start(bf16[2,32,1024]{2,1,0:T(8,128)(2,1)S(1)} %get-tuple-element.26), channel_id=1, source_target_pairs={{0,8},{2,0},{4,2},{6,4},{8,6},{10,16},{12,10},{14,12},{16,14},{18,... | collective-permute-start | bytes 393224 | tf_op jit(solution)/shard_map/ppermute | solution.py:308
  4.3 3.2 %collective-permute-start.1 = (bf16[2,32,1024]{2,1,0:T(8,128)(2,1)S(1)}, bf16[2,32,1024]{2,1,0:T(8,128)(2,1)S(1)}, u32[]{:S(2)}, u32[]{:S(2)}) collective-permute-start(bf16[2,32,1024]{2,1,0:T(8,128)(2,1)S(1)} %get-tuple-element.26), channel_id=1, source_target_pairs={{0,2},{2,0},{4,6},{6,4},{8,10},{10,8},{12,14},{14,12},{16,18},{18,... | collective-permute-start | bytes 393224 | tf_op jit(solution)/shard_map/ppermute | solution.py:306
  4.3 2.1 %copy-start.7 = (bf16[2,256]{1,0:T(2,128)(2,1)S(1)}, bf16[2,256]{1,0:T(2,128)(2,1)}, u32[]{:S(2)}) copy-start(bf16[2,256]{1,0:T(2,128)(2,1)} %taps_ref.1) | copy-start | bytes 3076
  4.3 8.4 %collective-permute-start.4 = (bf16[2,128,256]{2,1,0:T(8,128)(2,1)S(1)}, bf16[2,128,256]{2,1,0:T(8,128)(2,1)S(1)}, u32[]{:S(2)}, u32[]{:S(2)}) collective-permute-start(bf16[2,128,256]{2,1,0:T(8,128)(2,1)S(1)} %get-tuple-element.35), channel_id=1, source_target_pairs={{0,1},{1,0},{2,3},{3,2},{4,5},{5,4},{6,7},{7,6},{8,9},{9,8},{10,11... | collective-permute-start | bytes 393224 | tf_op jit(solution)/shard_map/ppermute | solution.py:309
  5.8 0.8 %copy-start.3 = (f32[2,2,128,8]{2,3,1,0:T(8,128)S(1)}, f32[2,2,128,8]{2,3,1,0:T(8,128)}, u32[]{:S(2)}) copy-start(f32[2,2,128,8]{2,3,1,0:T(8,128)} %param.11) | copy-start | bytes 49156
  5.8 0.8 %copy-start.4 = (s32[2,2,128]{2,1,0:T(2,128)S(1)}, s32[2,2,128]{2,1,0:T(2,128)}, u32[]{:S(2)}) copy-start(s32[2,2,128]{2,1,0:T(2,128)} %refs_0_.11) | copy-start | bytes 6148
  5.8 0.8 %copy-start.5 = (f32[2,2,128]{2,1,0:T(2,128)S(1)}, f32[2,2,128]{2,1,0:T(2,128)}, u32[]{:S(2)}) copy-start(f32[2,2,128]{2,1,0:T(2,128)} %refs_2_.5) | copy-start | bytes 6148
  5.8 0.8 %copy-start.6 = (f32[2,2,128]{2,1,0:T(2,128)S(1)}, f32[2,2,128]{2,1,0:T(2,128)}, u32[]{:S(2)}) copy-start(f32[2,2,128]{2,1,0:T(2,128)} %refs_3_.5) | copy-start | bytes 6148
  5.8 1.7 %copy-start.1 = (bf16[2,128,1024]{2,1,0:T(8,128)(2,1)S(1)}, bf16[2,128,1024]{2,1,0:T(8,128)(2,1)}, u32[]{:S(2)}) copy-start(bf16[2,128,1024]{2,1,0:T(8,128)(2,1)} %refs_0_.9) | copy-start | bytes 1572868
  5.8 6.8 %collective-permute-start.5 = (bf16[2,32,256]{2,1,0:T(8,128)(2,1)S(1)}, bf16[2,32,256]{2,1,0:T(8,128)(2,1)S(1)}, u32[]{:S(2)}, u32[]{:S(2)}) collective-permute-start(bf16[2,32,256]{2,1,0:T(8,128)(2,1)S(1)} %get-tuple-element.36), channel_id=1, source_target_pairs={{0,1},{1,3},{2,5},{3,0},{4,7},{5,2},{6,9},{7,4},{8,11},{9,6},{10,1... | collective-permute-start | bytes 98312 | tf_op jit(solution)/shard_map/ppermute | solution.py:311
  6.6 0.9 %copy-start.2 = (bf16[2,64,160]{2,1,0:T(8,128)(2,1)S(1)}, bf16[2,64,160]{2,1,0:T(8,128)(2,1)}, u32[]{:S(2)}) copy-start(bf16[2,64,160]{2,1,0:T(8,128)(2,1)} %refs_4_.5) | copy-start | bytes 122884
  8.2 5.8 %collective-permute-start.3 = (bf16[2,64,384]{2,1,0:T(8,128)(2,1)S(1)}, bf16[2,64,384]{2,1,0:T(8,128)(2,1)S(1)}, u32[]{:S(2)}, u32[]{:S(2)}) collective-permute-start(bf16[2,64,384]{2,1,0:T(8,128)(2,1)S(1)} %get-tuple-element.30.refs_7_.refs_0_), channel_id=1, source_target_pairs={{0,8},{2,10},{4,12},{6,14},{8,0},{10,2},{12,4},{14,6},{16,24},{18,... | collective-permute-start | bytes 294920 | tf_op jit(solution)/shard_map/ppermute | solution.py:326
  10.5 9.2 %collective-permute-start.2 = (bf16[2,64,384]{2,1,0:T(8,128)(2,1)S(1)}, bf16[2,64,384]{2,1,0:T(8,128)(2,1)S(1)}, u32[]{:S(2)}, u32[]{:S(2)}) collective-permute-start(bf16[2,64,384]{2,1,0:T(8,128)(2,1)S(1)} %get-tuple-element.31.refs_7_.refs_0_), channel_id=1, source_target_pairs={{0,16},{2,18},{4,20},{6,22},{8,24},{10,26},{12,28},{14,30},{16,0},... | collective-permute-start | bytes 294920 | tf_op jit(solution)/shard_map/ppermute | solution.py:326
  13.1 5.2 %collective-permute-start.6 = (bf16[2,64,256]{2,1,0:T(8,128)(2,1)S(1)}, bf16[2,64,256]{2,1,0:T(8,128)(2,1)S(1)}, u32[]{:S(2)}, u32[]{:S(2)}) collective-permute-start(bf16[2,64,256]{2,1,0:T(8,128)(2,1)S(1)} %get-tuple-element.37.refs_5_.refs_0_), channel_id=1, source_target_pairs={{0,8},{2,10},{4,12},{6,14},{8,0},{10,2},{12,4},{14,6},{16,24},{18,... | collective-permute-start | bytes 196616 | tf_op jit(solution)/shard_map/ppermute | solution.py:326
  14.3 9.2 %collective-permute-start.9 = (bf16[2,64,384]{2,1,0:T(8,128)(2,1)S(1)}, bf16[2,64,384]{2,1,0:T(8,128)(2,1)S(1)}, u32[]{:S(2)}, u32[]{:S(2)}) collective-permute-start(bf16[2,64,384]{2,1,0:T(8,128)(2,1)S(1)} %get-tuple-element.38.refs_4_.high), channel_id=1, source_target_pairs={{0,16},{2,18},{4,20},{6,22},{8,24},{10,26},{12,28},{14,30},{16,0},... | collective-permute-start | bytes 294920 | tf_op jit(solution)/shard_map/ppermute | solution.py:326
  18.5 6.0 %collective-permute-start.8 = (bf16[2,64,256]{2,1,0:T(8,128)(2,1)S(1)}, bf16[2,64,256]{2,1,0:T(8,128)(2,1)S(1)}, u32[]{:S(2)}, u32[]{:S(2)}) collective-permute-start(bf16[2,64,256]{2,1,0:T(8,128)(2,1)S(1)} %get-tuple-element.44.refs_7_.refs_0_), channel_id=1, source_target_pairs={{0,16},{2,18},{4,20},{6,22},{8,24},{10,26},{12,28},{14,30},{16,0},... | collective-permute-start | bytes 196616 | tf_op jit(solution)/shard_map/ppermute | solution.py:326
  20.2 5.4 %collective-permute-start.7 = (bf16[2,64,384]{2,1,0:T(8,128)(2,1)S(1)}, bf16[2,64,384]{2,1,0:T(8,128)(2,1)S(1)}, u32[]{:S(2)}, u32[]{:S(2)}) collective-permute-start(bf16[2,64,384]{2,1,0:T(8,128)(2,1)S(1)} %shard_map.83.refs_7_.refs_4_), channel_id=1, source_target_pairs={{0,8},{2,10},{4,12},{6,14},{8,0},{10,2},{12,4},{14,6},{16,24},{18,... | collective-permute-start | bytes 294920 | tf_op jit(solution)/shard_map/ppermute | solution.py:326
